TPU v7x, 32 devices: a whole 2x2x4 slice. The times are simulated.
32 devices in a mesh: node: 16 (over z, x, core), local: 2 (over y).
Axes of the slice: x: 2, y: 2, z: 4, core: 2. Of those that a mesh axis runs over, the one named last changes fastest.
Arguments:
- tokens: bfloat16 [2, 16, 3584], P('local', 'node'), may hold values from -6 to 6
- expert_ids: int32 [2, 16, 8], P('local', 'node'), may hold values from 0 to 15, all different within a row; in each aligned block of 16 rows (0 to 15, 16 to 31, ..., all dimensions but the last counted through in order) at most 16 rows name the same one
- route_probs: float32 [2, 16, 8], P('local', 'node'), may hold values from 0.05 to 1
- gate_weight: bfloat16 [16, 3584, 2048], P('node', None, 'local'), may hold values from -0.09375 to 0.09375
- up_weight: bfloat16 [16, 3584, 2048], P('node', None, 'local'), may hold values from -0.09375 to 0.09375
- down_weight: bfloat16 [16, 2048, 3584], P('node', None, 'local'), may hold values from -0.125 to 0.125
- out_grad: bfloat16 [2, 16, 3584], P('local', 'node'), may hold values from -6 to 6
Outputs:
- combined: bfloat16 [2, 16, 3584], P('local', 'node')
- input_grad: bfloat16 [2, 16, 3584], P('local', 'node')
- prob_grad: float32 [2, 16, 8], P('local', 'node')
Inputs may be any that keep to these rules, and one draw needn't show every extreme that they name: `expert_ids`: each row names 8 different experts. Among the 16 rows of one token group (one index of the first dimension) no expert is named by more than 16 rows, a bound that some block reaches.
All inputs are finite; a program needn't handle non-finite values.
Results may differ from a plain program's by a relative error of at most 0.018.
Values may be sent and summed in bfloat16 or wider, within the bound.
No kernel may reach another device: no remote copies, remote signals or barrier semaphores. Data moves between devices by JAX's collectives and lax.ppermute only.
A program may use at most 64 MiB of HBM per device.

v0:
```python
import jax
import jax.numpy as jnp
from jax import lax
from jax.sharding import PartitionSpec as P


def selector(flags, capacity):
    live = (flags > 0).astype(jnp.int32)
    order = jnp.cumsum(live) - live
    slot_ids = lax.broadcasted_iota(jnp.int32, (capacity, flags.shape[0]), 0)
    return ((slot_ids == order[None, :]) & (live[None, :] > 0)).astype(jnp.bfloat16)


def per_device(tokens, expert_ids, route_probs, gate_weight, up_weight, down_weight, out_grad):
    node_count = lax.axis_size("node")
    token_count = tokens.shape[1]
    width = tokens.shape[2]
    top_count = expert_ids.shape[2]
    column_rows = token_count * node_count
    capacity = min(column_rows, 5 * column_rows * top_count // (2 * node_count))
    slot_count = node_count * token_count
    gate_w = gate_weight[0]
    up_w = up_weight[0]
    down_w = down_weight[0]
    hidden_dev = gate_w.shape[1]
    onehot = (expert_ids[0][..., None] == jnp.arange(node_count, dtype=jnp.int32)).astype(
        jnp.float32
    )
    weights = jnp.einsum("tk,tke->te", route_probs[0], onehot)
    member = jnp.sum(onehot, axis=1)
    own_rows = tokens[0]
    zero_value = jnp.zeros((), jnp.bfloat16)
    own_flags = member.T.astype(jnp.bfloat16)
    send_rows = jnp.where(own_flags[:, :, None] > 0, own_rows[None], zero_value)
    recv_rows, recv_flags = (
        lax.all_to_all(send_rows, "node", split_axis=0, concat_axis=0, tiled=True),
        lax.all_to_all(own_flags, "node", split_axis=0, concat_axis=0, tiled=True),
    )
    select = selector(recv_flags.reshape(slot_count), capacity)
    packed_rows = jnp.dot(
        select, recv_rows.reshape(slot_count, width), preferred_element_type=jnp.float32
    ).astype(jnp.bfloat16)
    piece = lax.all_gather(packed_rows, "local", axis=0, tiled=True)
    gate_part = jnp.dot(piece, gate_w, preferred_element_type=jnp.float32)
    up_part = jnp.dot(piece, up_w, preferred_element_type=jnp.float32)
    joined = jnp.concatenate([gate_part, up_part], axis=1)
    gate_pre = joined[:, :hidden_dev]
    up_pre = joined[:, hidden_dev:]
    sigmoid_gate = jax.nn.sigmoid(gate_pre)
    silu_gate = gate_pre * sigmoid_gate
    hidden = (silu_gate * up_pre).astype(jnp.bfloat16)
    block = down_w
    routed_part = jnp.dot(
        lax.all_gather(hidden, "local", axis=1, tiled=True),
        block,
        preferred_element_type=jnp.float32,
    )
    routed_cols = routed_part.astype(jnp.bfloat16)
    routed_own = lax.all_to_all(routed_cols, "local", split_axis=0, concat_axis=1, tiled=True)
    routed_slots = jnp.dot(select.T, routed_own, preferred_element_type=jnp.float32).astype(
        jnp.bfloat16
    )
    routed_back = lax.all_to_all(
        routed_slots.reshape(node_count, token_count, width),
        "node",
        split_axis=0,
        concat_axis=0,
        tiled=True,
    )
    routed_wide = routed_back.astype(jnp.float32)
    combined = jnp.einsum("te,etd->td", weights, routed_wide).astype(jnp.bfloat16)
    grad_wide = out_grad[0].astype(jnp.float32)
    prob_terms = jnp.einsum("td,etd->te", grad_wide, routed_wide)
    prob_grad = jnp.einsum("te,tke->tk", prob_terms, onehot)
    scaled = (weights.T[:, :, None] * grad_wide[None]).astype(jnp.bfloat16)
    grad_recv = lax.all_to_all(scaled, "node", split_axis=0, concat_axis=0, tiled=True)
    grad_own = jnp.dot(
        select, grad_recv.reshape(slot_count, width), preferred_element_type=jnp.float32
    ).astype(jnp.bfloat16)
    grad_cols = lax.all_to_all(grad_own, "local", split_axis=1, concat_axis=0, tiled=True)
    block = down_w
    hidden_grad = (
        lax.psum_scatter(
            lax.dot_general(
                block, grad_cols, (((1,), (1,)), ((), ())), preferred_element_type=jnp.float32
            ).astype(jnp.bfloat16),
            "local",
            scatter_dimension=0,
            tiled=True,
        )
        .astype(jnp.float32)
        .T
    )
    gate_grad = (
        hidden_grad * up_pre * sigmoid_gate * (1.0 + gate_pre * (1.0 - sigmoid_gate))
    ).astype(jnp.bfloat16)
    up_grad = (hidden_grad * silu_gate).astype(jnp.bfloat16)
    first = lax.dot_general(
        gate_grad, gate_w, (((1,), (1,)), ((), ())), preferred_element_type=jnp.float32
    )
    second = lax.dot_general(
        up_grad, up_w, (((1,), (1,)), ((), ())), preferred_element_type=jnp.float32
    )
    input_own = lax.psum_scatter(
        (first + second).astype(jnp.bfloat16), "local", scatter_dimension=0, tiled=True
    )
    input_slots = jnp.dot(select.T, input_own, preferred_element_type=jnp.float32).astype(
        jnp.bfloat16
    )
    input_back = lax.all_to_all(
        input_slots.reshape(node_count, token_count, width),
        "node",
        split_axis=0,
        concat_axis=0,
        tiled=True,
    )
    input_grad = jnp.sum(input_back.astype(jnp.float32), axis=0).astype(jnp.bfloat16)
    return (combined[None], input_grad[None], prob_grad[None])


def solution(mesh):
    placed = (
        P("local", "node", None),
        P("local", "node", None),
        P("local", "node", None),
        P("node", None, "local"),
        P("node", None, "local"),
        P("node", None, "local"),
        P("local", "node", None),
    )
    return jax.shard_map(
        per_device,
        mesh=mesh,
        in_specs=placed,
        out_specs=(P("local", "node", None), P("local", "node", None), P("local", "node", None)),
        check_vma=False,
    )
```

profile of v0, /device:TPU:0, one launch (start us, length us, event | category | flops | bytes accessed | tf_op | source)
XLA Modules:
  0.0 135.0 jit_solution(1286836361363636059)
XLA Ops:
  8.6 7.4 %all-to-all-start = ((bf16[16,1,1]{2,1,0:T(2,128)(2,1)}), bf16[16,1,1]{2,1,0:T(2,128)(2,1)S(1)}, u32[]{:S(2)}, u32[]{:S(2)}) async-start(bf16[16,1,1]{2,1,0:T(2,128)(2,1)} %copy.32), calls=%async_computation | async-start | bytes 16384 | tf_op jit(solution)/shard_map/all_to_all | solution.py:37
  16.0 0.8 fusion.66
  16.9 0.8 reduce.5
  17.6 0.8 reduce.7
  20.6 1.3 reduce.10
  22.6 6.0 %all-to-all-start.4 = ((bf16[16,2,1792]{2,1,0:T(2,128)(2,1)}), bf16[16,2,1792]{2,1,0:T(2,128)(2,1)S(1)}, u32[]{:S(2)}, u32[]{:S(2)}) async-start(bf16[16,2,1792]{2,1,0:T(2,128)(2,1)} %reshape.385), calls=%async_computation.4 | async-start | bytes 229376 | tf_op jit(solution)/shard_map/all_to_all | solution.py:76
  29.2 7.1 %all-to-all-done.4 = bf16[16,2,1792]{2,1,0:T(2,128)(2,1)S(1)} async-done(((bf16[16,2,1792]{2,1,0:T(2,128)(2,1)}), bf16[16,2,1792]{2,1,0:T(2,128)(2,1)S(1)}, u32[]{:S(2)}, u32[]{:S(2)}) %all-to-all-start.4) | async-done | bytes 114720 | tf_op jit(solution)/shard_map/all_to_all | solution.py:76
  36.2 3.5 %all-to-all-start.1 = ((bf16[16,2,1792]{2,1,0:T(2,128)(2,1)}), bf16[16,2,1792]{2,1,0:T(2,128)(2,1)S(1)}, u32[]{:S(2)}, u32[]{:S(2)}) async-start(bf16[16,2,1792]{2,1,0:T(2,128)(2,1)} %reshape.381), calls=%async_computation.1 | async-start | bytes 229376 | tf_op jit(solution)/shard_map/all_to_all | solution.py:36
  40.7 6.7 %all-to-all-done.1 = bf16[16,2,1792]{2,1,0:T(2,128)(2,1)S(1)} async-done(((bf16[16,2,1792]{2,1,0:T(2,128)(2,1)}), bf16[16,2,1792]{2,1,0:T(2,128)(2,1)S(1)}, u32[]{:S(2)}, u32[]{:S(2)}) %all-to-all-start.1) | async-done | bytes 114720 | tf_op jit(solution)/shard_map/all_to_all | solution.py:36
  47.4 3.4 %all-to-all-start.5 = ((bf16[16,2,1792]{2,0,1:T(8,128)(2,1)}), bf16[16,2,1792]{2,0,1:T(8,128)(2,1)S(1)}, u32[]{:S(2)}, u32[]{:S(2)}) async-start(bf16[16,2,1792]{2,0,1:T(8,128)(2,1)} %bitcast.124), calls=%async_computation.5 | async-start | bytes 229376 | tf_op jit(solution)/shard_map/all_to_all | solution.py:80
  51.1 5.7 %all_gather.6 = bf16[32,3584]{1,0:T(8,128)(2,1)S(1)} all-gather(bf16[16,3584]{1,0:T(8,128)(2,1)S(1)} %convolution_convert_fusion.3), channel_id=1, replica_groups=mesh['node'=16,'local'=2] {'local'}, dimensions={0}, use_global_device_ids=true | all-gather | bytes 344064 | tf_op jit(solution)/shard_map/all_gather | solution.py:43
  56.8 4.5 %fusion.10 = f32[32,1024]{1,0:T(8,128)S(1)} fusion(bf16[32,3584]{1,0:T(8,128)(2,1)S(1)} %all_gather.6, bf16[1,3584,1024]{2,1,0:T(8,128)(2,1)} %param.10), kind=kOutput, calls=%fused_computation.10 | convolution fusion | flops 234881024 | bytes 7700480 | tf_op jit(solution)/shard_map/dot_general | solution.py:44
  61.3 6.0 %fusion.26 = bf16[2048,32]{0,1:T(8,128)(2,1)} fusion(bf16[32,1792]{1,0:T(8,128)(2,1)S(1)} %bitcast.128, bf16[1,2048,1792]{2,1,0:T(8,128)(2,1)} %param.12), kind=kOutput, calls=%fused_computation.22 | convolution fusion | flops 234946560 | bytes 7585792 | tf_op jit(solution)/shard_map/dot_general | solution.py:84
  67.3 4.5 %multiply_convert_fusion.1 = (bf16[32,1024]{1,0:T(8,128)(2,1)S(1)}, f32[32,1024]{1,0:T(8,128)S(1)}) fusion(f32[32,1024]{1,0:T(8,128)S(1)} %fusion.10, bf16[32,3584]{1,0:T(8,128)(2,1)S(1)} %all_gather.6, bf16[1,3584,1024]{2,1,0:T(8,128)(2,1)} %param.11), kind=kOutput, calls=%fused_computation.35 | convolution fusion | flops 235077632 | bytes 7897088 | tf_op jit(solution)/shard_map/dot_general | solution.py:45
  71.8 4.9 %all_gather.7 = bf16[32,2048]{1,0:T(8,128)(2,1)S(1)} all-gather(bf16[32,1024]{1,0:T(8,128)(2,1)S(1)} %get-tuple-element.3), channel_id=1, replica_groups=mesh['node'=16,'local'=2] {'local'}, dimensions={1}, use_global_device_ids=true | all-gather | bytes 196608 | tf_op jit(solution)/shard_map/all_gather | solution.py:54
  76.7 5.4 %fusion.4 = f32[32,3584]{1,0:T(8,128)S(1)} fusion(bf16[1,3584,1024]{2,1,0:T(8,128)(2,1)} %param.11, bf16[1024,32]{0,1:T(8,128)(2,1)} %reduce-scatter.3.cloned.1.call-done, f32[32,1024]{1,0:T(8,128)S(1)} %fusion.10), kind=kOutput, calls=%fused_computation.4 | convolution fusion | flops 235110400 | bytes 7995392 | tf_op jit(solution)/shard_map/dot_general | solution.py:101
  82.2 6.0 %fusion.15 = bf16[32,3584]{1,0:T(8,128)(2,1)} fusion(f32[32,3584]{1,0:T(8,128)S(1)} %fusion.4, bf16[1,3584,1024]{2,1,0:T(8,128)(2,1)} %param.10, f32[32,1024]{1,0:T(8,128)S(1)} %get-tuple-element.4, bf16[1024,32]{0,1:T(8,128)(2,1)S(1)} %copy-done.1, f32[32,1024]{1,0:T(8,128)S(1)} %fusion.10), kind=kOutput, calls=%fused_computation.13 | convolution fusion | flops 235470848 | bytes 8355840 | tf_op jit(solution)/shard_map/dot_general | solution.py:98
  88.2 4.4 %fusion.20 = bf16[32,1792]{1,0:T(8,128)(2,1)S(1)} fusion(bf16[32,2048]{1,0:T(8,128)(2,1)S(1)} %all_gather.7, bf16[1,2048,1792]{2,1,0:T(8,128)(2,1)} %param.12), kind=kOutput, calls=%fused_computation.20 | convolution fusion | flops 234938368 | bytes 7585792 | tf_op jit(solution)/shard_map/dot_general | solution.py:53
  92.6 7.2 %all_to_all.64 = bf16[2,16,1792]{2,1,0:T(8,128)(2,1)S(1)} all-to-all(bf16[2,16,1792]{2,1,0:T(8,128)(2,1)S(1)} %bitcast.129), channel_id=1, replica_groups=mesh['node'=16,'local'=2] {'local'}, dimensions={0} | all-to-all | bytes 229376 | tf_op jit(solution)/shard_map/all_to_all | solution.py:59
  100.8 12.7 %all_to_all.65 = bf16[16,2,1792]{2,1,0:T(2,128)(2,1)S(1)} all-to-all(bf16[16,2,1792]{2,1,0:T(2,128)(2,1)S(1)} %reshape.383), channel_id=1, replica_groups=mesh['node'=16,'local'=2] {'node'}, dimensions={0} | all-to-all | bytes 229376 | tf_op jit(solution)/shard_map/all_to_all | solution.py:63
  113.6 1.1 fusion.19
  116.0 3.5 %all-to-all-start.6 = ((bf16[16,2,1792]{2,1,0:T(2,128)(2,1)}), bf16[16,2,1792]{2,1,0:T(2,128)(2,1)S(1)}, u32[]{:S(2)}, u32[]{:S(2)}) async-start(bf16[16,2,1792]{2,1,0:T(2,128)(2,1)} %reshape.387), calls=%async_computation.8 | async-start | bytes 229376 | tf_op jit(solution)/shard_map/all_to_all | solution.py:110
  120.3 0.8 fusion.30
  121.1 6.1 %all-to-all-done.6 = bf16[16,2,1792]{2,1,0:T(2,128)(2,1)S(1)} async-done(((bf16[16,2,1792]{2,1,0:T(2,128)(2,1)}), bf16[16,2,1792]{2,1,0:T(2,128)(2,1)S(1)}, u32[]{:S(2)}, u32[]{:S(2)}) %all-to-all-start.6) | async-done | bytes 114720 | tf_op jit(solution)/shard_map/all_to_all | solution.py:110
  (49 shorter events, 10.2 us)
Async XLA Ops:
  7.2 8.8 %copy-start = (f32[1,1,8]{2,1,0:T(1,128)S(1)}, f32[1,1,8]{2,1,0:T(1,128)}, u32[]{:S(2)}) copy-start(f32[1,1,8]{2,1,0:T(1,128)} %param.9) | copy-start | bytes 100
  8.6 13.9 %all-to-all-start = ((bf16[16,1,1]{2,1,0:T(2,128)(2,1)}), bf16[16,1,1]{2,1,0:T(2,128)(2,1)S(1)}, u32[]{:S(2)}, u32[]{:S(2)}) async-start(bf16[16,1,1]{2,1,0:T(2,128)(2,1)} %copy.32), calls=%async_computation | async-start | bytes 16384 | tf_op jit(solution)/shard_map/all_to_all | solution.py:37
  22.6 13.7 %all-to-all-start.4 = ((bf16[16,2,1792]{2,1,0:T(2,128)(2,1)}), bf16[16,2,1792]{2,1,0:T(2,128)(2,1)S(1)}, u32[]{:S(2)}, u32[]{:S(2)}) async-start(bf16[16,2,1792]{2,1,0:T(2,128)(2,1)} %reshape.385), calls=%async_computation.4 | async-start | bytes 229376 | tf_op jit(solution)/shard_map/all_to_all | solution.py:76
  36.2 11.2 %all-to-all-start.1 = ((bf16[16,2,1792]{2,1,0:T(2,128)(2,1)}), bf16[16,2,1792]{2,1,0:T(2,128)(2,1)S(1)}, u32[]{:S(2)}, u32[]{:S(2)}) async-start(bf16[16,2,1792]{2,1,0:T(2,128)(2,1)} %reshape.381), calls=%async_computation.1 | async-start | bytes 229376 | tf_op jit(solution)/shard_map/all_to_all | solution.py:36
  47.4 13.9 %all-to-all-start.5 = ((bf16[16,2,1792]{2,0,1:T(8,128)(2,1)}), bf16[16,2,1792]{2,0,1:T(8,128)(2,1)S(1)}, u32[]{:S(2)}, u32[]{:S(2)}) async-start(bf16[16,2,1792]{2,0,1:T(8,128)(2,1)} %bitcast.124), calls=%async_computation.5 | async-start | bytes 229376 | tf_op jit(solution)/shard_map/all_to_all | solution.py:80
  50.8 26.0 %reduce-scatter.3.cloned.1.call-start = ((), (), s32[]{:S(2)}) async-start(), calls=%async_computation.9 | async-start | bytes 196608 | tf_op jit(solution)/shard_map/reduce_scatter | solution.py:83
  67.2 46.3 %reduce-scatter.5.cloned.1.call-start = ((), (), s32[]{:S(2)}) async-start(), calls=%async_computation.10 | async-start | bytes 344064 | tf_op jit(solution)/shard_map/reduce_scatter | solution.py:104
  76.7 5.4 %copy-start.1 = (bf16[1024,32]{0,1:T(8,128)(2,1)S(1)}, bf16[1024,32]{0,1:T(8,128)(2,1)}, u32[]{:S(2)}) copy-start(bf16[1024,32]{0,1:T(8,128)(2,1)} %reduce-scatter.3.cloned.1.call-done) | copy-start | bytes 196612
  88.2 32.1 %copy-start.2 = (bf16[1,1,3584]{2,1,0:T(2,128)(2,1)S(1)}, bf16[1,1,3584]{2,1,0:T(2,128)(2,1)}, u32[]{:S(2)}) copy-start(bf16[1,1,3584]{2,1,0:T(2,128)(2,1)} %param.13) | copy-start | bytes 21508
  88.2 32.1 %copy-start.3 = (s32[1,1,8]{2,1,0:T(1,128)S(1)}, s32[1,1,8]{2,1,0:T(1,128)}, u32[]{:S(2)}) copy-start(s32[1,1,8]{2,1,0:T(1,128)} %param.8) | copy-start | bytes 100
  116.0 11.2 %all-to-all-start.6 = ((bf16[16,2,1792]{2,1,0:T(2,128)(2,1)}), bf16[16,2,1792]{2,1,0:T(2,128)(2,1)S(1)}, u32[]{:S(2)}, u32[]{:S(2)}) async-start(bf16[16,2,1792]{2,1,0:T(2,128)(2,1)} %reshape.387), calls=%async_computation.8 | async-start | bytes 229376 | tf_op jit(solution)/shard_map/all_to_all | solution.py:110
Sparse Core Ops, SparseCore 0:
  67.4 8.7 reduce-scatter.2
  88.3 11.3 reduce-scatter.4
where the time goes:
time: 136 us; the launch traced here: 135 us
  matrix products  34.2 us (25%)
  blocking collectives  30.5 us (22%)
  starting transfers between devices  23.8 us (18%)
  waiting for transfers between devices  20 us (15%)
  between operations  14.3 us (11%)
  other arithmetic  6.7 us (5%)
  local copies, waits for them, and re-layouts  5.51 us (4%)
    all_to_all x1, blocking collectives, per_device(): lax.all_to_all(routed_slots.reshape(node_count, token_count, width), 'nod...  12.7 us
    all_to_all x1, starting transfers between devices, per_device(): lax.all_to_all(own_flags, 'node', split_axis=0, concat_axis=0, tiled=True)  7.36 us
    all_to_all x1, blocking collectives, per_device(): lax.all_to_all(routed_cols, 'local', split_axis=0, concat_axis=1, tiled=T...  7.18 us
    all_to_all x1, waiting for transfers between devices, per_device(): lax.all_to_all(scaled, 'node', split_axis=0, concat_axis=0, tiled=True)  7.09 us
    all_to_all x1, waiting for transfers between devices, per_device(): lax.all_to_all(send_rows, 'node', split_axis=0, concat_axis=0, tiled=True)  6.73 us
    all_to_all x1, waiting for transfers between devices, per_device(): lax.all_to_all(input_slots.reshape(node_count, token_count, width), 'node...  6.08 us
    dot_general x1, matrix products, per_device(): lax.dot_general(gate_grad, gate_w, (((1,), (1,)), ((), ())), preferred_el...  6.03 us
    all_to_all x1, starting transfers between devices, per_device(): lax.all_to_all(scaled, 'node', split_axis=0, concat_axis=0, tiled=True)  6.01 us
  transfers between devices with their start and end apart: 7, of which 3 were waited for; matrix products, arithmetic and copies ran while one was open for 18% of the time, Pallas kernels for 0%

commit v1 on v0

--- a/solution.py
+++ b/solution.py
@@ -1,7 +1,278 @@
+import functools
+
 import jax
 import jax.numpy as jnp
 from jax import lax
+from jax.experimental import pallas as pl
+from jax.experimental.pallas import tpu as pltpu
+from jax.sharding import Mesh
 from jax.sharding import PartitionSpec as P
+
+BF16 = jnp.bfloat16
+F32 = jnp.float32
+LANES = 128
+CHUNK = 512
+DISPATCH_ROWS = 16
+RETURN_ROWS = 16
+COLS = 256
+
+NT = (((1,), (1,)), ((), ()))
+VMEM = pl.BlockSpec(memory_space=pltpu.VMEM)
+SMEM = pl.BlockSpec(memory_space=pltpu.SMEM)
+
+
+def ceil_div(a, b):
+    return -(-a // b)
+
+
+def call(body, outs, ins, scratch=(), flops=0, moved=0, limit=48 << 20):
+    return pl.pallas_call(
+        body,
+        out_shape=tuple(jax.ShapeDtypeStruct(s, d) for s, d in outs),
+        in_specs=ins,
+        out_specs=tuple(VMEM for _ in outs),
+        scratch_shapes=list(scratch),
+        compiler_params=pltpu.CompilerParams(vmem_limit_bytes=limit),
+        cost_estimate=pl.CostEstimate(flops=flops, bytes_accessed=moved, transcendentals=0),
+    )
+
+
+def dot(a, b):
+    return jnp.dot(a, b, preferred_element_type=F32)
+
+
+def dot_nt(a, b):
+    return lax.dot_general(a, b, NT, preferred_element_type=F32)
+
+
+def pack_body(parts, ids_ref, probs_ref, tok_ref, grad_ref, out_ref, wide):
+    top = ids_ref.shape[2]
+    lane = lax.broadcasted_iota(jnp.int32, (1, LANES), 1)
+    weight = jnp.zeros((1, LANES), F32)
+    for k in range(top):
+        weight = jnp.where(lane == ids_ref[0, 0, k], probs_ref[0, 0, k], weight)
+    high = weight.astype(BF16).astype(F32)
+    wide[...] = jnp.zeros_like(wide)
+    for i in range(parts):
+        cols = pl.ds(i * CHUNK, CHUNK)
+        wide[i : i + 1, :] = tok_ref[0, :, cols].astype(F32)
+        wide[8 + i : 9 + i, :] = grad_ref[0, :, cols].astype(F32)
+    wide[7:8, 0:LANES] = high
+    wide[7:8, LANES : 2 * LANES] = weight - high
+    out_ref[...] = jnp.broadcast_to(wide[...].astype(BF16)[None], out_ref.shape)
+
+
+def first_body(
+    own_ref, other_ref, gate_ref, up_ref, down_ref,
+    send_ref, cot_ref, gate_out, up_out, weight_out,
+    wide, rows, grads,
+):
+    count = own_ref.shape[0]
+    parts = rows.shape[1] // CHUNK
+    hidden = gate_ref.shape[1]
+    feats = down_ref.shape[1]
+    local = lax.axis_index("local")
+    expert = lax.axis_index("chip") * 2 + lax.axis_index("core")
+    lane = lax.broadcasted_iota(jnp.int32, (count, LANES), 1)
+    for half, ref in enumerate((own_ref, other_ref)):
+        at = pl.ds(half * count, count)
+        wide[...] = ref[...].astype(F32)
+        for i in range(parts):
+            cols = pl.ds(i * CHUNK, CHUNK)
+            rows[at, cols] = wide[:, i, :].astype(BF16)
+            grads[at, cols] = wide[:, 8 + i, :].astype(BF16)
+        both = wide[:, 7, 0:LANES] + wide[:, 7, LANES : 2 * LANES]
+        both = jnp.sum(jnp.where(lane == expert, both, 0.0), axis=1, keepdims=True)
+        weight_out[at, :] = jnp.broadcast_to(both, (count, LANES))
+    grad_half = grads[:, pl.ds(pl.multiple_of(local * feats, LANES), feats)]
+    steps = hidden // COLS
+
+    def cot(n, carry):
+        at = pl.multiple_of(n * COLS, COLS)
+        own = dot_nt(grad_half, down_ref[pl.ds(pl.multiple_of(local * hidden + at, COLS), COLS), :])
+        cot_ref[:, pl.ds(at, COLS)] = own
+        away = dot_nt(
+            grad_half, down_ref[pl.ds(pl.multiple_of((1 - local) * hidden + at, COLS), COLS), :]
+        )
+        send_ref[:, pl.ds(at, COLS)] = away.astype(BF16)
+        return carry
+
+    lax.fori_loop(0, steps, cot, 0)
+    tokens = rows[...]
+
+    def forward(n, carry):
+        at = pl.multiple_of(n * COLS, COLS)
+        cols = pl.ds(at, COLS)
+        gate = dot(tokens, gate_ref[:, cols])
+        up = dot(tokens, up_ref[:, cols])
+        gate_out[:, cols] = gate
+        up_out[:, cols] = up
+        send_ref[:, pl.ds(pl.multiple_of(hidden + at, COLS), COLS)] = (
+            gate * jax.nn.sigmoid(gate) * up
+        ).astype(BF16)
+        return carry
+
+    lax.fori_loop(0, steps, forward, 0)
+
+
+def routed_own_body(send_ref, down_ref, out_ref):
+    hidden = send_ref.shape[1] // 2
+    local = lax.axis_index("local")
+    act = send_ref[:, hidden:]
+    at = pl.ds(pl.multiple_of(local * hidden, COLS), hidden)
+
+    def step(n, carry):
+        cols = pl.ds(pl.multiple_of(n * COLS, COLS), COLS)
+        out_ref[:, cols] = dot(act, down_ref[at, cols])
+        return carry
+
+    lax.fori_loop(0, out_ref.shape[1] // COLS, step, 0)
+
+
+def second_body(
+    send_ref, recv_ref, cot_ref, gate_in, up_in, weight_in, routed_in,
+    gate_ref, up_ref, down_ref,
+    mine_ref, other_ref,
+    wide,
+):
+    total, width2 = send_ref.shape
+    hidden = width2 // 2
+    feats = routed_in.shape[1]
+    width = gate_ref.shape[0]
+    count = total // 2
+    local = lax.axis_index("local")
+    expert = lax.axis_index("chip") * 2 + lax.axis_index("core")
+    weight = weight_in[:, 0:1]
+    gate, up = gate_in[...], up_in[...]
+    sig = jax.nn.sigmoid(gate)
+    cot = cot_ref[...] + recv_ref[:, :hidden].astype(F32)
+    prob = jnp.sum(cot * send_ref[:, hidden:].astype(F32), axis=1, keepdims=True)
+    hidden_grad = cot * weight
+    gate_grad = (hidden_grad * up * sig * (1.0 + gate * (1.0 - sig))).astype(BF16)
+    up_grad = (hidden_grad * (gate * sig)).astype(BF16)
+
+    def put(slot, value):
+        wide[:, slot // 3, (slot % 3) * LANES : (slot % 3 + 1) * LANES] = value
+
+    for n in range(width // COLS):
+        at = pl.ds(n * COLS, COLS)
+        part = dot_nt(gate_grad, gate_ref[at, :]) + dot_nt(up_grad, up_ref[at, :])
+        for j in range(COLS // LANES):
+            put(n * (COLS // LANES) + j, part[:, j * LANES : (j + 1) * LANES])
+    base = width // LANES
+    act = recv_ref[:, hidden:]
+    at = pl.ds(pl.multiple_of((1 - local) * hidden, COLS), hidden)
+    for n in range(feats // COLS):
+        cols = slice(n * COLS, (n + 1) * COLS)
+        part = (dot(act, down_ref[at, cols]) + routed_in[:, cols]).astype(BF16).astype(F32) * weight
+        for j in range(COLS // LANES):
+            put(base + n * (COLS // LANES) + j, part[:, j * LANES : (j + 1) * LANES])
+    base += feats // LANES
+    lane = lax.broadcasted_iota(jnp.int32, (total, LANES), 1)
+    prob = jnp.where(lane == expert, prob, 0.0)
+    high = prob.astype(BF16).astype(F32)
+    put(base, high)
+    put(base + 1, prob - high)
+    for slot in range(base + 2, 3 * RETURN_ROWS):
+        put(slot, jnp.zeros((total, LANES), F32))
+    mine_ref[...] = wide[:count].astype(BF16)
+    other_ref[...] = wide[count:].astype(BF16)
+
+
+def final_body(in_ref, ids_ref, comb_ref, grad_ref, prob_ref, wide):
+    groups = in_ref.shape[0]
+    width = comb_ref.shape[2]
+    feats = width // 2
+    parts = [
+        functools.reduce(lambda a, b: a + b, [in_ref[i].astype(F32) for i in range(j, groups, 2)])
+        for j in range(2)
+    ]
+    wide[0], wide[1] = parts
+
+    def get(j, slot):
+        return wide[j, slot // 3 : slot // 3 + 1, (slot % 3) * LANES : (slot % 3 + 1) * LANES]
+
+    base = width // LANES
+    for c in range(base):
+        grad_ref[0, :, c * LANES : (c + 1) * LANES] = (get(0, c) + get(1, c)).astype(BF16)
+    for j in range(2):
+        for c in range(feats // LANES):
+            at = j * feats + c * LANES
+            comb_ref[0, :, at : at + LANES] = get(j, base + c).astype(BF16)
+    base += feats // LANES
+    prob = get(0, base) + get(1, base) + get(0, base + 1) + get(1, base + 1)
+    lane = lax.broadcasted_iota(jnp.int32, (1, LANES), 1)
+    top = ids_ref.shape[2]
+    out = jnp.zeros((1, LANES), F32)
+    for k in range(top):
+        value = jnp.sum(jnp.where(lane == ids_ref[0, 0, k], prob, 0.0), axis=1, keepdims=True)
+        out = jnp.where(lane == k, value, out)
+    prob_ref[0] = out[:, :top]
+
+
+def swap(x, axis):
+    return lax.ppermute(x, axis, [(0, 1), (1, 0)])
+
+
+def fast_device(tokens, expert_ids, route_probs, gate_weight, up_weight, down_weight, out_grad):
+    chips = lax.axis_size("chip")
+    groups = chips * 2
+    total = 2 * groups
+    width = tokens.shape[2]
+    gate_w, up_w, down_w = gate_weight[0], up_weight[0], down_weight[0]
+    hidden = gate_w.shape[1]
+    feats = down_w.shape[1]
+    one = width * hidden * 2
+    (packed,) = call(
+        functools.partial(pack_body, width // CHUNK),
+        [((groups, DISPATCH_ROWS, CHUNK), BF16)],
+        [SMEM, SMEM, VMEM, VMEM],
+        [pltpu.VMEM((DISPATCH_ROWS, CHUNK), F32)],
+    )(expert_ids, route_probs, tokens, out_grad)
+    own = lax.all_to_all(packed, ("chip", "local"), split_axis=0, concat_axis=0, tiled=True)
+    other = swap(own, "core")
+    send, cot, gate, up, weight = call(
+        first_body,
+        [
+            ((total, 2 * hidden), BF16),
+            ((total, hidden), F32),
+            ((total, hidden), F32),
+            ((total, hidden), F32),
+            ((total, LANES), F32),
+        ],
+        [VMEM] * 5,
+        [
+            pltpu.VMEM((groups, DISPATCH_ROWS, CHUNK), F32),
+            pltpu.VMEM((total, width), BF16),
+            pltpu.VMEM((total, width), BF16),
+        ],
+        flops=total * 3 * one,
+        moved=3 * one,
+    )(own, other, gate_w, up_w, down_w)
+    recv = swap(send, "local")
+    (routed_own,) = call(
+        routed_own_body,
+        [((total, feats), F32)],
+        [VMEM] * 2,
+        flops=total * one // 2,
+        moved=one // 2,
+    )(send, down_w)
+    mine, away = call(
+        second_body,
+        [((groups, RETURN_ROWS, 3 * LANES), BF16)] * 2,
+        [VMEM] * 10,
+        [pltpu.VMEM((total, RETURN_ROWS, 3 * LANES), F32)],
+        flops=total * 5 * one // 2,
+        moved=5 * one // 2,
+    )(send, recv, cot, gate, up, weight, routed_own, gate_w, up_w, down_w)
+    summed = (mine.astype(F32) + swap(away, "core").astype(F32)).astype(BF16)
+    back = lax.all_to_all(summed, ("chip", "local"), split_axis=0, concat_axis=0, tiled=True)
+    return call(
+        final_body,
+        [((1, 1, width), BF16), ((1, 1, width), BF16), (expert_ids.shape, F32)],
+        [VMEM, SMEM],
+        [pltpu.VMEM((2, RETURN_ROWS, 3 * LANES), F32)],
+    )(back, expert_ids)
 
 
 def selector(flags, capacity):
@@ -119,19 +390,18 @@
 
 
 def solution(mesh):
-    placed = (
-        P("local", "node", None),
-        P("local", "node", None),
-        P("local", "node", None),
-        P("node", None, "local"),
-        P("node", None, "local"),
-        P("node", None, "local"),
-        P("local", "node", None),
-    )
+    node, local = mesh.shape["node"], mesh.shape["local"]
+    if local == 2 and node % 2 == 0 and node <= 16:
+        mesh = Mesh(mesh.devices.reshape(node // 2, 2, local), ("chip", "core", "local"))
+        body, nodes = fast_device, ("chip", "core")
+    else:
+        body, nodes = per_device, "node"
+    rows = P("local", nodes, None)
+    weights = P(nodes, None, "local")
     return jax.shard_map(
-        per_device,
+        body,
         mesh=mesh,
-        in_specs=placed,
-        out_specs=(P("local", "node", None), P("local", "node", None), P("local", "node", None)),
+        in_specs=(rows, rows, rows, weights, weights, weights, rows),
+        out_specs=(rows, rows, rows),
         check_vma=False,
     )

time: 136 us -> 71.4 us (0.53)
  matrix products: 34.2 us -> 0 us
  Pallas kernels: 0 us -> 32.8 us
  starting transfers between devices: 23.8 us -> 0.91 us
  waiting for transfers between devices: 20 us -> 3.25 us
  between operations: 14.3 us -> 0.68 us
  other arithmetic: 6.7 us -> 0.05 us
  local copies, waits for them, and re-layouts: 5.51 us -> 2.73 us
    dot_general x13 -> x0, matrix products: 34.2 us -> none  [the longest x1 6.03 us: per_device(): lax.dot_general(gate_grad, gate_w, (((1,), (1,)), ((), ())), preferred_el...]
    pallas_call x0 -> x5, Pallas kernels: none -> 32.8 us  [the longest x1 14 us: fast_device(): call(first_body, [((total, 2 * hidden), BF16), ((total, hidden), F32), ((...]
    all_to_all x5 -> x0, starting transfers between devices: 23.7 us -> none  [the longest x1 7.36 us: per_device(): lax.all_to_all(own_flags, 'node', split_axis=0, concat_axis=0, tiled=True)]
    all_to_all x5 -> x0, waiting for transfers between devices: 19.9 us -> none  [the longest x1 7.09 us: per_device(): lax.all_to_all(scaled, 'node', split_axis=0, concat_axis=0, tiled=True)]
    all_to_all x2, blocking collectives: 19.9 us -> 30.7 us  [the longest x1 18 us: fast_device(): lax.all_to_all(packed, ('chip', 'local'), split_axis=0, concat_axis=0, ti...]
    all_gather x2 -> x0, blocking collectives: 10.6 us -> none  [the longest x1 5.7 us: per_device(): piece = lax.all_gather(packed_rows, 'local', axis=0, tiled=True)]
    ppermute x0 -> x3, waiting for transfers between devices: none -> 3.25 us  [swap(): return lax.ppermute(x, axis, [(0, 1), (1, 0)])]
    select_n x2 -> x0, other arithmetic: 1.54 us -> none  [per_device(): send_rows = jnp.where(own_flags[:, :, None] > 0, own_rows[None], zero_value)]
  transfers between devices with their start and end apart: 7 -> 3, of which waited for: 3 -> 3; matrix products, arithmetic and copies ran while one was open for 18% -> 0% of each run, Pallas kernels for 0% -> 6%
where the time goes in v1:
time: 71.4 us; the launch traced here: 71.1 us
  Pallas kernels  32.8 us (46%)
  blocking collectives  30.7 us (43%)
  waiting for transfers between devices  3.25 us (5%)
  local copies, waits for them, and re-layouts  2.73 us (4%)
  starting transfers between devices  0.91 us (1%)
    all_to_all x1, blocking collectives, fast_device(): lax.all_to_all(packed, ('chip', 'local'), split_axis=0, concat_axis=0, ti...  18 us
    pallas_call x1, Pallas kernels, fast_device(): call(first_body, [((total, 2 * hidden), BF16), ((total, hidden), F32), ((...  14 us
    all_to_all x1, blocking collectives, fast_device(): lax.all_to_all(summed, ('chip', 'local'), split_axis=0, concat_axis=0, ti...  12.7 us
    pallas_call x1, Pallas kernels, fast_device(): call(second_body, [((groups, RETURN_ROWS, 3 * LANES), BF16)] * 2, [VMEM]...  12.4 us
    pallas_call x1, Pallas kernels, fast_device(): call(routed_own_body, [((total, feats), F32)], [VMEM] * 2, flops=total *...  4.48 us
    ppermute x3, waiting for transfers between devices, swap(): return lax.ppermute(x, axis, [(0, 1), (1, 0)])  3.25 us
    unnamed x10, local copies, waits for them, and re-layouts  2.73 us
  transfers between devices with their start and end apart: 3, of which 3 were waited for; matrix products, arithmetic and copies ran while one was open for 0% of the time, Pallas kernels for 6%

profile of v1, /device:TPU:0, one launch (start us, length us, event | category | flops | bytes accessed | tf_op | source)
XLA Modules:
  0.0 71.1 jit_solution(6980796690735104745)
XLA Ops:
  0.6 0.0 copy-start
  0.6 0.7 copy-done
  1.3 0.0 copy-start.1
  1.3 0.7 copy-done.1
  2.1 0.0 copy-start.2
  2.1 0.7 copy-done.2
  2.7 0.0 copy-start.4
  2.7 0.7 copy-done.4
  3.4 0.6 shard_map.94
  4.0 18.0 %all_to_all.10.own_ref = bf16[16,16,512]{2,1,0:T(8,128)(2,1)S(1)} all-to-all(bf16[16,16,512]{2,1,0:T(8,128)(2,1)S(1)} %shard_map.94), channel_id=1, replica_groups=mesh['chip'=8,'core'=2,'local'=2] {'chip','local'}, dimensions={0} | all-to-all | bytes 524288 | tf_op jit(solution)/shard_map/all_to_all | solution.py:232
  21.9 0.0 collective-permute-start
  21.9 1.5 %collective-permute-done.other_ref = bf16[16,16,512]{2,1,0:T(8,128)(2,1)S(1)} collective-permute-done((bf16[16,16,512]{2,1,0:T(8,128)(2,1)S(1)}, bf16[16,16,512]{2,1,0:T(8,128)(2,1)S(1)}, u32[]{:S(2)}, u32[]{:S(2)}) %collective-permute-start) | collective-permute-done | bytes 262176 | tf_op jit(solution)/shard_map/ppermute | solution.py:214
  23.5 14.0 %shard_map.95 = (bf16[32,2048]{1,0:T(8,128)(2,1)S(1)}, f32[32,1024]{1,0:T(8,128)S(1)}, f32[32,1024]{1,0:T(8,128)S(1)}, f32[32,1024]{1,0:T(8,128)S(1)}, f32[32,128]{1,0:T(8,128)S(1)}) custom-call(bf16[16,16,512]{2,1,0:T(8,128)(2,1)S(1)} %all_to_all.10.own_ref, bf16[16,16,512]{2,1,0:T(8,128)(2,1)S(1)} %collective-permute-done.other_ref, ...), custom_call_target="tpu_custom_call" | custom-call | flops 704643072 | bytes 22020096 | tf_op jit(solution)/shard_map/pallas_call | solution.py:234
  37.5 0.8 %collective-permute-start.1 = (bf16[32,2048]{1,0:T(8,128)(2,1)S(1)}, bf16[32,2048]{1,0:T(8,128)(2,1)S(1)}, u32[]{:S(2)}, u32[]{:S(2)}) collective-permute-start(bf16[32,2048]{1,0:T(8,128)(2,1)S(1)} %get-tuple-element.10.send_ref), channel_id=1, source_target_pairs={{0,1},{1,0},{2,3},{3,2},{4,5},{5,4},{6,7},{7,6},{8,9},{9,8},{10,11... | collective-permute-start | bytes 393224 | tf_op jit(solution)/shard_map/ppermute | solution.py:214
  38.4 4.5 %shard_map.96.routed_in = f32[32,1792]{1,0:T(8,128)S(1)} custom-call(bf16[32,2048]{1,0:T(8,128)(2,1)S(1)} %get-tuple-element.10.send_ref, bf16[2048,1792]{1,0:T(8,128)(2,1)} %bitcast.4), custom_call_target="tpu_custom_call" | custom-call | flops 117440512 | bytes 3670016 | tf_op jit(solution)/shard_map/pallas_call | solution.py:253
  42.8 0.3 collective-permute-done.1.recv_ref
  43.1 0.0 copy-start.3
  43.1 12.4 %shard_map.97 = (bf16[16,16,384]{2,1,0:T(8,128)(2,1)S(1)}, bf16[16,16,384]{2,1,0:T(8,128)(2,1)S(1)}) custom-call(bf16[32,2048]{1,0:T(8,128)(2,1)S(1)} %get-tuple-element.10.send_ref, bf16[32,2048]{1,0:T(8,128)(2,1)S(1)} %collective-permute-done.1.recv_ref, f32[32,1024]{1,0:T(8,128)S(1)} %get-tuple-element.11.cot_ref, ...), custom_call_target="tpu_custom_call" | custom-call | flops 587202560 | bytes 18350080 | tf_op jit(solution)/shard_map/pallas_call | solution.py:260
  55.6 0.1 collective-permute-start.2
  55.7 1.4 %collective-permute-done.2 = bf16[16,16,384]{2,1,0:T(8,128)(2,1)S(1)} collective-permute-done((bf16[16,16,384]{2,1,0:T(8,128)(2,1)S(1)}, bf16[16,16,384]{2,1,0:T(8,128)(2,1)S(1)}, u32[]{:S(2)}, u32[]{:S(2)}) %collective-permute-start.2) | collective-permute-done | bytes 196640 | tf_op jit(solution)/shard_map/ppermute | solution.py:214
  57.1 0.1 add_convert_fusion
  57.1 12.7 %all_to_all.11.in_ref = bf16[16,16,384]{2,1,0:T(8,128)(2,1)S(1)} all-to-all(bf16[16,16,384]{2,1,0:T(8,128)(2,1)S(1)} %add_convert_fusion), channel_id=1, replica_groups=mesh['chip'=8,'core'=2,'local'=2] {'chip','local'}, dimensions={0} | all-to-all | bytes 393216 | tf_op jit(solution)/shard_map/all_to_all | solution.py:269
  69.9 0.0 copy-done.3
  69.9 1.2 %shard_map.98 = (bf16[1,1,3584]{2,1,0:T(2,128)(2,1)}, bf16[1,1,3584]{2,1,0:T(2,128)(2,1)}, f32[1,1,8]{2,1,0:T(1,128)}) custom-call(bf16[16,16,384]{2,1,0:T(8,128)(2,1)S(1)} %all_to_all.11.in_ref, s32[1,1,8]{2,1,0:T(1,128)S(1)} %copy-done.3), custom_call_target="tpu_custom_call" | custom-call | tf_op jit(solution)/shard_map/pallas_call | solution.py:270
Async XLA Ops:
  0.6 0.7 %copy-start = (bf16[1,1,3584]{2,1,0:T(2,128)(2,1)S(1)}, bf16[1,1,3584]{2,1,0:T(2,128)(2,1)}, u32[]{:S(2)}) copy-start(bf16[1,1,3584]{2,1,0:T(2,128)(2,1)} %tok_ref.1) | copy-start | bytes 21508
  1.3 0.7 %copy-start.1 = (bf16[1,1,3584]{2,1,0:T(2,128)(2,1)S(1)}, bf16[1,1,3584]{2,1,0:T(2,128)(2,1)}, u32[]{:S(2)}) copy-start(bf16[1,1,3584]{2,1,0:T(2,128)(2,1)} %grad_ref.1) | copy-start | bytes 21508
  2.1 0.7 copy-start.2
  2.7 0.7 copy-start.4
  21.9 1.5 %collective-permute-start = (bf16[16,16,512]{2,1,0:T(8,128)(2,1)S(1)}, bf16[16,16,512]{2,1,0:T(8,128)(2,1)S(1)}, u32[]{:S(2)}, u32[]{:S(2)}) collective-permute-start(bf16[16,16,512]{2,1,0:T(8,128)(2,1)S(1)} %all_to_all.10.own_ref), channel_id=1, source_target_pairs={{0,2},{2,0},{1,3},{3,1},{4,6},{6,4},{5,7},{7,5},{8,10},{10,8},{9,1... | collective-permute-start | bytes 786440 | tf_op jit(solution)/shard_map/ppermute | solution.py:214
  37.5 5.6 %collective-permute-start.1 = (bf16[32,2048]{1,0:T(8,128)(2,1)S(1)}, bf16[32,2048]{1,0:T(8,128)(2,1)S(1)}, u32[]{:S(2)}, u32[]{:S(2)}) collective-permute-start(bf16[32,2048]{1,0:T(8,128)(2,1)S(1)} %get-tuple-element.10.send_ref), channel_id=1, source_target_pairs={{0,1},{1,0},{2,3},{3,2},{4,5},{5,4},{6,7},{7,6},{8,9},{9,8},{10,11... | collective-permute-start | bytes 393224 | tf_op jit(solution)/shard_map/ppermute | solution.py:214
  43.1 26.7 %copy-start.3 = (s32[1,1,8]{2,1,0:T(1,128)S(1)}, s32[1,1,8]{2,1,0:T(1,128)}, u32[]{:S(2)}) copy-start(s32[1,1,8]{2,1,0:T(1,128)} %ids_ref.3) | copy-start | bytes 100
  55.6 1.5 %collective-permute-start.2 = (bf16[16,16,384]{2,1,0:T(8,128)(2,1)S(1)}, bf16[16,16,384]{2,1,0:T(8,128)(2,1)S(1)}, u32[]{:S(2)}, u32[]{:S(2)}) collective-permute-start(bf16[16,16,384]{2,1,0:T(8,128)(2,1)S(1)} %get-tuple-element.16), channel_id=1, source_target_pairs={{0,2},{2,0},{1,3},{3,1},{4,6},{6,4},{5,7},{7,5},{8,10},{10,8},{9,1... | collective-permute-start | bytes 589832 | tf_op jit(solution)/shard_map/ppermute | solution.py:214

commit v2 on v0

--- a/solution.py
+++ b/solution.py
@@ -1,7 +1,364 @@
+import functools
+
 import jax
 import jax.numpy as jnp
 from jax import lax
+from jax.experimental import pallas as pl
+from jax.experimental.pallas import tpu as pltpu
+from jax.sharding import Mesh
 from jax.sharding import PartitionSpec as P
+
+BF16 = jnp.bfloat16
+F32 = jnp.float32
+LANES = 128
+COLS = 256
+ROWS = 16
+SPAN = COLS + LANES
+
+NT = (((1,), (1,)), ((), ()))
+VMEM = pl.BlockSpec(memory_space=pltpu.VMEM)
+ANY = pl.BlockSpec(memory_space=pl.ANY)
+SMEM = pl.BlockSpec(memory_space=pltpu.SMEM)
+
+
+def call(body, outs, ins, scratch=(), products=0, moved=0):
+    return pl.pallas_call(
+        body,
+        out_shape=tuple(outs),
+        in_specs=ins,
+        out_specs=tuple(VMEM for _ in outs),
+        scratch_shapes=list(scratch),
+        compiler_params=pltpu.CompilerParams(vmem_limit_bytes=12 << 20),
+        cost_estimate=pl.CostEstimate(
+            flops=int(products), bytes_accessed=int(moved), transcendentals=0
+        ),
+    )
+
+
+def shaped(shape, dtype):
+    return jax.ShapeDtypeStruct(shape, dtype)
+
+
+def in_hbm(*arrays):
+    return tuple(pltpu.with_memory_space_constraint(a, pltpu.HBM) for a in arrays)
+
+
+def dot(a, b):
+    return jnp.dot(a, b, preferred_element_type=F32)
+
+
+def dot_nt(a, b):
+    return lax.dot_general(a, b, NT, preferred_element_type=F32)
+
+
+def high_low(x):
+    high = x.astype(BF16).astype(F32)
+    return high, x - high
+
+
+def pack_body(
+    ids_hbm, probs_hbm, tok_hbm, grad_hbm, out_ref, wide, ids_ref, probs_ref, tok_ref, grad_ref, sems
+):
+    pairs = ((ids_hbm, ids_ref), (probs_hbm, probs_ref), (tok_hbm, tok_ref), (grad_hbm, grad_ref))
+    copies = [pltpu.make_async_copy(a, b, sems.at[i]) for i, (a, b) in enumerate(pairs)]
+    for copy in copies:
+        copy.start()
+    wide[...] = jnp.zeros_like(wide)
+    lane = lax.broadcasted_iota(jnp.int32, (1, LANES), 1)
+    weight = jnp.zeros((1, LANES), F32)
+    for copy in copies:
+        copy.wait()
+    for k in range(ids_ref.shape[2]):
+        weight = jnp.where(lane == ids_ref[0, 0, k], probs_ref[0, 0, k], weight)
+    width = tok_ref.shape[2]
+    meta = width // COLS
+    half = width // 2
+    for i in range(meta):
+        wide[i : i + 1, 0:COLS] = tok_ref[0, :, i * COLS : (i + 1) * COLS].astype(F32)
+    high, low = high_low(weight)
+    wide[meta : meta + 1, 0:LANES] = high
+    wide[meta : meta + 1, LANES:COLS] = low
+    for j in range(2):
+        for i in range(half // LANES):
+            at = j * half + i * LANES
+            wide[i : i + 1, COLS:SPAN] = grad_ref[0, :, at : at + LANES].astype(F32)
+        block = wide[...].astype(BF16)
+        for i in range(j, out_ref.shape[0], 2):
+            out_ref[i] = block
+
+
+def cot_body(
+    own_ref, other_ref, down_hbm, gate_hbm,
+    away_ref, cot_ref, weight_out, rows, down_ref, gate_ref,
+    wide, grads, sems,
+):
+    count = own_ref.shape[0]
+    width = rows.shape[1]
+    hidden = cot_ref.shape[1]
+    feats = down_ref.shape[1]
+    local = lax.axis_index("local")
+    expert = lax.axis_index("chip") * 2 + lax.axis_index("core")
+    steps = hidden // COLS
+    copies = []
+    for n in range(2 * steps):
+        base = (1 - local) * hidden if n < steps else local * hidden
+        at = pl.ds(pl.multiple_of(base + (n % steps) * COLS, COLS), COLS)
+        copies.append((pltpu.make_async_copy(down_hbm.at[0, at, :], down_ref.at[at, :], sems.at[n]), at))
+    gate_copy = pltpu.make_async_copy(
+        gate_hbm.at[0, :, 0 : gate_ref.shape[1]], gate_ref, sems.at[2 * steps]
+    )
+    for copy, _ in copies:
+        copy.start()
+    gate_copy.start()
+    lane = lax.broadcasted_iota(jnp.int32, (count, LANES), 1)
+    meta = width // COLS
+    for half, ref in enumerate((own_ref, other_ref)):
+        at = pl.ds(half * count, count)
+        wide[...] = ref[...].astype(F32)
+        for i in range(meta):
+            rows[at, i * COLS : (i + 1) * COLS] = wide[:, i, 0:COLS].astype(BF16)
+        for i in range(feats // LANES):
+            grads[at, i * LANES : (i + 1) * LANES] = wide[:, i, COLS:SPAN].astype(BF16)
+        both = wide[:, meta, 0:LANES] + wide[:, meta, LANES:COLS]
+        both = jnp.sum(jnp.where(lane == expert, both, 0.0), axis=1, keepdims=True)
+        weight_out[at, :] = jnp.broadcast_to(both, (count, LANES))
+    grad = grads[...]
+    for n, (copy, at) in enumerate(copies):
+        copy.wait()
+        part = dot_nt(grad, down_ref[at, :])
+        cols = slice((n % steps) * COLS, (n % steps + 1) * COLS)
+        if n < steps:
+            away_ref[:, cols] = part.astype(BF16)
+        else:
+            cot_ref[:, cols] = part
+    gate_copy.wait()
+
+
+def forward_body(
+    rows_ref, first_ref, gate_hbm, up_hbm,
+    gate_out, up_out, act_ref, second_ref, up_ref,
+    sems,
+):
+    split = first_ref.shape[1]
+    hidden = up_ref.shape[1]
+    steps = hidden // COLS
+    ups, gates = [], []
+    for n in range(steps):
+        cols = slice(n * COLS, (n + 1) * COLS)
+        ups.append(pltpu.make_async_copy(up_hbm.at[0, :, cols], up_ref.at[:, cols], sems.at[n]))
+        if n * COLS >= split:
+            into = slice(n * COLS - split, (n + 1) * COLS - split)
+            gates.append(
+                pltpu.make_async_copy(
+                    gate_hbm.at[0, :, cols], second_ref.at[:, into], sems.at[steps + n]
+                )
+            )
+        else:
+            gates.append(None)
+    for n in range(steps):
+        ups[n].start()
+        if gates[n] is not None:
+            gates[n].start()
+    tokens = rows_ref[...]
+    for n in range(steps):
+        cols = slice(n * COLS, (n + 1) * COLS)
+        if gates[n] is not None:
+            gates[n].wait()
+            weight = second_ref[:, n * COLS - split : (n + 1) * COLS - split]
+        else:
+            weight = first_ref[:, cols]
+        gate = dot(tokens, weight)
+        ups[n].wait()
+        up = dot(tokens, up_ref[:, cols])
+        gate_out[:, cols] = gate
+        up_out[:, cols] = up
+        act_ref[:, cols] = (gate * jax.nn.sigmoid(gate) * up).astype(BF16)
+
+
+def input_body(
+    cot_ref, recv_ref, gate_in, up_in, act_ref, weight_in, first_ref, second_ref, up_ref,
+    mine_ref, other_ref,
+    wide,
+):
+    total = cot_ref.shape[0]
+    count = total // 2
+    width = up_ref.shape[0]
+    split = first_ref.shape[1]
+    expert = lax.axis_index("chip") * 2 + lax.axis_index("core")
+    gate, up = gate_in[...], up_in[...]
+    sig = jax.nn.sigmoid(gate)
+    cot = cot_ref[...] + recv_ref[...].astype(F32)
+    prob = jnp.sum(cot * act_ref[...].astype(F32), axis=1, keepdims=True)
+    hidden_grad = cot * weight_in[:, 0:1]
+    gate_grad = (hidden_grad * up * sig * (1.0 + gate * (1.0 - sig))).astype(BF16)
+    up_grad = (hidden_grad * (gate * sig)).astype(BF16)
+    steps = width // COLS
+    for n in range(steps):
+        at = slice(n * COLS, (n + 1) * COLS)
+        wide[:, n, :] = (
+            dot_nt(gate_grad[:, :split], first_ref[at, :])
+            + dot_nt(gate_grad[:, split:], second_ref[at, :])
+            + dot_nt(up_grad, up_ref[at, :])
+        )
+    lane = lax.broadcasted_iota(jnp.int32, (total, LANES), 1)
+    high, low = high_low(jnp.where(lane == expert, prob, 0.0))
+    wide[:, steps, 0:LANES] = high
+    wide[:, steps, LANES:COLS] = low
+    for n in range(steps + 1, ROWS):
+        wide[:, n, :] = jnp.zeros((total, COLS), F32)
+    mine_ref[...] = wide[:count].astype(BF16)
+    other_ref[...] = wide[count:].astype(BF16)
+
+
+def routed_body(act_ref, recv_ref, weight_in, down_ref, after_ref, mine_ref, other_ref, wide):
+    total, hidden = act_ref.shape
+    count = total // 2
+    feats = down_ref.shape[1]
+    local = lax.axis_index("local")
+    weight = weight_in[:, 0:1]
+    act, recv = act_ref[...], recv_ref[...]
+    own = pl.ds(pl.multiple_of(local * hidden, COLS), hidden)
+    away = pl.ds(pl.multiple_of((1 - local) * hidden, COLS), hidden)
+    for n in range(feats // COLS):
+        cols = slice(n * COLS, (n + 1) * COLS)
+        part = dot(act, down_ref[own, cols]) + dot(recv, down_ref[away, cols])
+        part = part.astype(BF16).astype(F32) * weight
+        wide[:, 2 * n, :] = part[:, :LANES]
+        wide[:, 2 * n + 1, :] = part[:, LANES:]
+    for n in range(feats // LANES, ROWS):
+        wide[:, n, :] = jnp.zeros((total, LANES), F32)
+    mine_ref[...] = wide[:count].astype(BF16)
+    other_ref[...] = wide[count:].astype(BF16)
+
+
+def final_body(in_ref, ids_ref, comb_ref, grad_ref, prob_ref, wide):
+    groups = in_ref.shape[0]
+    width = comb_ref.shape[2]
+    half = width // 2
+    for j in range(2):
+        total = in_ref[j].astype(F32)
+        for i in range(j + 2, groups, 2):
+            total = total + in_ref[i].astype(F32)
+        wide[j] = total
+    meta = width // COLS
+    for c in range(meta):
+        grad_ref[0, :, c * COLS : (c + 1) * COLS] = (
+            wide[0, c : c + 1, 0:COLS] + wide[1, c : c + 1, 0:COLS]
+        ).astype(BF16)
+    for j in range(2):
+        for c in range(half // LANES):
+            at = j * half + c * LANES
+            comb_ref[0, :, at : at + LANES] = wide[j, c : c + 1, COLS:SPAN].astype(BF16)
+    prob = wide[0, meta : meta + 1, 0:COLS] + wide[1, meta : meta + 1, 0:COLS]
+    prob = prob[:, 0:LANES] + prob[:, LANES:COLS]
+    lane = lax.broadcasted_iota(jnp.int32, (1, LANES), 1)
+    top = ids_ref.shape[2]
+    out = jnp.zeros((1, LANES), F32)
+    for k in range(top):
+        value = jnp.sum(jnp.where(lane == ids_ref[0, 0, k], prob, 0.0), axis=1, keepdims=True)
+        out = jnp.where(lane == k, value, out)
+    prob_ref[0] = out[:, :top]
+
+
+def swap(x, axis):
+    return lax.ppermute(x, axis, [(0, 1), (1, 0)])
+
+
+def fast_device(tokens, expert_ids, route_probs, gate_weight, up_weight, down_weight, out_grad):
+    groups = lax.axis_size("chip") * 2
+    total = 2 * groups
+    width = tokens.shape[2]
+    hidden = gate_weight.shape[2]
+    feats = down_weight.shape[2]
+    split = hidden // 2
+    one = width * hidden * 2
+    gate_hbm, up_hbm, down_hbm = in_hbm(gate_weight, up_weight, down_weight)
+    (packed,) = call(
+        pack_body,
+        [shaped((groups, ROWS, SPAN), BF16)],
+        [ANY] * 4,
+        [
+            pltpu.VMEM((ROWS, SPAN), F32),
+            pltpu.SMEM(expert_ids.shape, expert_ids.dtype),
+            pltpu.SMEM(route_probs.shape, route_probs.dtype),
+            pltpu.VMEM(tokens.shape, BF16),
+            pltpu.VMEM(out_grad.shape, BF16),
+            pltpu.SemaphoreType.DMA((4,)),
+        ],
+    )(*in_hbm(expert_ids, route_probs, tokens, out_grad))
+    own = lax.all_to_all(packed, ("chip", "local"), split_axis=0, concat_axis=0, tiled=True)
+    other = swap(own, "core")
+    away, cot, weight, rows, down_w, gate_first = call(
+        cot_body,
+        [
+            shaped((total, hidden), BF16),
+            shaped((total, hidden), F32),
+            shaped((total, LANES), F32),
+            shaped((total, width), BF16),
+            pltpu.VMEM((2 * hidden, feats), BF16),
+            pltpu.VMEM((width, split), BF16),
+        ],
+        [VMEM, VMEM, ANY, ANY],
+        [
+            pltpu.VMEM((groups, ROWS, SPAN), F32),
+            pltpu.VMEM((total, feats), BF16),
+            pltpu.SemaphoreType.DMA((2 * hidden // COLS + 1,)),
+        ],
+        products=total * one,
+        moved=3 * one // 2,
+    )(own, other, down_hbm, gate_hbm)
+    cot_recv = swap(away, "local")
+    gate, up, act, gate_second, up_w = call(
+        forward_body,
+        [
+            shaped((total, hidden), F32),
+            shaped((total, hidden), F32),
+            shaped((total, hidden), BF16),
+            pltpu.VMEM((width, hidden - split), BF16),
+            pltpu.VMEM((width, hidden), BF16),
+        ],
+        [VMEM, VMEM, ANY, ANY],
+        [pltpu.SemaphoreType.DMA((2 * hidden // COLS,))],
+        products=total * 2 * one,
+        moved=3 * one // 2,
+    )(rows, gate_first, gate_hbm, up_hbm)
+    act_recv = swap(act, "local")
+    in_mine, in_away = call(
+        input_body,
+        [shaped((groups, ROWS, COLS), BF16)] * 2,
+        [VMEM] * 9,
+        [pltpu.VMEM((total, ROWS, COLS), F32)],
+        products=total * 2 * one,
+        moved=2 * one,
+    )(cot, cot_recv, gate, up, act, weight, gate_first, gate_second, up_w)
+    in_recv = swap(in_away, "core")
+    routed_mine, routed_away = call(
+        routed_body,
+        [shaped((groups, ROWS, LANES), BF16)] * 2,
+        [VMEM] * 4 + [ANY],
+        [pltpu.VMEM((total, ROWS, LANES), F32)],
+        products=total * one,
+        moved=one,
+    )(act, act_recv, weight, down_w, in_mine)
+    routed_recv = swap(routed_away, "core")
+    summed = jnp.concatenate(
+        [
+            (in_mine.astype(F32) + in_recv.astype(F32)).astype(BF16),
+            (routed_mine.astype(F32) + routed_recv.astype(F32)).astype(BF16),
+        ],
+        axis=2,
+    )
+    back = lax.all_to_all(summed, ("chip", "local"), split_axis=0, concat_axis=0, tiled=True)
+    return call(
+        final_body,
+        [
+            shaped((1, 1, width), BF16),
+            shaped((1, 1, width), BF16),
+            shaped(expert_ids.shape, F32),
+        ],
+        [VMEM, SMEM],
+        [pltpu.VMEM((2, ROWS, SPAN), F32)],
+    )(back, expert_ids)
 
 
 def selector(flags, capacity):
@@ -119,19 +476,18 @@
 
 
 def solution(mesh):
-    placed = (
-        P("local", "node", None),
-        P("local", "node", None),
-        P("local", "node", None),
-        P("node", None, "local"),
-        P("node", None, "local"),
-        P("node", None, "local"),
-        P("local", "node", None),
-    )
+    node, local = mesh.shape["node"], mesh.shape["local"]
+    if local == 2 and node % 2 == 0 and node <= 16:
+        mesh = Mesh(mesh.devices.reshape(node // 2, 2, local), ("chip", "core", "local"))
+        body, nodes = fast_device, ("chip", "core")
+    else:
+        body, nodes = per_device, "node"
+    rows = P("local", nodes, None)
+    weights = P(nodes, None, "local")
     return jax.shard_map(
-        per_device,
+        body,
         mesh=mesh,
-        in_specs=placed,
-        out_specs=(P("local", "node", None), P("local", "node", None), P("local", "node", None)),
+        in_specs=(rows, rows, rows, weights, weights, weights, rows),
+        out_specs=(rows, rows, rows),
         check_vma=False,
     )

time: 136 us -> 54.9 us (0.40)
  matrix products: 34.2 us -> 0 us
  starting transfers between devices: 23.8 us -> 2.73 us
  Pallas kernels: 0 us -> 19.6 us
  waiting for transfers between devices: 20 us -> 2.4 us
  between operations: 14.3 us -> 0.71 us
  other arithmetic: 6.7 us -> 0.08 us
  local copies, waits for them, and re-layouts: 5.51 us -> 0.01 us
  blocking collectives: 30.5 us -> 29.1 us
    dot_general x13 -> x0, matrix products: 34.2 us -> none  [the longest x1 6.03 us: per_device(): lax.dot_general(gate_grad, gate_w, (((1,), (1,)), ((), ())), preferred_el...]
    all_to_all x5 -> x0, starting transfers between devices: 23.7 us -> none  [the longest x1 7.36 us: per_device(): lax.all_to_all(own_flags, 'node', split_axis=0, concat_axis=0, tiled=True)]
    all_to_all x5 -> x0, waiting for transfers between devices: 19.9 us -> none  [the longest x1 7.09 us: per_device(): lax.all_to_all(scaled, 'node', split_axis=0, concat_axis=0, tiled=True)]
    pallas_call x0 -> x6, Pallas kernels: none -> 19.6 us  [the longest x1 6.03 us: fast_device(): call(cot_body, [shaped((total, hidden), BF16), shaped((total, hidden), F3...]
    all_gather x2 -> x0, blocking collectives: 10.6 us -> none  [the longest x1 5.7 us: per_device(): piece = lax.all_gather(packed_rows, 'local', axis=0, tiled=True)]
    all_to_all x2, blocking collectives: 19.9 us -> 29.1 us  [the longest x1 16.8 us: fast_device(): lax.all_to_all(packed, ('chip', 'local'), split_axis=0, concat_axis=0, ti...]
    ppermute x0 -> x5, starting transfers between devices: none -> 2.73 us  [swap(): return lax.ppermute(x, axis, [(0, 1), (1, 0)])]
    unnamed x16 -> x2, local copies, waits for them, and re-layouts: 2.42 us -> 0.01 us
  transfers between devices with their start and end apart: 7 -> 5, of which waited for: 3 -> 3; matrix products, arithmetic and copies ran while one was open for 18% -> 0% of each run, Pallas kernels for 0% -> 19%
where the time goes in v2:
time: 54.9 us; the launch traced here: 54.6 us
  blocking collectives  29.1 us (53%)
  Pallas kernels  19.6 us (36%)
  starting transfers between devices  2.73 us (5%)
  waiting for transfers between devices  2.4 us (4%)
  between operations  0.71 us (1%)
    all_to_all x1, blocking collectives, fast_device(): lax.all_to_all(packed, ('chip', 'local'), split_axis=0, concat_axis=0, ti...  16.8 us
    all_to_all x1, blocking collectives, fast_device(): lax.all_to_all(summed, ('chip', 'local'), split_axis=0, concat_axis=0, ti...  12.3 us
    pallas_call x1, Pallas kernels, fast_device(): call(cot_body, [shaped((total, hidden), BF16), shaped((total, hidden), F3...  6.03 us
    pallas_call x1, Pallas kernels, fast_device(): call(forward_body, [shaped((total, hidden), F32), shaped((total, hidden),...  5.66 us
    pallas_call x1, Pallas kernels, fast_device(): call(input_body, [shaped((groups, ROWS, COLS), BF16)] * 2, [VMEM] * 9, [p...  4.46 us
    ppermute x5, starting transfers between devices, swap(): return lax.ppermute(x, axis, [(0, 1), (1, 0)])  2.73 us
    ppermute x5, waiting for transfers between devices, swap(): return lax.ppermute(x, axis, [(0, 1), (1, 0)])  2.4 us
    pallas_call x1, Pallas kernels, fast_device(): call(routed_body, [shaped((groups, ROWS, LANES), BF16)] * 2, [VMEM] * 4 +...  1.44 us
  transfers between devices with their start and end apart: 5, of which 3 were waited for; matrix products, arithmetic and copies ran while one was open for 0% of the time, Pallas kernels for 19%

profile of v2, /device:TPU:0, one launch (start us, length us, event | category | flops | bytes accessed | tf_op | source)
XLA Modules:
  0.0 54.6 jit_solution(13574151334374598585)
XLA Ops:
  0.6 0.8 %shard_map.94 = bf16[16,16,384]{2,1,0:T(8,128)(2,1)S(1)} custom-call(s32[1,1,8]{2,1,0:T(1,128)} %ids_ref.1, f32[1,1,8]{2,1,0:T(1,128)} %probs_hbm.1, bf16[1,1,3584]{2,1,0:T(2,128)(2,1)} %tok_hbm.1, bf16[1,1,3584]{2,1,0:T(2,128)(2,1)} %grad_hbm.1), custom_call_target="tpu_custom_call" | custom-call | tf_op jit(solution)/shard_map/pallas_call | solution.py:276
  1.4 16.8 %all_to_all.10.own_ref = bf16[16,16,384]{2,1,0:T(8,128)(2,1)S(1)} all-to-all(bf16[16,16,384]{2,1,0:T(8,128)(2,1)S(1)} %shard_map.94), channel_id=1, replica_groups=mesh['chip'=8,'core'=2,'local'=2] {'chip','local'}, dimensions={0} | all-to-all | bytes 393216 | tf_op jit(solution)/shard_map/all_to_all | solution.py:289
  18.2 0.0 collective-permute-start
  18.2 1.4 %collective-permute-done.other_ref = bf16[16,16,384]{2,1,0:T(8,128)(2,1)S(1)} collective-permute-done((bf16[16,16,384]{2,1,0:T(8,128)(2,1)S(1)}, bf16[16,16,384]{2,1,0:T(8,128)(2,1)S(1)}, u32[]{:S(2)}, u32[]{:S(2)}) %collective-permute-start) | collective-permute-done | bytes 196640 | tf_op jit(solution)/shard_map/ppermute | solution.py:264
  19.6 6.0 %shard_map.95 = (bf16[32,1024]{1,0:T(8,128)(2,1)S(1)}, f32[32,1024]{1,0:T(8,128)S(1)}, f32[32,128]{1,0:T(8,128)S(1)}, bf16[32,3584]{1,0:T(8,128)(2,1)S(1)}, bf16...) custom-call(bf16[16,16,384]{2,1,0:T(8,128)(2,1)S(1)} %all_to_all.10.own_ref, ...), custom_call_target="tpu_custom_call" | custom-call | flops 234881024 | bytes 11010048 | tf_op jit(solution)/shard_map/pallas_call | solution.py:291
  25.7 1.0 %collective-permute-start.1 = (bf16[32,1024]{1,0:T(8,128)(2,1)S(1)}, bf16[32,1024]{1,0:T(8,128)(2,1)S(1)}, u32[]{:S(2)}, u32[]{:S(2)}) collective-permute-start(bf16[32,1024]{1,0:T(8,128)(2,1)S(1)} %get-tuple-element.19), channel_id=1, source_target_pairs={{0,1},{1,0},{2,3},{3,2},{4,5},{5,4},{6,7},{7,6},{8,9},{9,8},{10,11... | collective-permute-start | bytes 196616 | tf_op jit(solution)/shard_map/ppermute | solution.py:264
  26.7 5.7 %shard_map.96 = (f32[32,1024]{1,0:T(8,128)S(1)}, f32[32,1024]{1,0:T(8,128)S(1)}, bf16[32,1024]{1,0:T(8,128)(2,1)S(1)}, bf16[3584,512]{1,0:T(8,128)(2,1)S(1)}, bf16[3584,1024]{1,0:T(8,128)(2,1)S(1)}) custom-call(bf16[32,3584]{1,0:T(8,128)(2,1)S(1)} %get-tuple-element.20.rows_ref, bf16[3584,512]{1,0:T(8,128)(2,1)S(1)} %get-tuple-element.21.first_ref, ...), custom_call_target="tpu_custom_call" | custom-call | flops 469762048 | bytes 11010048 | tf_op jit(solution)/shard_map/pallas_call | solution.py:311
  32.4 1.1 %collective-permute-start.3 = (bf16[32,1024]{1,0:T(8,128)(2,1)S(1)}, bf16[32,1024]{1,0:T(8,128)(2,1)S(1)}, u32[]{:S(2)}, u32[]{:S(2)}) collective-permute-start(bf16[32,1024]{1,0:T(8,128)(2,1)S(1)} %get-tuple-element.24.act_ref), channel_id=1, source_target_pairs={{0,1},{1,0},{2,3},{3,2},{4,5},{5,4},{6,7},{7,6},{8,9},{9,8},{10,11... | collective-permute-start | bytes 196616 | tf_op jit(solution)/shard_map/ppermute | solution.py:264
  33.5 0.0 collective-permute-done.1.recv_ref
  33.5 4.5 %shard_map.97 = (bf16[16,16,256]{2,1,0:T(8,128)(2,1)S(1)}, bf16[16,16,256]{2,1,0:T(8,128)(2,1)S(1)}) custom-call(f32[32,1024]{1,0:T(8,128)S(1)} %get-tuple-element.18.cot_ref, bf16[32,1024]{1,0:T(8,128)(2,1)S(1)} %collective-permute-done.1.recv_ref, f32[32,1024]{1,0:T(8,128)S(1)} %get-tuple-element.22.gate_in, f32[32,1024]{1,0:T(8,128)S(1)} %get-tuple-element.23.up_in, ...), custom_call_target="tpu_custom_call" | custom-call | flops 469762048 | bytes 14680064 | tf_op jit(solution)/shard_map/pallas_call | solution.py:326
  38.0 0.0 copy-start
  38.0 0.0 collective-permute-done.3.recv_ref
  38.0 1.4 %shard_map.98 = (bf16[16,16,128]{2,1,0:T(8,128)(2,1)S(1)}, bf16[16,16,128]{2,1,0:T(8,128)(2,1)S(1)}) custom-call(bf16[32,1024]{1,0:T(8,128)(2,1)S(1)} %get-tuple-element.24.act_ref, bf16[32,1024]{1,0:T(8,128)(2,1)S(1)} %collective-permute-done.3.recv_ref, f32[32,128]{1,0:T(8,128)S(1)} %get-tuple-element.25.weight_in, ...), custom_call_target="tpu_custom_call" | custom-call | flops 234881024 | bytes 7340032 | tf_op jit(solution)/shard_map/pallas_call | solution.py:335
  39.4 0.1 collective-permute-start.4
  39.5 0.5 collective-permute-start.2
  40.0 0.7 %collective-permute-done.4 = bf16[16,16,128]{2,1,0:T(8,128)(2,1)S(1)} collective-permute-done((bf16[16,16,128]{2,1,0:T(8,128)(2,1)S(1)}, bf16[16,16,128]{2,1,0:T(8,128)(2,1)S(1)}, u32[]{:S(2)}, u32[]{:S(2)}) %collective-permute-start.4) | collective-permute-done | bytes 65568 | tf_op jit(solution)/shard_map/ppermute | solution.py:264
  40.8 0.2 collective-permute-done.2
  41.1 12.3 %all_to_all.11.in_ref = bf16[16,16,384]{2,1,0:T(8,128)(2,1)S(1)} all-to-all(bf16[16,16,384]{2,1,0:T(8,128)(2,1)S(1)} %pad_maximum_fusion), channel_id=1, replica_groups=mesh['chip'=8,'core'=2,'local'=2] {'chip','local'}, dimensions={0} | all-to-all | bytes 393216 | tf_op jit(solution)/shard_map/all_to_all | solution.py:351
  53.4 0.0 copy-done
  53.4 1.2 %shard_map.99 = (bf16[1,1,3584]{2,1,0:T(2,128)(2,1)}, bf16[1,1,3584]{2,1,0:T(2,128)(2,1)}, f32[1,1,8]{2,1,0:T(1,128)}) custom-call(bf16[16,16,384]{2,1,0:T(8,128)(2,1)S(1)} %all_to_all.11.in_ref, s32[1,1,8]{2,1,0:T(1,128)S(1)} %copy-done), custom_call_target="tpu_custom_call" | custom-call | tf_op jit(solution)/shard_map/pallas_call | solution.py:352
  (3 shorter events, 0.1 us)
Async XLA Ops:
  18.2 1.4 %collective-permute-start = (bf16[16,16,384]{2,1,0:T(8,128)(2,1)S(1)}, bf16[16,16,384]{2,1,0:T(8,128)(2,1)S(1)}, u32[]{:S(2)}, u32[]{:S(2)}) collective-permute-start(bf16[16,16,384]{2,1,0:T(8,128)(2,1)S(1)} %all_to_all.10.own_ref), channel_id=1, source_target_pairs={{0,2},{2,0},{1,3},{3,1},{4,6},{6,4},{5,7},{7,5},{8,10},{10,8},{9,1... | collective-permute-start | bytes 589832 | tf_op jit(solution)/shard_map/ppermute | solution.py:264
  25.7 7.8 %collective-permute-start.1 = (bf16[32,1024]{1,0:T(8,128)(2,1)S(1)}, bf16[32,1024]{1,0:T(8,128)(2,1)S(1)}, u32[]{:S(2)}, u32[]{:S(2)}) collective-permute-start(bf16[32,1024]{1,0:T(8,128)(2,1)S(1)} %get-tuple-element.19), channel_id=1, source_target_pairs={{0,1},{1,0},{2,3},{3,2},{4,5},{5,4},{6,7},{7,6},{8,9},{9,8},{10,11... | collective-permute-start | bytes 196616 | tf_op jit(solution)/shard_map/ppermute | solution.py:264
  32.4 5.6 %collective-permute-start.3 = (bf16[32,1024]{1,0:T(8,128)(2,1)S(1)}, bf16[32,1024]{1,0:T(8,128)(2,1)S(1)}, u32[]{:S(2)}, u32[]{:S(2)}) collective-permute-start(bf16[32,1024]{1,0:T(8,128)(2,1)S(1)} %get-tuple-element.24.act_ref), channel_id=1, source_target_pairs={{0,1},{1,0},{2,3},{3,2},{4,5},{5,4},{6,7},{7,6},{8,9},{9,8},{10,11... | collective-permute-start | bytes 196616 | tf_op jit(solution)/shard_map/ppermute | solution.py:264
  38.0 15.4 %copy-start = (s32[1,1,8]{2,1,0:T(1,128)S(1)}, s32[1,1,8]{2,1,0:T(1,128)}, u32[]{:S(2)}) copy-start(s32[1,1,8]{2,1,0:T(1,128)} %ids_ref.1) | copy-start | bytes 100
  39.4 1.3 %collective-permute-start.4 = (bf16[16,16,128]{2,1,0:T(8,128)(2,1)S(1)}, bf16[16,16,128]{2,1,0:T(8,128)(2,1)S(1)}, u32[]{:S(2)}, u32[]{:S(2)}) collective-permute-start(bf16[16,16,128]{2,1,0:T(8,128)(2,1)S(1)} %get-tuple-element.32), channel_id=1, source_target_pairs={{0,2},{2,0},{1,3},{3,1},{4,6},{6,4},{5,7},{7,5},{8,10},{10,8},{9,1... | collective-permute-start | bytes 196616 | tf_op jit(solution)/shard_map/ppermute | solution.py:264
  39.5 1.5 %collective-permute-start.2 = (bf16[16,16,256]{2,1,0:T(8,128)(2,1)S(1)}, bf16[16,16,256]{2,1,0:T(8,128)(2,1)S(1)}, u32[]{:S(2)}, u32[]{:S(2)}) collective-permute-start(bf16[16,16,256]{2,1,0:T(8,128)(2,1)S(1)} %get-tuple-element.29), channel_id=1, source_target_pairs={{0,2},{2,0},{1,3},{3,1},{4,6},{6,4},{5,7},{7,5},{8,10},{10,8},{9,1... | collective-permute-start | bytes 393224 | tf_op jit(solution)/shard_map/ppermute | solution.py:264

commit v3 on v2

--- a/solution.py
+++ b/solution.py
@@ -1,4 +1,5 @@
 import functools
+import math
 
 import jax
 import jax.numpy as jnp
@@ -14,6 +15,7 @@
 COLS = 256
 ROWS = 16
 SPAN = COLS + LANES
+TAKE = 2 * COLS
 
 NT = (((1,), (1,)), ((), ()))
 VMEM = pl.BlockSpec(memory_space=pltpu.VMEM)
@@ -79,115 +81,136 @@
     wide[meta : meta + 1, 0:LANES] = high
     wide[meta : meta + 1, LANES:COLS] = low
     for j in range(2):
+        cols = slice(COLS + j * LANES, COLS + (j + 1) * LANES)
         for i in range(half // LANES):
             at = j * half + i * LANES
-            wide[i : i + 1, COLS:SPAN] = grad_ref[0, :, at : at + LANES].astype(F32)
-        block = wide[...].astype(BF16)
-        for i in range(j, out_ref.shape[0], 2):
-            out_ref[i] = block
+            wide[i : i + 1, cols] = grad_ref[0, :, at : at + LANES].astype(F32)
+    out_ref[0] = wide[...].astype(BF16)
+
+
+def load_body(*refs, parts):
+    count = len(parts)
+    sems = refs[-1]
+    copies = []
+    for i, (rows, cols) in enumerate(parts):
+        src = refs[i].at[0, slice(*rows), slice(*cols)]
+        copies.append(pltpu.make_async_copy(src, refs[count + 1 + i], sems.at[i]))
+    for copy in copies:
+        copy.start()
+    refs[-2][...] = jnp.zeros_like(refs[-2])
+    for copy in copies:
+        copy.wait()
+
+
+def load(parts, after):
+    bounds = tuple((rows, cols) for _, rows, cols in parts)
+    shapes = [(r[1] - r[0], c[1] - c[0]) for r, c in bounds]
+    return call(
+        functools.partial(load_body, parts=bounds),
+        [pltpu.VMEM(shape, BF16) for shape in shapes] + [pltpu.VMEM((8, LANES), F32)],
+        [ANY] * (len(parts) + 1),
+        [pltpu.SemaphoreType.DMA((len(parts),))],
+        moved=sum(4 * a * b for a, b in shapes),
+    )(*(w for w, _, _ in parts), after)
 
 
 def cot_body(
-    own_ref, other_ref, down_hbm, gate_hbm,
-    away_ref, cot_ref, weight_out, rows, down_ref, gate_ref,
-    wide, grads, sems,
+    rows_in, low_ref, high_ref, *refs
 ):
-    count = own_ref.shape[0]
+    away_ref, cot_ref, weight_out, rows, wide, grads = refs[-6:]
+    total = rows_in.shape[0]
     width = rows.shape[1]
     hidden = cot_ref.shape[1]
-    feats = down_ref.shape[1]
+    feats = low_ref.shape[1]
     local = lax.axis_index("local")
     expert = lax.axis_index("chip") * 2 + lax.axis_index("core")
-    steps = hidden // COLS
-    copies = []
-    for n in range(2 * steps):
-        base = (1 - local) * hidden if n < steps else local * hidden
-        at = pl.ds(pl.multiple_of(base + (n % steps) * COLS, COLS), COLS)
-        copies.append((pltpu.make_async_copy(down_hbm.at[0, at, :], down_ref.at[at, :], sems.at[n]), at))
-    gate_copy = pltpu.make_async_copy(
-        gate_hbm.at[0, :, 0 : gate_ref.shape[1]], gate_ref, sems.at[2 * steps]
-    )
-    for copy, _ in copies:
-        copy.start()
-    gate_copy.start()
-    lane = lax.broadcasted_iota(jnp.int32, (count, LANES), 1)
+    lane = lax.broadcasted_iota(jnp.int32, (total, LANES), 1)
     meta = width // COLS
-    for half, ref in enumerate((own_ref, other_ref)):
-        at = pl.ds(half * count, count)
-        wide[...] = ref[...].astype(F32)
-        for i in range(meta):
-            rows[at, i * COLS : (i + 1) * COLS] = wide[:, i, 0:COLS].astype(BF16)
-        for i in range(feats // LANES):
-            grads[at, i * LANES : (i + 1) * LANES] = wide[:, i, COLS:SPAN].astype(BF16)
-        both = wide[:, meta, 0:LANES] + wide[:, meta, LANES:COLS]
-        both = jnp.sum(jnp.where(lane == expert, both, 0.0), axis=1, keepdims=True)
-        weight_out[at, :] = jnp.broadcast_to(both, (count, LANES))
+    wide[...] = rows_in[...].astype(F32)
+    side = pl.ds(pl.multiple_of(COLS + local * LANES, LANES), LANES)
+    for i in range(feats // LANES):
+        grads[:, i * LANES : (i + 1) * LANES] = wide[:, i, side].astype(BF16)
     grad = grads[...]
-    for n, (copy, at) in enumerate(copies):
-        copy.wait()
-        part = dot_nt(grad, down_ref[at, :])
-        cols = slice((n % steps) * COLS, (n % steps + 1) * COLS)
-        if n < steps:
-            away_ref[:, cols] = part.astype(BF16)
+
+    def products(own, away):
+        for n in range(hidden // COLS):
+            at = slice(n * COLS, (n + 1) * COLS)
+            away_ref[:, at] = dot_nt(grad, away[at, :]).astype(BF16)
+        for n in range(hidden // COLS):
+            at = slice(n * COLS, (n + 1) * COLS)
+            cot_ref[:, at] = dot_nt(grad, own[at, :])
+
+    @pl.when(local == 0)
+    def _():
+        products(low_ref, high_ref)
+
+    @pl.when(local == 1)
+    def _():
+        products(high_ref, low_ref)
+
+    for i in range(meta):
+        rows[:, i * COLS : (i + 1) * COLS] = wide[:, i, 0:COLS].astype(BF16)
+    both = wide[:, meta, 0:LANES] + wide[:, meta, LANES:COLS]
+    both = jnp.sum(jnp.where(lane == expert, both, 0.0), axis=1, keepdims=True)
+    weight_out[...] = jnp.broadcast_to(both, (total, LANES))
+
+
+def forward_body(rows_ref, gate_first, gate_second, up_first, up_second, gate_out, up_out, act_ref):
+    split = gate_first.shape[1]
+    hidden = act_ref.shape[1]
+    tokens = rows_ref[...]
+    for n in range(hidden // COLS):
+        cols = slice(n * COLS, (n + 1) * COLS)
+        if n * COLS < split:
+            gate, up = dot(tokens, gate_first[:, cols]), dot(tokens, up_first[:, cols])
         else:
-            cot_ref[:, cols] = part
-    gate_copy.wait()
-
-
-def forward_body(
-    rows_ref, first_ref, gate_hbm, up_hbm,
-    gate_out, up_out, act_ref, second_ref, up_ref,
-    sems,
-):
-    split = first_ref.shape[1]
-    hidden = up_ref.shape[1]
-    steps = hidden // COLS
-    ups, gates = [], []
-    for n in range(steps):
-        cols = slice(n * COLS, (n + 1) * COLS)
-        ups.append(pltpu.make_async_copy(up_hbm.at[0, :, cols], up_ref.at[:, cols], sems.at[n]))
-        if n * COLS >= split:
-            into = slice(n * COLS - split, (n + 1) * COLS - split)
-            gates.append(
-                pltpu.make_async_copy(
-                    gate_hbm.at[0, :, cols], second_ref.at[:, into], sems.at[steps + n]
-                )
-            )
-        else:
-            gates.append(None)
-    for n in range(steps):
-        ups[n].start()
-        if gates[n] is not None:
-            gates[n].start()
-    tokens = rows_ref[...]
-    for n in range(steps):
-        cols = slice(n * COLS, (n + 1) * COLS)
-        if gates[n] is not None:
-            gates[n].wait()
-            weight = second_ref[:, n * COLS - split : (n + 1) * COLS - split]
-        else:
-            weight = first_ref[:, cols]
-        gate = dot(tokens, weight)
-        ups[n].wait()
-        up = dot(tokens, up_ref[:, cols])
+            at = slice(n * COLS - split, (n + 1) * COLS - split)
+            gate, up = dot(tokens, gate_second[:, at]), dot(tokens, up_second[:, at])
         gate_out[:, cols] = gate
         up_out[:, cols] = up
         act_ref[:, cols] = (gate * jax.nn.sigmoid(gate) * up).astype(BF16)
 
 
+def place(ref, block):
+    count = ref.shape[0]
+    chip, local = lax.axis_index("chip"), lax.axis_index("local")
+    for r in range(count):
+        step = r % (count // 2)
+        chip_to = jnp.bitwise_xor(chip, arrival(step, count // 2))
+        local_to = jnp.bitwise_xor(local, r // (count // 2))
+        ref[chip_to * 2 + local_to] = block(r).astype(BF16)
+
+
+def crossed(x):
+    size = x.shape[0] // 4
+    return jnp.concatenate([x[i * size : (i + 1) * size] for i in (1, 0, 3, 2)], axis=0)
+
+
+def arrival(step, chips):
+    return sum(mask for i, mask in enumerate(chip_masks(chips)) if step >> i & 1)
+
+
+def chip_masks(chips):
+    masks, bit = [], 1
+    while bit < chips:
+        masks.append(bit)
+        bit *= 2
+    return masks[1:] + masks[:1]
+
+
 def input_body(
-    cot_ref, recv_ref, gate_in, up_in, act_ref, weight_in, first_ref, second_ref, up_ref,
+    cot_ref, recv_ref, gate_in, up_in, act_ref, weight_in,
+    gate_first, gate_second, up_first, up_second,
     mine_ref, other_ref,
     wide,
 ):
     total = cot_ref.shape[0]
     count = total // 2
-    width = up_ref.shape[0]
-    split = first_ref.shape[1]
+    width, split = gate_first.shape
     expert = lax.axis_index("chip") * 2 + lax.axis_index("core")
     gate, up = gate_in[...], up_in[...]
     sig = jax.nn.sigmoid(gate)
-    cot = cot_ref[...] + recv_ref[...].astype(F32)
+    cot = cot_ref[...] + crossed(recv_ref[...].astype(F32))
     prob = jnp.sum(cot * act_ref[...].astype(F32), axis=1, keepdims=True)
     hidden_grad = cot * weight_in[:, 0:1]
     gate_grad = (hidden_grad * up * sig * (1.0 + gate * (1.0 - sig))).astype(BF16)
@@ -196,9 +219,10 @@
     for n in range(steps):
         at = slice(n * COLS, (n + 1) * COLS)
         wide[:, n, :] = (
-            dot_nt(gate_grad[:, :split], first_ref[at, :])
-            + dot_nt(gate_grad[:, split:], second_ref[at, :])
-            + dot_nt(up_grad, up_ref[at, :])
+            dot_nt(gate_grad[:, :split], gate_first[at, :])
+            + dot_nt(gate_grad[:, split:], gate_second[at, :])
+            + dot_nt(up_grad[:, :split], up_first[at, :])
+            + dot_nt(up_grad[:, split:], up_second[at, :])
         )
     lane = lax.broadcasted_iota(jnp.int32, (total, LANES), 1)
     high, low = high_low(jnp.where(lane == expert, prob, 0.0))
@@ -206,29 +230,29 @@
     wide[:, steps, LANES:COLS] = low
     for n in range(steps + 1, ROWS):
         wide[:, n, :] = jnp.zeros((total, COLS), F32)
-    mine_ref[...] = wide[:count].astype(BF16)
-    other_ref[...] = wide[count:].astype(BF16)
-
-
-def routed_body(act_ref, recv_ref, weight_in, down_ref, after_ref, mine_ref, other_ref, wide):
+    place(mine_ref, lambda r: wide[r])
+    place(other_ref, lambda r: wide[count + r])
+
+
+def routed_body(act_ref, recv_ref, weight_in, low_ref, high_ref, after_ref, mine_ref, other_ref, wide):
     total, hidden = act_ref.shape
     count = total // 2
-    feats = down_ref.shape[1]
+    feats = low_ref.shape[1]
     local = lax.axis_index("local")
     weight = weight_in[:, 0:1]
-    act, recv = act_ref[...], recv_ref[...]
-    own = pl.ds(pl.multiple_of(local * hidden, COLS), hidden)
-    away = pl.ds(pl.multiple_of((1 - local) * hidden, COLS), hidden)
+    act, recv = act_ref[...], crossed(recv_ref[...].astype(F32)).astype(BF16)
+    low = jnp.where(local == 0, act, recv)
+    high = jnp.where(local == 0, recv, act)
     for n in range(feats // COLS):
         cols = slice(n * COLS, (n + 1) * COLS)
-        part = dot(act, down_ref[own, cols]) + dot(recv, down_ref[away, cols])
+        part = dot(low, low_ref[:, cols]) + dot(high, high_ref[:, cols])
         part = part.astype(BF16).astype(F32) * weight
         wide[:, 2 * n, :] = part[:, :LANES]
         wide[:, 2 * n + 1, :] = part[:, LANES:]
     for n in range(feats // LANES, ROWS):
         wide[:, n, :] = jnp.zeros((total, LANES), F32)
-    mine_ref[...] = wide[:count].astype(BF16)
-    other_ref[...] = wide[count:].astype(BF16)
+    place(mine_ref, lambda r: wide[r])
+    place(other_ref, lambda r: wide[count + r])
 
 
 def final_body(in_ref, ids_ref, comb_ref, grad_ref, prob_ref, wide):
@@ -264,8 +288,15 @@
     return lax.ppermute(x, axis, [(0, 1), (1, 0)])
 
 
+def trade(x, mask):
+    axes = ("chip", "core", "local")
+    size = math.prod(lax.axis_size(axis) for axis in axes)
+    return lax.ppermute(x, axes, [(i, i ^ mask) for i in range(size)])
+
+
 def fast_device(tokens, expert_ids, route_probs, gate_weight, up_weight, down_weight, out_grad):
-    groups = lax.axis_size("chip") * 2
+    chips = lax.axis_size("chip")
+    groups = chips * 2
     total = 2 * groups
     width = tokens.shape[2]
     hidden = gate_weight.shape[2]
@@ -275,10 +306,10 @@
     gate_hbm, up_hbm, down_hbm = in_hbm(gate_weight, up_weight, down_weight)
     (packed,) = call(
         pack_body,
-        [shaped((groups, ROWS, SPAN), BF16)],
+        [shaped((1, ROWS, TAKE), BF16)],
         [ANY] * 4,
         [
-            pltpu.VMEM((ROWS, SPAN), F32),
+            pltpu.VMEM((ROWS, TAKE), F32),
             pltpu.SMEM(expert_ids.shape, expert_ids.dtype),
             pltpu.SMEM(route_probs.shape, route_probs.dtype),
             pltpu.VMEM(tokens.shape, BF16),
@@ -286,60 +317,74 @@
             pltpu.SemaphoreType.DMA((4,)),
         ],
     )(*in_hbm(expert_ids, route_probs, tokens, out_grad))
-    own = lax.all_to_all(packed, ("chip", "local"), split_axis=0, concat_axis=0, tiled=True)
-    other = swap(own, "core")
-    away, cot, weight, rows, down_w, gate_first = call(
+    first, second = (0, split), (split, hidden)
+    pieces = [
+        (down_hbm, (0, hidden), (0, feats)),
+        (down_hbm, (hidden, 2 * hidden), (0, feats)),
+        (gate_hbm, (0, width), first),
+        (gate_hbm, (0, width), second),
+        (up_hbm, (0, width), first),
+        (up_hbm, (0, width), second),
+    ]
+    masks = [4 * mask for mask in chip_masks(chips)] + [1, 2]
+    loaded, gathered, after = [], packed, []
+    for step, mask in enumerate(masks):
+        left = len(masks) - step
+        take = -(-len(pieces) // left) if step >= len(masks) - 2 else min(1, len(pieces))
+        moved = trade(gathered, mask)
+        *parts, token = load(pieces[:take], gathered)
+        pieces = pieces[take:]
+        loaded += parts
+        after.append(token)
+        gathered = jnp.concatenate([gathered, moved], axis=0)
+        gathered, after[-1] = lax.optimization_barrier((gathered, after[-1]))
+    down_low, down_high, gate_first, gate_second, up_first, up_second = loaded
+    away, cot, weight, rows = call(
         cot_body,
         [
             shaped((total, hidden), BF16),
             shaped((total, hidden), F32),
             shaped((total, LANES), F32),
             shaped((total, width), BF16),
-            pltpu.VMEM((2 * hidden, feats), BF16),
-            pltpu.VMEM((width, split), BF16),
         ],
-        [VMEM, VMEM, ANY, ANY],
+        [VMEM] * 3 + [ANY] * len(after),
         [
-            pltpu.VMEM((groups, ROWS, SPAN), F32),
+            pltpu.VMEM((total, ROWS, TAKE), F32),
             pltpu.VMEM((total, feats), BF16),
-            pltpu.SemaphoreType.DMA((2 * hidden // COLS + 1,)),
         ],
         products=total * one,
-        moved=3 * one // 2,
-    )(own, other, down_hbm, gate_hbm)
+        moved=one,
+    )(gathered, down_low, down_high, *after)
     cot_recv = swap(away, "local")
-    gate, up, act, gate_second, up_w = call(
+    gate, up, act = call(
         forward_body,
         [
             shaped((total, hidden), F32),
             shaped((total, hidden), F32),
             shaped((total, hidden), BF16),
-            pltpu.VMEM((width, hidden - split), BF16),
-            pltpu.VMEM((width, hidden), BF16),
         ],
-        [VMEM, VMEM, ANY, ANY],
-        [pltpu.SemaphoreType.DMA((2 * hidden // COLS,))],
+        [VMEM] * 5,
         products=total * 2 * one,
-        moved=3 * one // 2,
-    )(rows, gate_first, gate_hbm, up_hbm)
+        moved=2 * one,
+    )(rows, gate_first, gate_second, up_first, up_second)
     act_recv = swap(act, "local")
     in_mine, in_away = call(
         input_body,
         [shaped((groups, ROWS, COLS), BF16)] * 2,
-        [VMEM] * 9,
+        [VMEM] * 10,
         [pltpu.VMEM((total, ROWS, COLS), F32)],
         products=total * 2 * one,
         moved=2 * one,
-    )(cot, cot_recv, gate, up, act, weight, gate_first, gate_second, up_w)
+    )(cot, cot_recv, gate, up, act, weight, gate_first, gate_second, up_first, up_second)
     in_recv = swap(in_away, "core")
     routed_mine, routed_away = call(
         routed_body,
         [shaped((groups, ROWS, LANES), BF16)] * 2,
-        [VMEM] * 4 + [ANY],
+        [VMEM] * 5 + [ANY],
         [pltpu.VMEM((total, ROWS, LANES), F32)],
         products=total * one,
         moved=one,
-    )(act, act_recv, weight, down_w, in_mine)
+    )(act, act_recv, weight, down_low, down_high, in_mine)
     routed_recv = swap(routed_away, "core")
     summed = jnp.concatenate(
         [

time: 54.9 us -> 56.2 us (1.024)
  blocking collectives: 29.1 us -> 16.1 us
  starting transfers between devices: 2.73 us -> 11.7 us
  Pallas kernels: 19.6 us -> 25 us
    all_to_all x1 -> x0, blocking collectives: 16.8 us -> none  [fast_device(): lax.all_to_all(packed, ('chip', 'local'), split_axis=0, concat_axis=0, ti...]
    pallas_call x3 -> x8, Pallas kernels: 6.71 us -> 18 us  [the longest x5 11.4 us: load(): call(functools.partial(load_body, parts=bounds), [pltpu.VMEM(shape, BF16)...]
    ppermute x0 -> x5, starting transfers between devices: none -> 9.02 us  [trade(): return lax.ppermute(x, axes, [(i, i ^ mask) for i in range(size)])]
    all_to_all x1, blocking collectives: 12.3 us -> 16.1 us  [fast_device(): lax.all_to_all(summed, ('chip', 'local'), split_axis=0, concat_axis=0, ti...]
    pallas_call x1, Pallas kernels: 5.66 us -> 2.63 us  [fast_device(): call(forward_body, [shaped((total, hidden), F32), shaped((total, hidden),...]
    pallas_call x1, Pallas kernels: 6.03 us -> 3.07 us  [fast_device(): call(cot_body, [shaped((total, hidden), BF16), shaped((total, hidden), F3...]
    ppermute x5 -> x4, waiting for transfers between devices: 2.4 us -> 0.97 us  [swap(): return lax.ppermute(x, axis, [(0, 1), (1, 0)])]
    ppermute x0 -> x5, waiting for transfers between devices: none -> 1.09 us  [trade(): return lax.ppermute(x, axes, [(i, i ^ mask) for i in range(size)])]
  transfers between devices with their start and end apart: 5 -> 9, of which waited for: 3 -> 5; matrix products, arithmetic and copies ran while one was open for 0% -> 0% of each run, Pallas kernels for 19% -> 33%
where the time goes in v3:
time: 56.2 us; the launch traced here: 55.8 us
  Pallas kernels  25 us (44%)
  blocking collectives  16.1 us (29%)
  starting transfers between devices  11.7 us (21%)
  waiting for transfers between devices  2.06 us (4%)
  between operations  0.8 us (1%)
    all_to_all x1, blocking collectives, fast_device(): lax.all_to_all(summed, ('chip', 'local'), split_axis=0, concat_axis=0, ti...  16.1 us
    pallas_call x5, Pallas kernels, load(): call(functools.partial(load_body, parts=bounds), [pltpu.VMEM(shape, BF16)...  11.4 us
    ppermute x5, starting transfers between devices, trade(): return lax.ppermute(x, axes, [(i, i ^ mask) for i in range(size)])  9.02 us
    pallas_call x1, Pallas kernels, fast_device(): call(input_body, [shaped((groups, ROWS, COLS), BF16)] * 2, [VMEM] * 10, [...  4.44 us
    pallas_call x1, Pallas kernels, fast_device(): call(cot_body, [shaped((total, hidden), BF16), shaped((total, hidden), F3...  3.07 us
    ppermute x4, starting transfers between devices, swap(): return lax.ppermute(x, axis, [(0, 1), (1, 0)])  2.72 us
    pallas_call x1, Pallas kernels, fast_device(): call(forward_body, [shaped((total, hidden), F32), shaped((total, hidden),...  2.63 us
    pallas_call x1, Pallas kernels, fast_device(): call(routed_body, [shaped((groups, ROWS, LANES), BF16)] * 2, [VMEM] * 5 +...  1.45 us
  transfers between devices with their start and end apart: 9, of which 5 were waited for; matrix products, arithmetic and copies ran while one was open for 0% of the time, Pallas kernels for 33%

profile of v3, /device:TPU:0, one launch (start us, length us, event | category | flops | bytes accessed | tf_op | source)
XLA Modules:
  0.0 55.8 jit_solution(10679028814103300565)
XLA Ops:
  0.6 0.8 %shard_map.94.refs_1_ = bf16[1,16,512]{2,1,0:T(8,128)(2,1)S(1)} custom-call(s32[1,1,8]{2,1,0:T(1,128)} %ids_ref.1, f32[1,1,8]{2,1,0:T(1,128)} %probs_hbm.1, bf16[1,1,3584]{2,1,0:T(2,128)(2,1)} %tok_hbm.1, bf16[1,1,3584]{2,1,0:T(2,128)(2,1)} %grad_hbm.1), custom_call_target="tpu_custom_call" | custom-call | tf_op jit(solution)/shard_map/pallas_call | solution.py:307
  1.4 3.1 %collective-permute-start = (bf16[1,16,512]{2,1,0:T(8,128)(2,1)S(1)}, bf16[1,16,512]{2,1,0:T(8,128)(2,1)S(1)}, u32[]{:S(2)}, u32[]{:S(2)}) collective-permute-start(bf16[1,16,512]{2,1,0:T(8,128)(2,1)S(1)} %shard_map.94.refs_1_), channel_id=1, source_target_pairs={{0,8},{1,9},{2,10},{3,11},{4,12},{5,13},{6,14},{7,15},{8,0},{9,1},... | collective-permute-start | bytes 49160 | tf_op jit(solution)/shard_map/ppermute | solution.py:294
  4.5 2.0 %shard_map.95 = (bf16[1024,1792]{1,0:T(8,128)(2,1)S(1)}, f32[8,128]{1,0:T(8,128)S(1)}) custom-call(bf16[1,2048,1792]{2,1,0:T(8,128)(2,1)} %refs_0_.6, bf16[1,16,512]{2,1,0:T(8,128)(2,1)S(1)} %shard_map.94.refs_1_), custom_call_target="tpu_custom_call" | custom-call | bytes 7340032 | tf_op jit(solution)/shard_map/pallas_call | solution.py:108
  6.6 2.7 %collective-permute-start.1 = (bf16[2,16,512]{2,1,0:T(8,128)(2,1)S(1)}, bf16[2,16,512]{2,1,0:T(8,128)(2,1)S(1)}, u32[]{:S(2)}, u32[]{:S(2)}) collective-permute-start(bf16[2,16,512]{2,1,0:T(8,128)(2,1)S(1)} %pad_maximum_fusion.5.refs_1_), channel_id=1, source_target_pairs={{0,16},{1,17},{2,18},{3,19},{4,20},{5,21},{6,22},{7,23},{8,24},{9,... | collective-permute-start | bytes 98312 | tf_op jit(solution)/shard_map/ppermute | solution.py:294
  9.3 2.0 %shard_map.96 = (bf16[1024,1792]{1,0:T(8,128)(2,1)S(1)}, f32[8,128]{1,0:T(8,128)S(1)}) custom-call(bf16[1,2048,1792]{2,1,0:T(8,128)(2,1)} %refs_0_.6, bf16[2,16,512]{2,1,0:T(8,128)(2,1)S(1)} %pad_maximum_fusion.5.refs_1_), custom_call_target="tpu_custom_call" | custom-call | bytes 7340032 | tf_op jit(solution)/shard_map/pallas_call | solution.py:108
  11.3 0.1 collective-permute-done.1
  11.5 1.6 %collective-permute-start.2 = (bf16[4,16,512]{2,1,0:T(8,128)(2,1)S(1)}, bf16[4,16,512]{2,1,0:T(8,128)(2,1)S(1)}, u32[]{:S(2)}, u32[]{:S(2)}) collective-permute-start(bf16[4,16,512]{2,1,0:T(8,128)(2,1)S(1)} %pad_maximum_fusion.4.refs_1_), channel_id=1, source_target_pairs={{0,4},{1,5},{2,6},{3,7},{4,0},{5,1},{6,2},{7,3},{8,12},{9,13},{10,... | collective-permute-start | bytes 196616 | tf_op jit(solution)/shard_map/ppermute | solution.py:294
  13.1 2.0 %shard_map.97 = (bf16[3584,512]{1,0:T(8,128)(2,1)S(1)}, f32[8,128]{1,0:T(8,128)S(1)}) custom-call(bf16[1,3584,1024]{2,1,0:T(8,128)(2,1)} %refs_0_.8, bf16[4,16,512]{2,1,0:T(8,128)(2,1)S(1)} %pad_maximum_fusion.4.refs_1_), custom_call_target="tpu_custom_call" | custom-call | bytes 7340032 | tf_op jit(solution)/shard_map/pallas_call | solution.py:108
  15.1 0.7 %collective-permute-done.2 = bf16[4,16,512]{2,1,0:T(8,128)(2,1)S(1)} collective-permute-done((bf16[4,16,512]{2,1,0:T(8,128)(2,1)S(1)}, bf16[4,16,512]{2,1,0:T(8,128)(2,1)S(1)}, u32[]{:S(2)}, u32[]{:S(2)}) %collective-permute-start.2) | collective-permute-done | bytes 65568 | tf_op jit(solution)/shard_map/ppermute | solution.py:294
  15.8 1.6 %collective-permute-start.3 = (bf16[8,16,512]{2,1,0:T(8,128)(2,1)S(1)}, bf16[8,16,512]{2,1,0:T(8,128)(2,1)S(1)}, u32[]{:S(2)}, u32[]{:S(2)}) collective-permute-start(bf16[8,16,512]{2,1,0:T(8,128)(2,1)S(1)} %pad_maximum_fusion.3.refs_2_), channel_id=1, source_target_pairs={{0,1},{1,0},{2,3},{3,2},{4,5},{5,4},{6,7},{7,6},{8,9},{9,8},{10,11... | collective-permute-start | bytes 393224 | tf_op jit(solution)/shard_map/ppermute | solution.py:294
  17.5 3.2 %shard_map.98 = (bf16[3584,512]{1,0:T(8,128)(2,1)S(1)}, bf16[3584,512]{1,0:T(8,128)(2,1)S(1)}, f32[8,128]{1,0:T(8,128)S(1)}) custom-call(bf16[1,3584,1024]{2,1,0:T(8,128)(2,1)} %refs_0_.8, bf16[1,3584,1024]{2,1,0:T(8,128)(2,1)} %refs_0_.9, bf16[8,16,512]{2,1,0:T(8,128)(2,1)S(1)} %pad_maximum_fusion.3.refs_2_), custom_call_target="tpu_custom_call" | custom-call | bytes 14680064 | tf_op jit(solution)/shard_map/pallas_call | solution.py:108
  20.6 0.2 collective-permute-done.3
  21.0 2.1 %shard_map.99 = (bf16[3584,512]{1,0:T(8,128)(2,1)S(1)}, f32[8,128]{1,0:T(8,128)S(1)}) custom-call(bf16[1,3584,1024]{2,1,0:T(8,128)(2,1)} %refs_0_.9, bf16[16,16,512]{2,1,0:T(8,128)(2,1)S(1)} %pad_maximum_fusion.1.refs_1_), custom_call_target="tpu_custom_call" | custom-call | bytes 7340032 | tf_op jit(solution)/shard_map/pallas_call | solution.py:108
  23.1 3.1 %shard_map.100 = (bf16[32,1024]{1,0:T(8,128)(2,1)S(1)}, f32[32,1024]{1,0:T(8,128)S(1)}, f32[32,128]{1,0:T(8,128)S(1)}, bf16[32,3584]{1,0:T(8,128)(2,1)S(1)}) custom-call(bf16[32,16,512]{2,1,0:T(8,128)(2,1)S(1)} %pad_maximum_fusion.rows_in, bf16[1024,1792]{1,0:T(8,128)(2,1)S(1)} %get-tuple-element.45.low_ref, ...), custom_call_target="tpu_custom_call" | custom-call | flops 234881024 | bytes 7340032 | tf_op jit(solution)/shard_map/pallas_call | solution.py:342
  26.2 1.6 %collective-permute-start.5 = (bf16[32,1024]{1,0:T(8,128)(2,1)S(1)}, bf16[32,1024]{1,0:T(8,128)(2,1)S(1)}, u32[]{:S(2)}, u32[]{:S(2)}) collective-permute-start(bf16[32,1024]{1,0:T(8,128)(2,1)S(1)} %get-tuple-element.53), channel_id=1, source_target_pairs={{0,1},{1,0},{2,3},{3,2},{4,5},{5,4},{6,7},{7,6},{8,9},{9,8},{10,11... | collective-permute-start | bytes 196616 | tf_op jit(solution)/shard_map/ppermute | solution.py:288
  27.8 2.6 %shard_map.101 = (f32[32,1024]{1,0:T(8,128)S(1)}, f32[32,1024]{1,0:T(8,128)S(1)}, bf16[32,1024]{1,0:T(8,128)(2,1)S(1)}) custom-call(bf16[32,3584]{1,0:T(8,128)(2,1)S(1)} %get-tuple-element.54.rows_ref, bf16[3584,512]{1,0:T(8,128)(2,1)S(1)} %get-tuple-element.55.gate_first, bf16[3584,512]{1,0:T(8,128)(2,1)S(1)} %get-tuple-element.56.gate_second, ...), custom_call_target="tpu_custom_call" | custom-call | flops 469762048 | bytes 14680064 | tf_op jit(solution)/shard_map/pallas_call | solution.py:359
  30.4 0.6 %collective-permute-start.7 = (bf16[32,1024]{1,0:T(8,128)(2,1)S(1)}, bf16[32,1024]{1,0:T(8,128)(2,1)S(1)}, u32[]{:S(2)}, u32[]{:S(2)}) collective-permute-start(bf16[32,1024]{1,0:T(8,128)(2,1)S(1)} %get-tuple-element.61.act_ref), channel_id=1, source_target_pairs={{0,1},{1,0},{2,3},{3,2},{4,5},{5,4},{6,7},{7,6},{8,9},{9,8},{10,11... | collective-permute-start | bytes 196616 | tf_op jit(solution)/shard_map/ppermute | solution.py:288
  31.0 4.4 %shard_map.102 = (bf16[16,16,256]{2,1,0:T(8,128)(2,1)S(1)}, bf16[16,16,256]{2,1,0:T(8,128)(2,1)S(1)}) custom-call(f32[32,1024]{1,0:T(8,128)S(1)} %get-tuple-element.52.cot_ref, bf16[32,1024]{1,0:T(8,128)(2,1)S(1)} %collective-permute-done.5.recv_ref, f32[32,1024]{1,0:T(8,128)S(1)} %get-tuple-element.59.gate_in, f32[32,1024]{1,0:T(8,128)S(1)} %get-tuple-element.60.up_in, ...), custom_call_target="tpu_custom_call" | custom-call | flops 469762048 | bytes 14680064 | tf_op jit(solution)/shard_map/pallas_call | solution.py:371
  35.5 1.4 %shard_map.103 = (bf16[16,16,128]{2,1,0:T(8,128)(2,1)S(1)}, bf16[16,16,128]{2,1,0:T(8,128)(2,1)S(1)}) custom-call(bf16[32,1024]{1,0:T(8,128)(2,1)S(1)} %get-tuple-element.61.act_ref, bf16[32,1024]{1,0:T(8,128)(2,1)S(1)} %collective-permute-done.7.recv_ref, f32[32,128]{1,0:T(8,128)S(1)} %get-tuple-element.62.weight_in, ...), custom_call_target="tpu_custom_call" | custom-call | flops 234881024 | bytes 7340032 | tf_op jit(solution)/shard_map/pallas_call | solution.py:380
  37.0 0.5 collective-permute-start.6
  37.5 0.7 %collective-permute-done.8 = bf16[16,16,128]{2,1,0:T(8,128)(2,1)S(1)} collective-permute-done((bf16[16,16,128]{2,1,0:T(8,128)(2,1)S(1)}, bf16[16,16,128]{2,1,0:T(8,128)(2,1)S(1)}, u32[]{:S(2)}, u32[]{:S(2)}) %collective-permute-start.8) | collective-permute-done | bytes 65568 | tf_op jit(solution)/shard_map/ppermute | solution.py:288
  38.3 0.2 collective-permute-done.6
  38.6 16.1 %all_to_all.5.in_ref = bf16[16,16,384]{2,1,0:T(8,128)(2,1)S(1)} all-to-all(bf16[16,16,384]{2,1,0:T(8,128)(2,1)S(1)} %pad_maximum_fusion.2), channel_id=1, replica_groups=mesh['chip'=8,'core'=2,'local'=2] {'chip','local'}, dimensions={0} | all-to-all | bytes 393216 | tf_op jit(solution)/shard_map/all_to_all | solution.py:396
  54.6 1.2 %shard_map.104 = (bf16[1,1,3584]{2,1,0:T(2,128)(2,1)}, bf16[1,1,3584]{2,1,0:T(2,128)(2,1)}, f32[1,1,8]{2,1,0:T(1,128)}) custom-call(bf16[16,16,384]{2,1,0:T(8,128)(2,1)S(1)} %all_to_all.5.in_ref, s32[1,1,8]{2,1,0:T(1,128)S(1)} %copy-done), custom_call_target="tpu_custom_call" | custom-call | tf_op jit(solution)/shard_map/pallas_call | solution.py:397
  (16 shorter events, 0.3 us)
Async XLA Ops:
  1.4 5.1 %collective-permute-start = (bf16[1,16,512]{2,1,0:T(8,128)(2,1)S(1)}, bf16[1,16,512]{2,1,0:T(8,128)(2,1)S(1)}, u32[]{:S(2)}, u32[]{:S(2)}) collective-permute-start(bf16[1,16,512]{2,1,0:T(8,128)(2,1)S(1)} %shard_map.94.refs_1_), channel_id=1, source_target_pairs={{0,8},{1,9},{2,10},{3,11},{4,12},{5,13},{6,14},{7,15},{8,0},{9,1},... | collective-permute-start | bytes 49160 | tf_op jit(solution)/shard_map/ppermute | solution.py:294
  6.6 4.9 %collective-permute-start.1 = (bf16[2,16,512]{2,1,0:T(8,128)(2,1)S(1)}, bf16[2,16,512]{2,1,0:T(8,128)(2,1)S(1)}, u32[]{:S(2)}, u32[]{:S(2)}) collective-permute-start(bf16[2,16,512]{2,1,0:T(8,128)(2,1)S(1)} %pad_maximum_fusion.5.refs_1_), channel_id=1, source_target_pairs={{0,16},{1,17},{2,18},{3,19},{4,20},{5,21},{6,22},{7,23},{8,24},{9,... | collective-permute-start | bytes 98312 | tf_op jit(solution)/shard_map/ppermute | solution.py:294
  11.5 4.3 %collective-permute-start.2 = (bf16[4,16,512]{2,1,0:T(8,128)(2,1)S(1)}, bf16[4,16,512]{2,1,0:T(8,128)(2,1)S(1)}, u32[]{:S(2)}, u32[]{:S(2)}) collective-permute-start(bf16[4,16,512]{2,1,0:T(8,128)(2,1)S(1)} %pad_maximum_fusion.4.refs_1_), channel_id=1, source_target_pairs={{0,4},{1,5},{2,6},{3,7},{4,0},{5,1},{6,2},{7,3},{8,12},{9,13},{10,... | collective-permute-start | bytes 196616 | tf_op jit(solution)/shard_map/ppermute | solution.py:294
  15.8 5.0 %collective-permute-start.3 = (bf16[8,16,512]{2,1,0:T(8,128)(2,1)S(1)}, bf16[8,16,512]{2,1,0:T(8,128)(2,1)S(1)}, u32[]{:S(2)}, u32[]{:S(2)}) collective-permute-start(bf16[8,16,512]{2,1,0:T(8,128)(2,1)S(1)} %pad_maximum_fusion.3.refs_2_), channel_id=1, source_target_pairs={{0,1},{1,0},{2,3},{3,2},{4,5},{5,4},{6,7},{7,6},{8,9},{9,8},{10,11... | collective-permute-start | bytes 393224 | tf_op jit(solution)/shard_map/ppermute | solution.py:294
  20.9 2.1 %collective-permute-start.4 = (bf16[16,16,512]{2,1,0:T(8,128)(2,1)S(1)}, bf16[16,16,512]{2,1,0:T(8,128)(2,1)S(1)}, u32[]{:S(2)}, u32[]{:S(2)}) collective-permute-start(bf16[16,16,512]{2,1,0:T(8,128)(2,1)S(1)} %pad_maximum_fusion.1.refs_1_), channel_id=1, source_target_pairs={{0,2},{1,3},{2,0},{3,1},{4,6},{5,7},{6,4},{7,5},{8,10},{9,11},{10,... | collective-permute-start | bytes 786440 | tf_op jit(solution)/shard_map/ppermute | solution.py:294
  26.2 4.8 %collective-permute-start.5 = (bf16[32,1024]{1,0:T(8,128)(2,1)S(1)}, bf16[32,1024]{1,0:T(8,128)(2,1)S(1)}, u32[]{:S(2)}, u32[]{:S(2)}) collective-permute-start(bf16[32,1024]{1,0:T(8,128)(2,1)S(1)} %get-tuple-element.53), channel_id=1, source_target_pairs={{0,1},{1,0},{2,3},{3,2},{4,5},{5,4},{6,7},{7,6},{8,9},{9,8},{10,11... | collective-permute-start | bytes 196616 | tf_op jit(solution)/shard_map/ppermute | solution.py:288
  30.4 5.0 %collective-permute-start.7 = (bf16[32,1024]{1,0:T(8,128)(2,1)S(1)}, bf16[32,1024]{1,0:T(8,128)(2,1)S(1)}, u32[]{:S(2)}, u32[]{:S(2)}) collective-permute-start(bf16[32,1024]{1,0:T(8,128)(2,1)S(1)} %get-tuple-element.61.act_ref), channel_id=1, source_target_pairs={{0,1},{1,0},{2,3},{3,2},{4,5},{5,4},{6,7},{7,6},{8,9},{9,8},{10,11... | collective-permute-start | bytes 196616 | tf_op jit(solution)/shard_map/ppermute | solution.py:288
  35.5 19.2 %copy-start = (s32[1,1,8]{2,1,0:T(1,128)S(1)}, s32[1,1,8]{2,1,0:T(1,128)}, u32[]{:S(2)}) copy-start(s32[1,1,8]{2,1,0:T(1,128)} %ids_ref.1) | copy-start | bytes 100
  36.9 1.3 %collective-permute-start.8 = (bf16[16,16,128]{2,1,0:T(8,128)(2,1)S(1)}, bf16[16,16,128]{2,1,0:T(8,128)(2,1)S(1)}, u32[]{:S(2)}, u32[]{:S(2)}) collective-permute-start(bf16[16,16,128]{2,1,0:T(8,128)(2,1)S(1)} %get-tuple-element.66), channel_id=1, source_target_pairs={{0,2},{2,0},{1,3},{3,1},{4,6},{6,4},{5,7},{7,5},{8,10},{10,8},{9,1... | collective-permute-start | bytes 196616 | tf_op jit(solution)/shard_map/ppermute | solution.py:288
  37.0 1.5 %collective-permute-start.6 = (bf16[16,16,256]{2,1,0:T(8,128)(2,1)S(1)}, bf16[16,16,256]{2,1,0:T(8,128)(2,1)S(1)}, u32[]{:S(2)}, u32[]{:S(2)}) collective-permute-start(bf16[16,16,256]{2,1,0:T(8,128)(2,1)S(1)} %get-tuple-element.64), channel_id=1, source_target_pairs={{0,2},{2,0},{1,3},{3,1},{4,6},{6,4},{5,7},{7,5},{8,10},{10,8},{9,1... | collective-permute-start | bytes 393224 | tf_op jit(solution)/shard_map/ppermute | solution.py:288

commit v4 on v2

--- a/solution.py
+++ b/solution.py
@@ -12,6 +12,7 @@
 F32 = jnp.float32
 LANES = 128
 COLS = 256
+DEPTH = 512
 ROWS = 16
 SPAN = COLS + LANES
 
@@ -49,6 +50,10 @@
 
 def dot_nt(a, b):
     return lax.dot_general(a, b, NT, preferred_element_type=F32)
+
+
+def from_rows(weight, turned):
+    return dot(weight, turned).T
 
 
 def high_low(x):
@@ -87,8 +92,30 @@
             out_ref[i] = block
 
 
+def side_rows(local, hidden, n):
+    return pl.ds(pl.multiple_of(local * hidden + n * COLS, COLS), COLS)
+
+
+def load_body(down_hbm, after_ref, away_ref, token_ref, sems):
+    hidden = away_ref.shape[0]
+    away = 1 - lax.axis_index("local")
+    copies = [
+        pltpu.make_async_copy(
+            down_hbm.at[0, side_rows(away, hidden, n), :],
+            away_ref.at[n * COLS : (n + 1) * COLS, :],
+            sems.at[n],
+        )
+        for n in range(hidden // COLS)
+    ]
+    for copy in copies:
+        copy.start()
+    token_ref[...] = jnp.zeros_like(token_ref)
+    for copy in copies:
+        copy.wait()
+
+
 def cot_body(
-    own_ref, other_ref, down_hbm, gate_hbm,
+    own_ref, other_ref, loaded_ref, after_ref, down_hbm, gate_hbm,
     away_ref, cot_ref, weight_out, rows, down_ref, gate_ref,
     wide, grads, sems,
 ):
@@ -100,90 +127,73 @@
     expert = lax.axis_index("chip") * 2 + lax.axis_index("core")
     steps = hidden // COLS
     copies = []
-    for n in range(2 * steps):
-        base = (1 - local) * hidden if n < steps else local * hidden
-        at = pl.ds(pl.multiple_of(base + (n % steps) * COLS, COLS), COLS)
-        copies.append((pltpu.make_async_copy(down_hbm.at[0, at, :], down_ref.at[at, :], sems.at[n]), at))
-    gate_copy = pltpu.make_async_copy(
-        gate_hbm.at[0, :, 0 : gate_ref.shape[1]], gate_ref, sems.at[2 * steps]
-    )
-    for copy, _ in copies:
+    for n in range(steps):
+        into = down_ref.at[n * COLS : (n + 1) * COLS, :]
+        copies.append(
+            pltpu.make_async_copy(down_hbm.at[0, side_rows(local, hidden, n), :], into, sems.at[n])
+        )
+    for n in range(width // DEPTH):
+        at = slice(n * DEPTH, (n + 1) * DEPTH)
+        copies.append(
+            pltpu.make_async_copy(gate_hbm.at[0, at, :], gate_ref.at[at, :], sems.at[steps + n])
+        )
+    for copy in copies:
         copy.start()
-    gate_copy.start()
+
     lane = lax.broadcasted_iota(jnp.int32, (count, LANES), 1)
     meta = width // COLS
     for half, ref in enumerate((own_ref, other_ref)):
         at = pl.ds(half * count, count)
         wide[...] = ref[...].astype(F32)
+        for i in range(feats // LANES):
+            grads[at, i * LANES : (i + 1) * LANES] = wide[:, i, COLS:SPAN].astype(BF16)
         for i in range(meta):
             rows[at, i * COLS : (i + 1) * COLS] = wide[:, i, 0:COLS].astype(BF16)
-        for i in range(feats // LANES):
-            grads[at, i * LANES : (i + 1) * LANES] = wide[:, i, COLS:SPAN].astype(BF16)
         both = wide[:, meta, 0:LANES] + wide[:, meta, LANES:COLS]
         both = jnp.sum(jnp.where(lane == expert, both, 0.0), axis=1, keepdims=True)
         weight_out[at, :] = jnp.broadcast_to(both, (count, LANES))
-    grad = grads[...]
-    for n, (copy, at) in enumerate(copies):
+    grad = grads[...].T
+    for n in range(steps):
+        at = slice(n * COLS, (n + 1) * COLS)
+        away_ref[:, at] = from_rows(loaded_ref[at, :], grad).astype(BF16)
+    for n in range(steps):
+        at = slice(n * COLS, (n + 1) * COLS)
+        copies[n].wait()
+        cot_ref[:, at] = from_rows(down_ref[at, :], grad)
+    for copy in copies[steps:]:
         copy.wait()
-        part = dot_nt(grad, down_ref[at, :])
-        cols = slice((n % steps) * COLS, (n % steps + 1) * COLS)
-        if n < steps:
-            away_ref[:, cols] = part.astype(BF16)
-        else:
-            cot_ref[:, cols] = part
-    gate_copy.wait()
-
-
-def forward_body(
-    rows_ref, first_ref, gate_hbm, up_hbm,
-    gate_out, up_out, act_ref, second_ref, up_ref,
-    sems,
-):
-    split = first_ref.shape[1]
-    hidden = up_ref.shape[1]
-    steps = hidden // COLS
-    ups, gates = [], []
-    for n in range(steps):
-        cols = slice(n * COLS, (n + 1) * COLS)
-        ups.append(pltpu.make_async_copy(up_hbm.at[0, :, cols], up_ref.at[:, cols], sems.at[n]))
-        if n * COLS >= split:
-            into = slice(n * COLS - split, (n + 1) * COLS - split)
-            gates.append(
-                pltpu.make_async_copy(
-                    gate_hbm.at[0, :, cols], second_ref.at[:, into], sems.at[steps + n]
-                )
-            )
-        else:
-            gates.append(None)
-    for n in range(steps):
-        ups[n].start()
-        if gates[n] is not None:
-            gates[n].start()
-    tokens = rows_ref[...]
-    for n in range(steps):
-        cols = slice(n * COLS, (n + 1) * COLS)
-        if gates[n] is not None:
-            gates[n].wait()
-            weight = second_ref[:, n * COLS - split : (n + 1) * COLS - split]
-        else:
-            weight = first_ref[:, cols]
-        gate = dot(tokens, weight)
-        ups[n].wait()
-        up = dot(tokens, up_ref[:, cols])
-        gate_out[:, cols] = gate
-        up_out[:, cols] = up
-        act_ref[:, cols] = (gate * jax.nn.sigmoid(gate) * up).astype(BF16)
+
+
+def forward_body(rows_ref, gate_ref, up_hbm, gate_out, up_out, act_ref, up_ref, sems):
+    width, hidden = gate_ref.shape
+    pieces = [slice(n * DEPTH, (n + 1) * DEPTH) for n in range(width // DEPTH)]
+    columns = [slice(n * COLS, (n + 1) * COLS) for n in range(hidden // COLS)]
+    copies = [
+        pltpu.make_async_copy(up_hbm.at[0, at, :], up_ref.at[at, :], sems.at[n])
+        for n, at in enumerate(pieces)
+    ]
+    for copy in copies:
+        copy.start()
+    for cols in columns:
+        gate_out[:, cols] = dot(rows_ref[...], gate_ref[:, cols])
+    for n, at in enumerate(pieces):
+        copies[n].wait()
+        for cols in columns:
+            part = dot(rows_ref[:, at], up_ref[at, cols])
+            up_out[:, cols] = part if n == 0 else up_out[:, cols] + part
+    for cols in columns:
+        gate = gate_out[:, cols]
+        act_ref[:, cols] = (gate * jax.nn.sigmoid(gate) * up_out[:, cols]).astype(BF16)
 
 
 def input_body(
-    cot_ref, recv_ref, gate_in, up_in, act_ref, weight_in, first_ref, second_ref, up_ref,
+    cot_ref, recv_ref, gate_in, up_in, act_ref, weight_in, gate_ref, up_ref,
     mine_ref, other_ref,
     wide,
 ):
     total = cot_ref.shape[0]
     count = total // 2
     width = up_ref.shape[0]
-    split = first_ref.shape[1]
     expert = lax.axis_index("chip") * 2 + lax.axis_index("core")
     gate, up = gate_in[...], up_in[...]
     sig = jax.nn.sigmoid(gate)
@@ -192,14 +202,11 @@
     hidden_grad = cot * weight_in[:, 0:1]
     gate_grad = (hidden_grad * up * sig * (1.0 + gate * (1.0 - sig))).astype(BF16)
     up_grad = (hidden_grad * (gate * sig)).astype(BF16)
+    gate_turned, up_turned = gate_grad.T, up_grad.T
     steps = width // COLS
     for n in range(steps):
         at = slice(n * COLS, (n + 1) * COLS)
-        wide[:, n, :] = (
-            dot_nt(gate_grad[:, :split], first_ref[at, :])
-            + dot_nt(gate_grad[:, split:], second_ref[at, :])
-            + dot_nt(up_grad, up_ref[at, :])
-        )
+        wide[:, n, :] = (dot(gate_ref[at, :], gate_turned) + dot(up_ref[at, :], up_turned)).T
     lane = lax.broadcasted_iota(jnp.int32, (total, LANES), 1)
     high, low = high_low(jnp.where(lane == expert, prob, 0.0))
     wide[:, steps, 0:LANES] = high
@@ -210,18 +217,17 @@
     other_ref[...] = wide[count:].astype(BF16)
 
 
-def routed_body(act_ref, recv_ref, weight_in, down_ref, after_ref, mine_ref, other_ref, wide):
-    total, hidden = act_ref.shape
+def routed_body(
+    act_ref, recv_ref, weight_in, own_ref, away_ref, after_ref, mine_ref, other_ref, wide
+):
+    total = act_ref.shape[0]
     count = total // 2
-    feats = down_ref.shape[1]
-    local = lax.axis_index("local")
+    feats = own_ref.shape[1]
     weight = weight_in[:, 0:1]
     act, recv = act_ref[...], recv_ref[...]
-    own = pl.ds(pl.multiple_of(local * hidden, COLS), hidden)
-    away = pl.ds(pl.multiple_of((1 - local) * hidden, COLS), hidden)
     for n in range(feats // COLS):
         cols = slice(n * COLS, (n + 1) * COLS)
-        part = dot(act, down_ref[own, cols]) + dot(recv, down_ref[away, cols])
+        part = dot(act, own_ref[:, cols]) + dot(recv, away_ref[:, cols])
         part = part.astype(BF16).astype(F32) * weight
         wide[:, 2 * n, :] = part[:, :LANES]
         wide[:, 2 * n + 1, :] = part[:, LANES:]
@@ -270,7 +276,6 @@
     width = tokens.shape[2]
     hidden = gate_weight.shape[2]
     feats = down_weight.shape[2]
-    split = hidden // 2
     one = width * hidden * 2
     gate_hbm, up_hbm, down_hbm = in_hbm(gate_weight, up_weight, down_weight)
     (packed,) = call(
@@ -288,58 +293,64 @@
     )(*in_hbm(expert_ids, route_probs, tokens, out_grad))
     own = lax.all_to_all(packed, ("chip", "local"), split_axis=0, concat_axis=0, tiled=True)
     other = swap(own, "core")
-    away, cot, weight, rows, down_w, gate_first = call(
+    down_away, loaded = call(
+        load_body,
+        [pltpu.VMEM((hidden, feats), BF16), pltpu.VMEM((8, LANES), F32)],
+        [ANY, ANY],
+        [pltpu.SemaphoreType.DMA((hidden // COLS,))],
+        moved=one,
+    )(down_hbm, own)
+    away, cot, weight, rows, down_own, gate_w = call(
         cot_body,
         [
             shaped((total, hidden), BF16),
             shaped((total, hidden), F32),
             shaped((total, LANES), F32),
             shaped((total, width), BF16),
-            pltpu.VMEM((2 * hidden, feats), BF16),
-            pltpu.VMEM((width, split), BF16),
+            pltpu.VMEM((hidden, feats), BF16),
+            pltpu.VMEM((width, hidden), BF16),
         ],
-        [VMEM, VMEM, ANY, ANY],
+        [VMEM, VMEM, VMEM, ANY, ANY, ANY],
         [
             pltpu.VMEM((groups, ROWS, SPAN), F32),
             pltpu.VMEM((total, feats), BF16),
-            pltpu.SemaphoreType.DMA((2 * hidden // COLS + 1,)),
+            pltpu.SemaphoreType.DMA((hidden // COLS + width // DEPTH,)),
         ],
         products=total * one,
-        moved=3 * one // 2,
-    )(own, other, down_hbm, gate_hbm)
+        moved=2 * one,
+    )(own, other, down_away, loaded, down_hbm, gate_hbm)
     cot_recv = swap(away, "local")
-    gate, up, act, gate_second, up_w = call(
+    gate, up, act, up_w = call(
         forward_body,
         [
             shaped((total, hidden), F32),
             shaped((total, hidden), F32),
             shaped((total, hidden), BF16),
-            pltpu.VMEM((width, hidden - split), BF16),
             pltpu.VMEM((width, hidden), BF16),
         ],
-        [VMEM, VMEM, ANY, ANY],
-        [pltpu.SemaphoreType.DMA((2 * hidden // COLS,))],
+        [VMEM, VMEM, ANY],
+        [pltpu.SemaphoreType.DMA((width // DEPTH,))],
         products=total * 2 * one,
         moved=3 * one // 2,
-    )(rows, gate_first, gate_hbm, up_hbm)
+    )(rows, gate_w, up_hbm)
     act_recv = swap(act, "local")
     in_mine, in_away = call(
         input_body,
         [shaped((groups, ROWS, COLS), BF16)] * 2,
-        [VMEM] * 9,
+        [VMEM] * 8,
         [pltpu.VMEM((total, ROWS, COLS), F32)],
         products=total * 2 * one,
         moved=2 * one,
-    )(cot, cot_recv, gate, up, act, weight, gate_first, gate_second, up_w)
+    )(cot, cot_recv, gate, up, act, weight, gate_w, up_w)
     in_recv = swap(in_away, "core")
     routed_mine, routed_away = call(
         routed_body,
         [shaped((groups, ROWS, LANES), BF16)] * 2,
-        [VMEM] * 4 + [ANY],
+        [VMEM] * 5 + [ANY],
         [pltpu.VMEM((total, ROWS, LANES), F32)],
         products=total * one,
         moved=one,
-    )(act, act_recv, weight, down_w, in_mine)
+    )(act, act_recv, weight, down_own, down_away, in_mine)
     routed_recv = swap(routed_away, "core")
     summed = jnp.concatenate(
         [

time: 54.9 us -> 53 us (0.965)
  waiting for transfers between devices: 2.4 us -> 0.97 us
  Pallas kernels: 19.6 us -> 19 us
    pallas_call x2 -> x3, Pallas kernels: 5.9 us -> 7.68 us  [the longest x1 4.2 us: fast_device(): call(input_body, [shaped((groups, ROWS, COLS), BF16)] * 2, [VMEM] * 8, [p...]
    pallas_call x1, Pallas kernels: 5.66 us -> 3.91 us  [fast_device(): call(forward_body, [shaped((total, hidden), F32), shaped((total, hidden),...]
    ppermute x5, waiting for transfers between devices: 2.4 us -> 0.97 us  [swap(): return lax.ppermute(x, axis, [(0, 1), (1, 0)])]
    pallas_call x1, Pallas kernels: 6.03 us -> 5.44 us  [fast_device(): call(cot_body, [shaped((total, hidden), BF16), shaped((total, hidden), F3...]
  transfers between devices with their start and end apart: 5 -> 5, of which waited for: 3 -> 2; matrix products, arithmetic and copies ran while one was open for 0% -> 0% of each run, Pallas kernels for 19% -> 19%
where the time goes in v4:
time: 53 us; the launch traced here: 52.6 us
  blocking collectives  29.1 us (55%)
  Pallas kernels  19 us (36%)
  starting transfers between devices  2.73 us (5%)
  waiting for transfers between devices  0.97 us (2%)
  between operations  0.73 us (1%)
    all_to_all x1, blocking collectives, fast_device(): lax.all_to_all(packed, ('chip', 'local'), split_axis=0, concat_axis=0, ti...  16.8 us
    all_to_all x1, blocking collectives, fast_device(): lax.all_to_all(summed, ('chip', 'local'), split_axis=0, concat_axis=0, ti...  12.3 us
    pallas_call x1, Pallas kernels, fast_device(): call(cot_body, [shaped((total, hidden), BF16), shaped((total, hidden), F3...  5.44 us
    pallas_call x1, Pallas kernels, fast_device(): call(input_body, [shaped((groups, ROWS, COLS), BF16)] * 2, [VMEM] * 8, [p...  4.2 us
    pallas_call x1, Pallas kernels, fast_device(): call(forward_body, [shaped((total, hidden), F32), shaped((total, hidden),...  3.91 us
    ppermute x5, starting transfers between devices, swap(): return lax.ppermute(x, axis, [(0, 1), (1, 0)])  2.73 us
    pallas_call x1, Pallas kernels, fast_device(): call(load_body, [pltpu.VMEM((hidden, feats), BF16), pltpu.VMEM((8, LANES)...  2.04 us
    pallas_call x1, Pallas kernels, fast_device(): call(routed_body, [shaped((groups, ROWS, LANES), BF16)] * 2, [VMEM] * 5 +...  1.43 us
  transfers between devices with their start and end apart: 5, of which 2 were waited for; matrix products, arithmetic and copies ran while one was open for 0% of the time, Pallas kernels for 19%

profile of v4, /device:TPU:0, one launch (start us, length us, event | category | flops | bytes accessed | tf_op | source)
XLA Modules:
  0.0 52.6 jit_solution(12859107704981498131)
XLA Ops:
  0.6 0.8 %shard_map.94 = bf16[16,16,384]{2,1,0:T(8,128)(2,1)S(1)} custom-call(s32[1,1,8]{2,1,0:T(1,128)} %ids_ref.1, f32[1,1,8]{2,1,0:T(1,128)} %probs_hbm.1, bf16[1,1,3584]{2,1,0:T(2,128)(2,1)} %tok_hbm.1, bf16[1,1,3584]{2,1,0:T(2,128)(2,1)} %grad_hbm.1), custom_call_target="tpu_custom_call" | custom-call | tf_op jit(solution)/shard_map/pallas_call | solution.py:281
  1.4 16.8 %all_to_all.10.after_ref.own_ref = bf16[16,16,384]{2,1,0:T(8,128)(2,1)S(1)} all-to-all(bf16[16,16,384]{2,1,0:T(8,128)(2,1)S(1)} %shard_map.94), channel_id=1, replica_groups=mesh['chip'=8,'core'=2,'local'=2] {'chip','local'}, dimensions={0} | all-to-all | bytes 393216 | tf_op jit(solution)/shard_map/all_to_all | solution.py:294
  18.2 0.0 collective-permute-start
  18.2 2.0 %shard_map.95 = (bf16[1024,1792]{1,0:T(8,128)(2,1)S(1)}, f32[8,128]{1,0:T(8,128)S(1)}) custom-call(bf16[1,2048,1792]{2,1,0:T(8,128)(2,1)} %down_hbm.3, bf16[16,16,384]{2,1,0:T(8,128)(2,1)S(1)} %all_to_all.10.after_ref.own_ref), custom_call_target="tpu_custom_call" | custom-call | bytes 7340032 | tf_op jit(solution)/shard_map/pallas_call | solution.py:296
  20.3 0.0 collective-permute-done.other_ref
  20.3 5.4 %shard_map.96 = (bf16[32,1024]{1,0:T(8,128)(2,1)S(1)}, f32[32,1024]{1,0:T(8,128)S(1)}, f32[32,128]{1,0:T(8,128)S(1)}, bf16[32,3584]{1,0:T(8,128)(2,1)S(1)}, bf16...) custom-call(bf16[16,16,384]{2,1,0:T(8,128)(2,1)S(1)} %all_to_all.10.after_ref.own_ref, ...), custom_call_target="tpu_custom_call" | custom-call | flops 234881024 | bytes 14680064 | tf_op jit(solution)/shard_map/pallas_call | solution.py:303
  25.7 1.0 %collective-permute-start.1 = (bf16[32,1024]{1,0:T(8,128)(2,1)S(1)}, bf16[32,1024]{1,0:T(8,128)(2,1)S(1)}, u32[]{:S(2)}, u32[]{:S(2)}) collective-permute-start(bf16[32,1024]{1,0:T(8,128)(2,1)S(1)} %get-tuple-element.22), channel_id=1, source_target_pairs={{0,1},{1,0},{2,3},{3,2},{4,5},{5,4},{6,7},{7,6},{8,9},{9,8},{10,11... | collective-permute-start | bytes 196616 | tf_op jit(solution)/shard_map/ppermute | solution.py:270
  26.7 3.9 %shard_map.97 = (f32[32,1024]{1,0:T(8,128)S(1)}, f32[32,1024]{1,0:T(8,128)S(1)}, bf16[32,1024]{1,0:T(8,128)(2,1)S(1)}, bf16[3584,1024]{1,0:T(8,128)(2,1)S(1)}) custom-call(bf16[32,3584]{1,0:T(8,128)(2,1)S(1)} %get-tuple-element.23.rows_ref, bf16[3584,1024]{1,0:T(8,128)(2,1)S(1)} %get-tuple-element.24.gate_ref, bf16[1,3584,1024]{2,1,0:T(8,128)(2,1)} %up_hbm.1), custom_call_target="tpu_custom_call" | custom-call | flops 469762048 | bytes 11010048 | tf_op jit(solution)/shard_map/pallas_call | solution.py:323
  30.6 1.2 %collective-permute-start.3 = (bf16[32,1024]{1,0:T(8,128)(2,1)S(1)}, bf16[32,1024]{1,0:T(8,128)(2,1)S(1)}, u32[]{:S(2)}, u32[]{:S(2)}) collective-permute-start(bf16[32,1024]{1,0:T(8,128)(2,1)S(1)} %get-tuple-element.27.act_ref), channel_id=1, source_target_pairs={{0,1},{1,0},{2,3},{3,2},{4,5},{5,4},{6,7},{7,6},{8,9},{9,8},{10,11... | collective-permute-start | bytes 196616 | tf_op jit(solution)/shard_map/ppermute | solution.py:270
  31.8 0.0 collective-permute-done.1.recv_ref
  31.8 4.2 %shard_map.98 = (bf16[16,16,256]{2,1,0:T(8,128)(2,1)S(1)}, bf16[16,16,256]{2,1,0:T(8,128)(2,1)S(1)}) custom-call(f32[32,1024]{1,0:T(8,128)S(1)} %get-tuple-element.21.cot_ref, bf16[32,1024]{1,0:T(8,128)(2,1)S(1)} %collective-permute-done.1.recv_ref, f32[32,1024]{1,0:T(8,128)S(1)} %get-tuple-element.25.gate_in, f32[32,1024]{1,0:T(8,128)S(1)} %get-tuple-element.26.up_in, ...), custom_call_target="tpu_custom_call" | custom-call | flops 469762048 | bytes 14680064 | tf_op jit(solution)/shard_map/pallas_call | solution.py:337
  36.0 0.0 copy-start
  36.0 0.0 collective-permute-done.3.recv_ref
  36.0 1.4 %shard_map.99 = (bf16[16,16,128]{2,1,0:T(8,128)(2,1)S(1)}, bf16[16,16,128]{2,1,0:T(8,128)(2,1)S(1)}) custom-call(bf16[32,1024]{1,0:T(8,128)(2,1)S(1)} %get-tuple-element.27.act_ref, bf16[32,1024]{1,0:T(8,128)(2,1)S(1)} %collective-permute-done.3.recv_ref, f32[32,128]{1,0:T(8,128)S(1)} %get-tuple-element.28.weight_in, ...), custom_call_target="tpu_custom_call" | custom-call | flops 234881024 | bytes 7340032 | tf_op jit(solution)/shard_map/pallas_call | solution.py:346
  37.5 0.1 collective-permute-start.4
  37.5 0.5 collective-permute-start.2
  38.0 0.7 %collective-permute-done.4 = bf16[16,16,128]{2,1,0:T(8,128)(2,1)S(1)} collective-permute-done((bf16[16,16,128]{2,1,0:T(8,128)(2,1)S(1)}, bf16[16,16,128]{2,1,0:T(8,128)(2,1)S(1)}, u32[]{:S(2)}, u32[]{:S(2)}) %collective-permute-start.4) | collective-permute-done | bytes 65568 | tf_op jit(solution)/shard_map/ppermute | solution.py:270
  38.8 0.2 collective-permute-done.2
  39.1 12.3 %all_to_all.11.in_ref = bf16[16,16,384]{2,1,0:T(8,128)(2,1)S(1)} all-to-all(bf16[16,16,384]{2,1,0:T(8,128)(2,1)S(1)} %pad_maximum_fusion), channel_id=1, replica_groups=mesh['chip'=8,'core'=2,'local'=2] {'chip','local'}, dimensions={0} | all-to-all | bytes 393216 | tf_op jit(solution)/shard_map/all_to_all | solution.py:362
  51.4 0.0 copy-done
  51.4 1.2 %shard_map.100 = (bf16[1,1,3584]{2,1,0:T(2,128)(2,1)}, bf16[1,1,3584]{2,1,0:T(2,128)(2,1)}, f32[1,1,8]{2,1,0:T(1,128)}) custom-call(bf16[16,16,384]{2,1,0:T(8,128)(2,1)S(1)} %all_to_all.11.in_ref, s32[1,1,8]{2,1,0:T(1,128)S(1)} %copy-done), custom_call_target="tpu_custom_call" | custom-call | tf_op jit(solution)/shard_map/pallas_call | solution.py:363
  (3 shorter events, 0.1 us)
Async XLA Ops:
  18.2 2.1 %collective-permute-start = (bf16[16,16,384]{2,1,0:T(8,128)(2,1)S(1)}, bf16[16,16,384]{2,1,0:T(8,128)(2,1)S(1)}, u32[]{:S(2)}, u32[]{:S(2)}) collective-permute-start(bf16[16,16,384]{2,1,0:T(8,128)(2,1)S(1)} %all_to_all.10.after_ref.own_ref), channel_id=1, source_target_pairs={{0,2},{2,0},{1,3},{3,1},{4,6},{6,4},{5,7},{7,5},{8,10},{10,8},{9,1... | collective-permute-start | bytes 589832 | tf_op jit(solution)/shard_map/ppermute | solution.py:270
  25.7 6.1 %collective-permute-start.1 = (bf16[32,1024]{1,0:T(8,128)(2,1)S(1)}, bf16[32,1024]{1,0:T(8,128)(2,1)S(1)}, u32[]{:S(2)}, u32[]{:S(2)}) collective-permute-start(bf16[32,1024]{1,0:T(8,128)(2,1)S(1)} %get-tuple-element.22), channel_id=1, source_target_pairs={{0,1},{1,0},{2,3},{3,2},{4,5},{5,4},{6,7},{7,6},{8,9},{9,8},{10,11... | collective-permute-start | bytes 196616 | tf_op jit(solution)/shard_map/ppermute | solution.py:270
  30.6 5.4 %collective-permute-start.3 = (bf16[32,1024]{1,0:T(8,128)(2,1)S(1)}, bf16[32,1024]{1,0:T(8,128)(2,1)S(1)}, u32[]{:S(2)}, u32[]{:S(2)}) collective-permute-start(bf16[32,1024]{1,0:T(8,128)(2,1)S(1)} %get-tuple-element.27.act_ref), channel_id=1, source_target_pairs={{0,1},{1,0},{2,3},{3,2},{4,5},{5,4},{6,7},{7,6},{8,9},{9,8},{10,11... | collective-permute-start | bytes 196616 | tf_op jit(solution)/shard_map/ppermute | solution.py:270
  36.0 15.4 %copy-start = (s32[1,1,8]{2,1,0:T(1,128)S(1)}, s32[1,1,8]{2,1,0:T(1,128)}, u32[]{:S(2)}) copy-start(s32[1,1,8]{2,1,0:T(1,128)} %ids_ref.1) | copy-start | bytes 100
  37.5 1.3 %collective-permute-start.4 = (bf16[16,16,128]{2,1,0:T(8,128)(2,1)S(1)}, bf16[16,16,128]{2,1,0:T(8,128)(2,1)S(1)}, u32[]{:S(2)}, u32[]{:S(2)}) collective-permute-start(bf16[16,16,128]{2,1,0:T(8,128)(2,1)S(1)} %get-tuple-element.34), channel_id=1, source_target_pairs={{0,2},{2,0},{1,3},{3,1},{4,6},{6,4},{5,7},{7,5},{8,10},{10,8},{9,1... | collective-permute-start | bytes 196616 | tf_op jit(solution)/shard_map/ppermute | solution.py:270
  37.5 1.5 %collective-permute-start.2 = (bf16[16,16,256]{2,1,0:T(8,128)(2,1)S(1)}, bf16[16,16,256]{2,1,0:T(8,128)(2,1)S(1)}, u32[]{:S(2)}, u32[]{:S(2)}) collective-permute-start(bf16[16,16,256]{2,1,0:T(8,128)(2,1)S(1)} %get-tuple-element.31), channel_id=1, source_target_pairs={{0,2},{2,0},{1,3},{3,1},{4,6},{6,4},{5,7},{7,5},{8,10},{10,8},{9,1... | collective-permute-start | bytes 393224 | tf_op jit(solution)/shard_map/ppermute | solution.py:270

commit v5 on v4

--- a/solution.py
+++ b/solution.py
@@ -50,10 +50,6 @@
 
 def dot_nt(a, b):
     return lax.dot_general(a, b, NT, preferred_element_type=F32)
-
-
-def from_rows(weight, turned):
-    return dot(weight, turned).T
 
 
 def high_low(x):
@@ -96,7 +92,27 @@
     return pl.ds(pl.multiple_of(local * hidden + n * COLS, COLS), COLS)
 
 
-def load_body(down_hbm, after_ref, away_ref, token_ref, sems):
+def unpack_grads(wide, grads, first):
+    count = wide.shape[0]
+    for i in range(grads.shape[1] // LANES):
+        grads[first : first + count, i * LANES : (i + 1) * LANES] = wide[:, i, COLS:SPAN].astype(BF16)
+
+
+def unpack_row(wide, rows, first, i):
+    count = wide.shape[0]
+    rows[first : first + count, i * COLS : (i + 1) * COLS] = wide[:, i, 0:COLS].astype(BF16)
+
+
+def unpack_weight(wide, weight_out, first, meta):
+    count = wide.shape[0]
+    expert = lax.axis_index("chip") * 2 + lax.axis_index("core")
+    lane = lax.broadcasted_iota(jnp.int32, (count, LANES), 1)
+    both = wide[:, meta, 0:LANES] + wide[:, meta, LANES:COLS]
+    both = jnp.sum(jnp.where(lane == expert, both, 0.0), axis=1, keepdims=True)
+    weight_out[first : first + count, :] = jnp.broadcast_to(both, (count, LANES))
+
+
+def load_body(down_hbm, in_ref, away_ref, rows, grads, weight_out, wide, sems):
     hidden = away_ref.shape[0]
     away = 1 - lax.axis_index("local")
     copies = [
@@ -109,22 +125,25 @@
     ]
     for copy in copies:
         copy.start()
-    token_ref[...] = jnp.zeros_like(token_ref)
+    meta = rows.shape[1] // COLS
+    wide[...] = in_ref[...].astype(F32)
+    unpack_grads(wide, grads, 0)
+    for i in range(meta):
+        unpack_row(wide, rows, 0, i)
+    unpack_weight(wide, weight_out, 0, meta)
     for copy in copies:
         copy.wait()
 
 
 def cot_body(
-    own_ref, other_ref, loaded_ref, after_ref, down_hbm, gate_hbm,
+    other_ref, rows_in, grads_in, weight_in, loaded_ref, down_hbm, gate_hbm,
     away_ref, cot_ref, weight_out, rows, down_ref, gate_ref,
     wide, grads, sems,
 ):
-    count = own_ref.shape[0]
+    count = other_ref.shape[0]
     width = rows.shape[1]
     hidden = cot_ref.shape[1]
-    feats = down_ref.shape[1]
     local = lax.axis_index("local")
-    expert = lax.axis_index("chip") * 2 + lax.axis_index("core")
     steps = hidden // COLS
     copies = []
     for n in range(steps):
@@ -132,68 +151,73 @@
         copies.append(
             pltpu.make_async_copy(down_hbm.at[0, side_rows(local, hidden, n), :], into, sems.at[n])
         )
-    for n in range(width // DEPTH):
+    for n in range(gate_ref.shape[0] // DEPTH):
         at = slice(n * DEPTH, (n + 1) * DEPTH)
         copies.append(
             pltpu.make_async_copy(gate_hbm.at[0, at, :], gate_ref.at[at, :], sems.at[steps + n])
         )
     for copy in copies:
         copy.start()
-
-    lane = lax.broadcasted_iota(jnp.int32, (count, LANES), 1)
     meta = width // COLS
-    for half, ref in enumerate((own_ref, other_ref)):
-        at = pl.ds(half * count, count)
-        wide[...] = ref[...].astype(F32)
-        for i in range(feats // LANES):
-            grads[at, i * LANES : (i + 1) * LANES] = wide[:, i, COLS:SPAN].astype(BF16)
-        for i in range(meta):
-            rows[at, i * COLS : (i + 1) * COLS] = wide[:, i, 0:COLS].astype(BF16)
-        both = wide[:, meta, 0:LANES] + wide[:, meta, LANES:COLS]
-        both = jnp.sum(jnp.where(lane == expert, both, 0.0), axis=1, keepdims=True)
-        weight_out[at, :] = jnp.broadcast_to(both, (count, LANES))
-    grad = grads[...].T
+    wide[...] = other_ref[...].astype(F32)
+    unpack_grads(wide, grads, count)
+    grads[:count, :] = grads_in[...]
+    grad = grads[...]
     for n in range(steps):
         at = slice(n * COLS, (n + 1) * COLS)
-        away_ref[:, at] = from_rows(loaded_ref[at, :], grad).astype(BF16)
+        away_ref[:, at] = dot_nt(grad, loaded_ref[at, :]).astype(BF16)
+        for i in range(n, meta, steps):
+            unpack_row(wide, rows, count, i)
+    unpack_weight(wide, weight_out, count, meta)
+    weight_out[:count, :] = weight_in[...]
+    rows[:count, :] = rows_in[...]
     for n in range(steps):
         at = slice(n * COLS, (n + 1) * COLS)
         copies[n].wait()
-        cot_ref[:, at] = from_rows(down_ref[at, :], grad)
+        cot_ref[:, at] = dot_nt(grad, down_ref[at, :])
     for copy in copies[steps:]:
         copy.wait()
 
 
-def forward_body(rows_ref, gate_ref, up_hbm, gate_out, up_out, act_ref, up_ref, sems):
-    width, hidden = gate_ref.shape
-    pieces = [slice(n * DEPTH, (n + 1) * DEPTH) for n in range(width // DEPTH)]
+def forward_body(
+    rows_ref, gate_ref, gate_hbm, up_hbm, gate_out, up_out, act_ref, gate_rest, up_ref, sems
+):
+    early, hidden = gate_ref.shape
+    width = up_ref.shape[0]
     columns = [slice(n * COLS, (n + 1) * COLS) for n in range(hidden // COLS)]
+    pieces = []
+    for n in range(early // DEPTH, width // DEPTH):
+        at = slice(n * DEPTH, (n + 1) * DEPTH)
+        held = gate_rest.at[n * DEPTH - early : (n + 1) * DEPTH - early, :]
+        pieces.append((gate_hbm.at[0, at, :], held, at, gate_out, False))
+    for n in range(width // DEPTH):
+        at = slice(n * DEPTH, (n + 1) * DEPTH)
+        pieces.append((up_hbm.at[0, at, :], up_ref.at[at, :], at, up_out, n == 0))
     copies = [
-        pltpu.make_async_copy(up_hbm.at[0, at, :], up_ref.at[at, :], sems.at[n])
-        for n, at in enumerate(pieces)
+        pltpu.make_async_copy(piece[0], piece[1], sems.at[i]) for i, piece in enumerate(pieces)
     ]
     for copy in copies:
         copy.start()
     for cols in columns:
-        gate_out[:, cols] = dot(rows_ref[...], gate_ref[:, cols])
-    for n, at in enumerate(pieces):
-        copies[n].wait()
+        gate_out[:, cols] = dot(rows_ref[:, :early], gate_ref[:, cols])
+    for copy, (_, held, at, out, fresh) in zip(copies, pieces):
+        copy.wait()
         for cols in columns:
-            part = dot(rows_ref[:, at], up_ref[at, cols])
-            up_out[:, cols] = part if n == 0 else up_out[:, cols] + part
+            part = dot(rows_ref[:, at], held[:, cols])
+            out[:, cols] = part if fresh else out[:, cols] + part
     for cols in columns:
         gate = gate_out[:, cols]
         act_ref[:, cols] = (gate * jax.nn.sigmoid(gate) * up_out[:, cols]).astype(BF16)
 
 
 def input_body(
-    cot_ref, recv_ref, gate_in, up_in, act_ref, weight_in, gate_ref, up_ref,
+    cot_ref, recv_ref, gate_in, up_in, act_ref, weight_in, gate_ref, gate_rest, up_ref,
     mine_ref, other_ref,
     wide,
 ):
     total = cot_ref.shape[0]
     count = total // 2
-    width = up_ref.shape[0]
+    width, early = up_ref.shape[0], gate_ref.shape[0]
     expert = lax.axis_index("chip") * 2 + lax.axis_index("core")
     gate, up = gate_in[...], up_in[...]
     sig = jax.nn.sigmoid(gate)
@@ -206,7 +230,12 @@
     steps = width // COLS
     for n in range(steps):
         at = slice(n * COLS, (n + 1) * COLS)
-        wide[:, n, :] = (dot(gate_ref[at, :], gate_turned) + dot(up_ref[at, :], up_turned)).T
+        if n * COLS < early:
+            part = dot(gate_ref[at, :], gate_turned)
+        else:
+            part = dot(gate_rest[n * COLS - early : (n + 1) * COLS - early, :], gate_turned)
+        part += dot(up_ref[at, :], up_turned)
+        wide[:, n, :] = part.astype(BF16).T.astype(F32)
     lane = lax.broadcasted_iota(jnp.int32, (total, LANES), 1)
     high, low = high_low(jnp.where(lane == expert, prob, 0.0))
     wide[:, steps, 0:LANES] = high
@@ -277,6 +306,7 @@
     hidden = gate_weight.shape[2]
     feats = down_weight.shape[2]
     one = width * hidden * 2
+    early = width // DEPTH * 5 // 7 * DEPTH
     gate_hbm, up_hbm, down_hbm = in_hbm(gate_weight, up_weight, down_weight)
     (packed,) = call(
         pack_body,
@@ -293,11 +323,16 @@
     )(*in_hbm(expert_ids, route_probs, tokens, out_grad))
     own = lax.all_to_all(packed, ("chip", "local"), split_axis=0, concat_axis=0, tiled=True)
     other = swap(own, "core")
-    down_away, loaded = call(
+    down_away, own_rows, own_grads, own_weight = call(
         load_body,
-        [pltpu.VMEM((hidden, feats), BF16), pltpu.VMEM((8, LANES), F32)],
-        [ANY, ANY],
-        [pltpu.SemaphoreType.DMA((hidden // COLS,))],
+        [
+            pltpu.VMEM((hidden, feats), BF16),
+            shaped((groups, width), BF16),
+            shaped((groups, feats), BF16),
+            shaped((groups, LANES), F32),
+        ],
+        [ANY, VMEM],
+        [pltpu.VMEM((groups, ROWS, SPAN), F32), pltpu.SemaphoreType.DMA((hidden // COLS,))],
         moved=one,
     )(down_hbm, own)
     away, cot, weight, rows, down_own, gate_w = call(
@@ -308,40 +343,41 @@
             shaped((total, LANES), F32),
             shaped((total, width), BF16),
             pltpu.VMEM((hidden, feats), BF16),
-            pltpu.VMEM((width, hidden), BF16),
-        ],
-        [VMEM, VMEM, VMEM, ANY, ANY, ANY],
+            pltpu.VMEM((early, hidden), BF16),
+        ],
+        [VMEM] * 5 + [ANY] * 2,
         [
             pltpu.VMEM((groups, ROWS, SPAN), F32),
             pltpu.VMEM((total, feats), BF16),
-            pltpu.SemaphoreType.DMA((hidden // COLS + width // DEPTH,)),
+            pltpu.SemaphoreType.DMA((hidden // COLS + early // DEPTH,)),
         ],
         products=total * one,
         moved=2 * one,
-    )(own, other, down_away, loaded, down_hbm, gate_hbm)
+    )(other, own_rows, own_grads, own_weight, down_away, down_hbm, gate_hbm)
     cot_recv = swap(away, "local")
-    gate, up, act, up_w = call(
+    gate, up, act, gate_rest, up_w = call(
         forward_body,
         [
             shaped((total, hidden), F32),
             shaped((total, hidden), F32),
             shaped((total, hidden), BF16),
+            pltpu.VMEM((width - early, hidden), BF16),
             pltpu.VMEM((width, hidden), BF16),
         ],
-        [VMEM, VMEM, ANY],
-        [pltpu.SemaphoreType.DMA((width // DEPTH,))],
+        [VMEM, VMEM, ANY, ANY],
+        [pltpu.SemaphoreType.DMA(((2 * width - early) // DEPTH,))],
         products=total * 2 * one,
         moved=3 * one // 2,
-    )(rows, gate_w, up_hbm)
+    )(rows, gate_w, gate_hbm, up_hbm)
     act_recv = swap(act, "local")
     in_mine, in_away = call(
         input_body,
         [shaped((groups, ROWS, COLS), BF16)] * 2,
-        [VMEM] * 8,
+        [VMEM] * 9,
         [pltpu.VMEM((total, ROWS, COLS), F32)],
         products=total * 2 * one,
         moved=2 * one,
-    )(cot, cot_recv, gate, up, act, weight, gate_w, up_w)
+    )(cot, cot_recv, gate, up, act, weight, gate_w, gate_rest, up_w)
     in_recv = swap(in_away, "core")
     routed_mine, routed_away = call(
         routed_body,

time: 53 us -> 52.6 us (level)
    pallas_call x1, Pallas kernels: 5.44 us -> 4.84 us  [fast_device(): call(cot_body, [shaped((total, hidden), BF16), shaped((total, hidden), F3...]
  transfers between devices with their start and end apart: 5 -> 5, of which waited for: 2 -> 2; matrix products, arithmetic and copies ran while one was open for 0% -> 0% of each run, Pallas kernels for 19% -> 20%
where the time goes in v5:
time: 52.6 us; the launch traced here: 52.3 us
  blocking collectives  29.1 us (55%)
  Pallas kernels  18.7 us (36%)
  starting transfers between devices  2.73 us (5%)
  waiting for transfers between devices  0.97 us (2%)
  between operations  0.73 us (1%)
    all_to_all x1, blocking collectives, fast_device(): lax.all_to_all(packed, ('chip', 'local'), split_axis=0, concat_axis=0, ti...  16.8 us
    all_to_all x1, blocking collectives, fast_device(): lax.all_to_all(summed, ('chip', 'local'), split_axis=0, concat_axis=0, ti...  12.3 us
    pallas_call x1, Pallas kernels, fast_device(): call(cot_body, [shaped((total, hidden), BF16), shaped((total, hidden), F3...  4.84 us
    pallas_call x1, Pallas kernels, fast_device(): call(input_body, [shaped((groups, ROWS, COLS), BF16)] * 2, [VMEM] * 9, [p...  4.24 us
    pallas_call x1, Pallas kernels, fast_device(): call(forward_body, [shaped((total, hidden), F32), shaped((total, hidden),...  4.07 us
    ppermute x5, starting transfers between devices, swap(): return lax.ppermute(x, axis, [(0, 1), (1, 0)])  2.73 us
    pallas_call x1, Pallas kernels, fast_device(): call(load_body, [pltpu.VMEM((hidden, feats), BF16), shaped((groups, width...  2.07 us
    pallas_call x1, Pallas kernels, fast_device(): call(routed_body, [shaped((groups, ROWS, LANES), BF16)] * 2, [VMEM] * 5 +...  1.43 us
  transfers between devices with their start and end apart: 5, of which 2 were waited for; matrix products, arithmetic and copies ran while one was open for 0% of the time, Pallas kernels for 20%

profile of v5, /device:TPU:0, one launch (start us, length us, event | category | flops | bytes accessed | tf_op | source)
XLA Modules:
  0.0 52.3 jit_solution(8402858978100522940)
XLA Ops:
  0.6 0.8 %shard_map.94 = bf16[16,16,384]{2,1,0:T(8,128)(2,1)S(1)} custom-call(s32[1,1,8]{2,1,0:T(1,128)} %ids_ref.1, f32[1,1,8]{2,1,0:T(1,128)} %probs_hbm.1, bf16[1,1,3584]{2,1,0:T(2,128)(2,1)} %tok_hbm.1, bf16[1,1,3584]{2,1,0:T(2,128)(2,1)} %grad_hbm.1), custom_call_target="tpu_custom_call" | custom-call | tf_op jit(solution)/shard_map/pallas_call | solution.py:311
  1.4 16.8 %all_to_all.10.in_ref = bf16[16,16,384]{2,1,0:T(8,128)(2,1)S(1)} all-to-all(bf16[16,16,384]{2,1,0:T(8,128)(2,1)S(1)} %shard_map.94), channel_id=1, replica_groups=mesh['chip'=8,'core'=2,'local'=2] {'chip','local'}, dimensions={0} | all-to-all | bytes 393216 | tf_op jit(solution)/shard_map/all_to_all | solution.py:324
  18.2 0.0 collective-permute-start
  18.2 2.1 %shard_map.95 = (bf16[1024,1792]{1,0:T(8,128)(2,1)S(1)}, bf16[16,3584]{1,0:T(8,128)(2,1)S(1)}, bf16[16,1792]{1,0:T(8,128)(2,1)S(1)}, f32[16,128]{1,0:T(8,128)S(1)}) custom-call(bf16[1,2048,1792]{2,1,0:T(8,128)(2,1)} %down_hbm.3, bf16[16,16,384]{2,1,0:T(8,128)(2,1)S(1)} %all_to_all.10.in_ref), custom_call_target="tpu_custom_call" | custom-call | bytes 7340032 | tf_op jit(solution)/shard_map/pallas_call | solution.py:326
  20.3 0.0 collective-permute-done.other_ref
  20.3 4.8 %shard_map.96 = (bf16[32,1024]{1,0:T(8,128)(2,1)S(1)}, f32[32,1024]{1,0:T(8,128)S(1)}, f32[32,128]{1,0:T(8,128)S(1)}, bf16[32,3584]{1,0:T(8,128)(2,1)S(1)}, bf16...) custom-call(bf16[16,16,384]{2,1,0:T(8,128)(2,1)S(1)} %collective-permute-done.other_ref, ...), custom_call_target="tpu_custom_call" | custom-call | flops 234881024 | bytes 14680064 | tf_op jit(solution)/shard_map/pallas_call | solution.py:338
  25.1 1.0 %collective-permute-start.1 = (bf16[32,1024]{1,0:T(8,128)(2,1)S(1)}, bf16[32,1024]{1,0:T(8,128)(2,1)S(1)}, u32[]{:S(2)}, u32[]{:S(2)}) collective-permute-start(bf16[32,1024]{1,0:T(8,128)(2,1)S(1)} %get-tuple-element.27), channel_id=1, source_target_pairs={{0,1},{1,0},{2,3},{3,2},{4,5},{5,4},{6,7},{7,6},{8,9},{9,8},{10,11... | collective-permute-start | bytes 196616 | tf_op jit(solution)/shard_map/ppermute | solution.py:299
  26.2 4.1 %shard_map.97 = (f32[32,1024]{1,0:T(8,128)S(1)}, f32[32,1024]{1,0:T(8,128)S(1)}, bf16[32,1024]{1,0:T(8,128)(2,1)S(1)}, bf16[1024,1024]{1,0:T(8,128)(2,1)S(1)}, bf16[3584,1024]{1,0:T(8,128)(2,1)S(1)}) custom-call(bf16[32,3584]{1,0:T(8,128)(2,1)S(1)} %get-tuple-element.28.rows_ref, bf16[2560,1024]{1,0:T(8,128)(2,1)S(1)} %get-tuple-element.29.gate_ref, ...), custom_call_target="tpu_custom_call" | custom-call | flops 469762048 | bytes 11010048 | tf_op jit(solution)/shard_map/pallas_call | solution.py:358
  30.2 1.1 %collective-permute-start.3 = (bf16[32,1024]{1,0:T(8,128)(2,1)S(1)}, bf16[32,1024]{1,0:T(8,128)(2,1)S(1)}, u32[]{:S(2)}, u32[]{:S(2)}) collective-permute-start(bf16[32,1024]{1,0:T(8,128)(2,1)S(1)} %get-tuple-element.32.act_ref), channel_id=1, source_target_pairs={{0,1},{1,0},{2,3},{3,2},{4,5},{5,4},{6,7},{7,6},{8,9},{9,8},{10,11... | collective-permute-start | bytes 196616 | tf_op jit(solution)/shard_map/ppermute | solution.py:299
  31.4 0.0 collective-permute-done.1.recv_ref
  31.4 4.2 %shard_map.98 = (bf16[16,16,256]{2,1,0:T(8,128)(2,1)S(1)}, bf16[16,16,256]{2,1,0:T(8,128)(2,1)S(1)}) custom-call(f32[32,1024]{1,0:T(8,128)S(1)} %get-tuple-element.26.cot_ref, bf16[32,1024]{1,0:T(8,128)(2,1)S(1)} %collective-permute-done.1.recv_ref, f32[32,1024]{1,0:T(8,128)S(1)} %get-tuple-element.30.gate_in, f32[32,1024]{1,0:T(8,128)S(1)} %get-tuple-element.31.up_in, ...), custom_call_target="tpu_custom_call" | custom-call | flops 469762048 | bytes 14680064 | tf_op jit(solution)/shard_map/pallas_call | solution.py:373
  35.6 0.0 copy-start
  35.6 0.0 collective-permute-done.3.recv_ref
  35.7 1.4 %shard_map.99 = (bf16[16,16,128]{2,1,0:T(8,128)(2,1)S(1)}, bf16[16,16,128]{2,1,0:T(8,128)(2,1)S(1)}) custom-call(bf16[32,1024]{1,0:T(8,128)(2,1)S(1)} %get-tuple-element.32.act_ref, bf16[32,1024]{1,0:T(8,128)(2,1)S(1)} %collective-permute-done.3.recv_ref, f32[32,128]{1,0:T(8,128)S(1)} %get-tuple-element.33.weight_in, ...), custom_call_target="tpu_custom_call" | custom-call | flops 234881024 | bytes 7340032 | tf_op jit(solution)/shard_map/pallas_call | solution.py:382
  37.1 0.1 collective-permute-start.4
  37.2 0.5 collective-permute-start.2
  37.7 0.7 %collective-permute-done.4 = bf16[16,16,128]{2,1,0:T(8,128)(2,1)S(1)} collective-permute-done((bf16[16,16,128]{2,1,0:T(8,128)(2,1)S(1)}, bf16[16,16,128]{2,1,0:T(8,128)(2,1)S(1)}, u32[]{:S(2)}, u32[]{:S(2)}) %collective-permute-start.4) | collective-permute-done | bytes 65568 | tf_op jit(solution)/shard_map/ppermute | solution.py:299
  38.4 0.2 collective-permute-done.2
  38.7 12.3 %all_to_all.11.in_ref = bf16[16,16,384]{2,1,0:T(8,128)(2,1)S(1)} all-to-all(bf16[16,16,384]{2,1,0:T(8,128)(2,1)S(1)} %pad_maximum_fusion), channel_id=1, replica_groups=mesh['chip'=8,'core'=2,'local'=2] {'chip','local'}, dimensions={0} | all-to-all | bytes 393216 | tf_op jit(solution)/shard_map/all_to_all | solution.py:398
  51.1 0.0 copy-done
  51.1 1.2 %shard_map.100 = (bf16[1,1,3584]{2,1,0:T(2,128)(2,1)}, bf16[1,1,3584]{2,1,0:T(2,128)(2,1)}, f32[1,1,8]{2,1,0:T(1,128)}) custom-call(bf16[16,16,384]{2,1,0:T(8,128)(2,1)S(1)} %all_to_all.11.in_ref, s32[1,1,8]{2,1,0:T(1,128)S(1)} %copy-done), custom_call_target="tpu_custom_call" | custom-call | tf_op jit(solution)/shard_map/pallas_call | solution.py:399
  (3 shorter events, 0.1 us)
Async XLA Ops:
  18.2 2.1 %collective-permute-start = (bf16[16,16,384]{2,1,0:T(8,128)(2,1)S(1)}, bf16[16,16,384]{2,1,0:T(8,128)(2,1)S(1)}, u32[]{:S(2)}, u32[]{:S(2)}) collective-permute-start(bf16[16,16,384]{2,1,0:T(8,128)(2,1)S(1)} %all_to_all.10.in_ref), channel_id=1, source_target_pairs={{0,2},{2,0},{1,3},{3,1},{4,6},{6,4},{5,7},{7,5},{8,10},{10,8},{9,1... | collective-permute-start | bytes 589832 | tf_op jit(solution)/shard_map/ppermute | solution.py:299
  25.1 6.2 %collective-permute-start.1 = (bf16[32,1024]{1,0:T(8,128)(2,1)S(1)}, bf16[32,1024]{1,0:T(8,128)(2,1)S(1)}, u32[]{:S(2)}, u32[]{:S(2)}) collective-permute-start(bf16[32,1024]{1,0:T(8,128)(2,1)S(1)} %get-tuple-element.27), channel_id=1, source_target_pairs={{0,1},{1,0},{2,3},{3,2},{4,5},{5,4},{6,7},{7,6},{8,9},{9,8},{10,11... | collective-permute-start | bytes 196616 | tf_op jit(solution)/shard_map/ppermute | solution.py:299
  30.2 5.4 %collective-permute-start.3 = (bf16[32,1024]{1,0:T(8,128)(2,1)S(1)}, bf16[32,1024]{1,0:T(8,128)(2,1)S(1)}, u32[]{:S(2)}, u32[]{:S(2)}) collective-permute-start(bf16[32,1024]{1,0:T(8,128)(2,1)S(1)} %get-tuple-element.32.act_ref), channel_id=1, source_target_pairs={{0,1},{1,0},{2,3},{3,2},{4,5},{5,4},{6,7},{7,6},{8,9},{9,8},{10,11... | collective-permute-start | bytes 196616 | tf_op jit(solution)/shard_map/ppermute | solution.py:299
  35.6 15.4 %copy-start = (s32[1,1,8]{2,1,0:T(1,128)S(1)}, s32[1,1,8]{2,1,0:T(1,128)}, u32[]{:S(2)}) copy-start(s32[1,1,8]{2,1,0:T(1,128)} %ids_ref.1) | copy-start | bytes 100
  37.1 1.3 %collective-permute-start.4 = (bf16[16,16,128]{2,1,0:T(8,128)(2,1)S(1)}, bf16[16,16,128]{2,1,0:T(8,128)(2,1)S(1)}, u32[]{:S(2)}, u32[]{:S(2)}) collective-permute-start(bf16[16,16,128]{2,1,0:T(8,128)(2,1)S(1)} %get-tuple-element.40), channel_id=1, source_target_pairs={{0,2},{2,0},{1,3},{3,1},{4,6},{6,4},{5,7},{7,5},{8,10},{10,8},{9,1... | collective-permute-start | bytes 196616 | tf_op jit(solution)/shard_map/ppermute | solution.py:299
  37.2 1.5 %collective-permute-start.2 = (bf16[16,16,256]{2,1,0:T(8,128)(2,1)S(1)}, bf16[16,16,256]{2,1,0:T(8,128)(2,1)S(1)}, u32[]{:S(2)}, u32[]{:S(2)}) collective-permute-start(bf16[16,16,256]{2,1,0:T(8,128)(2,1)S(1)} %get-tuple-element.37), channel_id=1, source_target_pairs={{0,2},{2,0},{1,3},{3,1},{4,6},{6,4},{5,7},{7,5},{8,10},{10,8},{9,1... | collective-permute-start | bytes 393224 | tf_op jit(solution)/shard_map/ppermute | solution.py:299

commit v6 on v5

--- a/solution.py
+++ b/solution.py
@@ -12,7 +12,6 @@
 F32 = jnp.float32
 LANES = 128
 COLS = 256
-DEPTH = 512
 ROWS = 16
 SPAN = COLS + LANES
 
@@ -58,7 +57,7 @@
 
 
 def pack_body(
-    ids_hbm, probs_hbm, tok_hbm, grad_hbm, out_ref, wide, ids_ref, probs_ref, tok_ref, grad_ref, sems
+    ids_hbm, probs_hbm, tok_hbm, grad_hbm, gate_hbm, up_hbm, down_hbm, out_ref, wide, ids_ref, probs_ref, tok_ref, grad_ref, sems
 ):
     pairs = ((ids_hbm, ids_ref), (probs_hbm, probs_ref), (tok_hbm, tok_ref), (grad_hbm, grad_ref))
     copies = [pltpu.make_async_copy(a, b, sems.at[i]) for i, (a, b) in enumerate(pairs)]
@@ -112,52 +111,25 @@
     weight_out[first : first + count, :] = jnp.broadcast_to(both, (count, LANES))
 
 
-def load_body(down_hbm, in_ref, away_ref, rows, grads, weight_out, wide, sems):
-    hidden = away_ref.shape[0]
-    away = 1 - lax.axis_index("local")
-    copies = [
-        pltpu.make_async_copy(
-            down_hbm.at[0, side_rows(away, hidden, n), :],
-            away_ref.at[n * COLS : (n + 1) * COLS, :],
-            sems.at[n],
-        )
-        for n in range(hidden // COLS)
-    ]
-    for copy in copies:
-        copy.start()
+def unpack_body(in_ref, rows, grads, weight_out, wide):
     meta = rows.shape[1] // COLS
     wide[...] = in_ref[...].astype(F32)
     unpack_grads(wide, grads, 0)
     for i in range(meta):
         unpack_row(wide, rows, 0, i)
     unpack_weight(wide, weight_out, 0, meta)
-    for copy in copies:
-        copy.wait()
 
 
 def cot_body(
-    other_ref, rows_in, grads_in, weight_in, loaded_ref, down_hbm, gate_hbm,
-    away_ref, cot_ref, weight_out, rows, down_ref, gate_ref,
-    wide, grads, sems,
+    other_ref, rows_in, grads_in, weight_in, down_ref,
+    away_ref, cot_ref, weight_out, rows,
+    wide, grads,
 ):
     count = other_ref.shape[0]
     width = rows.shape[1]
     hidden = cot_ref.shape[1]
     local = lax.axis_index("local")
     steps = hidden // COLS
-    copies = []
-    for n in range(steps):
-        into = down_ref.at[n * COLS : (n + 1) * COLS, :]
-        copies.append(
-            pltpu.make_async_copy(down_hbm.at[0, side_rows(local, hidden, n), :], into, sems.at[n])
-        )
-    for n in range(gate_ref.shape[0] // DEPTH):
-        at = slice(n * DEPTH, (n + 1) * DEPTH)
-        copies.append(
-            pltpu.make_async_copy(gate_hbm.at[0, at, :], gate_ref.at[at, :], sems.at[steps + n])
-        )
-    for copy in copies:
-        copy.start()
     meta = width // COLS
     wide[...] = other_ref[...].astype(F32)
     unpack_grads(wide, grads, count)
@@ -165,59 +137,35 @@
     grad = grads[...]
     for n in range(steps):
         at = slice(n * COLS, (n + 1) * COLS)
-        away_ref[:, at] = dot_nt(grad, loaded_ref[at, :]).astype(BF16)
-        for i in range(n, meta, steps):
-            unpack_row(wide, rows, count, i)
+        away_ref[:, at] = dot_nt(grad, down_ref[side_rows(1 - local, hidden, n), :]).astype(BF16)
+    for n in range(steps):
+        at = slice(n * COLS, (n + 1) * COLS)
+        cot_ref[:, at] = dot_nt(grad, down_ref[side_rows(local, hidden, n), :])
+    for i in range(meta):
+        unpack_row(wide, rows, count, i)
     unpack_weight(wide, weight_out, count, meta)
     weight_out[:count, :] = weight_in[...]
     rows[:count, :] = rows_in[...]
-    for n in range(steps):
-        at = slice(n * COLS, (n + 1) * COLS)
-        copies[n].wait()
-        cot_ref[:, at] = dot_nt(grad, down_ref[at, :])
-    for copy in copies[steps:]:
-        copy.wait()
-
-
-def forward_body(
-    rows_ref, gate_ref, gate_hbm, up_hbm, gate_out, up_out, act_ref, gate_rest, up_ref, sems
-):
-    early, hidden = gate_ref.shape
-    width = up_ref.shape[0]
-    columns = [slice(n * COLS, (n + 1) * COLS) for n in range(hidden // COLS)]
-    pieces = []
-    for n in range(early // DEPTH, width // DEPTH):
-        at = slice(n * DEPTH, (n + 1) * DEPTH)
-        held = gate_rest.at[n * DEPTH - early : (n + 1) * DEPTH - early, :]
-        pieces.append((gate_hbm.at[0, at, :], held, at, gate_out, False))
-    for n in range(width // DEPTH):
-        at = slice(n * DEPTH, (n + 1) * DEPTH)
-        pieces.append((up_hbm.at[0, at, :], up_ref.at[at, :], at, up_out, n == 0))
-    copies = [
-        pltpu.make_async_copy(piece[0], piece[1], sems.at[i]) for i, piece in enumerate(pieces)
-    ]
-    for copy in copies:
-        copy.start()
-    for cols in columns:
-        gate_out[:, cols] = dot(rows_ref[:, :early], gate_ref[:, cols])
-    for copy, (_, held, at, out, fresh) in zip(copies, pieces):
-        copy.wait()
-        for cols in columns:
-            part = dot(rows_ref[:, at], held[:, cols])
-            out[:, cols] = part if fresh else out[:, cols] + part
-    for cols in columns:
-        gate = gate_out[:, cols]
-        act_ref[:, cols] = (gate * jax.nn.sigmoid(gate) * up_out[:, cols]).astype(BF16)
+
+
+def forward_body(rows_ref, gate_ref, up_ref, gate_out, up_out, act_ref):
+    tokens = rows_ref[...]
+    for n in range(gate_ref.shape[1] // COLS):
+        cols = slice(n * COLS, (n + 1) * COLS)
+        gate, up = dot(tokens, gate_ref[:, cols]), dot(tokens, up_ref[:, cols])
+        gate_out[:, cols] = gate
+        up_out[:, cols] = up
+        act_ref[:, cols] = (gate * jax.nn.sigmoid(gate) * up).astype(BF16)
 
 
 def input_body(
-    cot_ref, recv_ref, gate_in, up_in, act_ref, weight_in, gate_ref, gate_rest, up_ref,
+    cot_ref, recv_ref, gate_in, up_in, act_ref, weight_in, gate_ref, up_ref,
     mine_ref, other_ref,
     wide,
 ):
     total = cot_ref.shape[0]
     count = total // 2
-    width, early = up_ref.shape[0], gate_ref.shape[0]
+    width = up_ref.shape[0]
     expert = lax.axis_index("chip") * 2 + lax.axis_index("core")
     gate, up = gate_in[...], up_in[...]
     sig = jax.nn.sigmoid(gate)
@@ -230,12 +178,7 @@
     steps = width // COLS
     for n in range(steps):
         at = slice(n * COLS, (n + 1) * COLS)
-        if n * COLS < early:
-            part = dot(gate_ref[at, :], gate_turned)
-        else:
-            part = dot(gate_rest[n * COLS - early : (n + 1) * COLS - early, :], gate_turned)
-        part += dot(up_ref[at, :], up_turned)
-        wide[:, n, :] = part.astype(BF16).T.astype(F32)
+        wide[:, n, :] = (dot(gate_ref[at, :], gate_turned) + dot(up_ref[at, :], up_turned)).T
     lane = lax.broadcasted_iota(jnp.int32, (total, LANES), 1)
     high, low = high_low(jnp.where(lane == expert, prob, 0.0))
     wide[:, steps, 0:LANES] = high
@@ -246,17 +189,18 @@
     other_ref[...] = wide[count:].astype(BF16)
 
 
-def routed_body(
-    act_ref, recv_ref, weight_in, own_ref, away_ref, after_ref, mine_ref, other_ref, wide
-):
-    total = act_ref.shape[0]
+def routed_body(act_ref, recv_ref, weight_in, down_ref, after_ref, mine_ref, other_ref, wide):
+    total, hidden = act_ref.shape
     count = total // 2
-    feats = own_ref.shape[1]
+    feats = down_ref.shape[1]
+    local = lax.axis_index("local")
     weight = weight_in[:, 0:1]
     act, recv = act_ref[...], recv_ref[...]
+    own = pl.ds(pl.multiple_of(local * hidden, COLS), hidden)
+    away = pl.ds(pl.multiple_of((1 - local) * hidden, COLS), hidden)
     for n in range(feats // COLS):
         cols = slice(n * COLS, (n + 1) * COLS)
-        part = dot(act, own_ref[:, cols]) + dot(recv, away_ref[:, cols])
+        part = dot(act, down_ref[own, cols]) + dot(recv, down_ref[away, cols])
         part = part.astype(BF16).astype(F32) * weight
         wide[:, 2 * n, :] = part[:, :LANES]
         wide[:, 2 * n + 1, :] = part[:, LANES:]
@@ -306,12 +250,11 @@
     hidden = gate_weight.shape[2]
     feats = down_weight.shape[2]
     one = width * hidden * 2
-    early = width // DEPTH * 5 // 7 * DEPTH
-    gate_hbm, up_hbm, down_hbm = in_hbm(gate_weight, up_weight, down_weight)
+    gate_w, up_w, down_w = gate_weight[0], up_weight[0], down_weight[0]
     (packed,) = call(
         pack_body,
         [shaped((groups, ROWS, SPAN), BF16)],
-        [ANY] * 4,
+        [ANY] * 7,
         [
             pltpu.VMEM((ROWS, SPAN), F32),
             pltpu.SMEM(expert_ids.shape, expert_ids.dtype),
@@ -320,73 +263,64 @@
             pltpu.VMEM(out_grad.shape, BF16),
             pltpu.SemaphoreType.DMA((4,)),
         ],
-    )(*in_hbm(expert_ids, route_probs, tokens, out_grad))
+        moved=12 * one,
+    )(*in_hbm(expert_ids, route_probs, tokens, out_grad, gate_w, up_w, down_w))
     own = lax.all_to_all(packed, ("chip", "local"), split_axis=0, concat_axis=0, tiled=True)
     other = swap(own, "core")
-    down_away, own_rows, own_grads, own_weight = call(
-        load_body,
-        [
-            pltpu.VMEM((hidden, feats), BF16),
+    own_rows, own_grads, own_weight = call(
+        unpack_body,
+        [
             shaped((groups, width), BF16),
             shaped((groups, feats), BF16),
             shaped((groups, LANES), F32),
         ],
-        [ANY, VMEM],
-        [pltpu.VMEM((groups, ROWS, SPAN), F32), pltpu.SemaphoreType.DMA((hidden // COLS,))],
-        moved=one,
-    )(down_hbm, own)
-    away, cot, weight, rows, down_own, gate_w = call(
+        [VMEM],
+        [pltpu.VMEM((groups, ROWS, SPAN), F32)],
+        moved=one // 4,
+    )(own)
+    away, cot, weight, rows = call(
         cot_body,
         [
             shaped((total, hidden), BF16),
             shaped((total, hidden), F32),
             shaped((total, LANES), F32),
             shaped((total, width), BF16),
-            pltpu.VMEM((hidden, feats), BF16),
-            pltpu.VMEM((early, hidden), BF16),
-        ],
-        [VMEM] * 5 + [ANY] * 2,
-        [
-            pltpu.VMEM((groups, ROWS, SPAN), F32),
-            pltpu.VMEM((total, feats), BF16),
-            pltpu.SemaphoreType.DMA((hidden // COLS + early // DEPTH,)),
-        ],
+        ],
+        [VMEM] * 5,
+        [pltpu.VMEM((groups, ROWS, SPAN), F32), pltpu.VMEM((total, feats), BF16)],
         products=total * one,
-        moved=2 * one,
-    )(other, own_rows, own_grads, own_weight, down_away, down_hbm, gate_hbm)
+        moved=one,
+    )(other, own_rows, own_grads, own_weight, down_w)
     cot_recv = swap(away, "local")
-    gate, up, act, gate_rest, up_w = call(
+    gate, up, act = call(
         forward_body,
         [
             shaped((total, hidden), F32),
             shaped((total, hidden), F32),
             shaped((total, hidden), BF16),
-            pltpu.VMEM((width - early, hidden), BF16),
-            pltpu.VMEM((width, hidden), BF16),
-        ],
-        [VMEM, VMEM, ANY, ANY],
-        [pltpu.SemaphoreType.DMA(((2 * width - early) // DEPTH,))],
+        ],
+        [VMEM] * 3,
         products=total * 2 * one,
-        moved=3 * one // 2,
-    )(rows, gate_w, gate_hbm, up_hbm)
+        moved=2 * one,
+    )(rows, gate_w, up_w)
     act_recv = swap(act, "local")
     in_mine, in_away = call(
         input_body,
         [shaped((groups, ROWS, COLS), BF16)] * 2,
-        [VMEM] * 9,
+        [VMEM] * 8,
         [pltpu.VMEM((total, ROWS, COLS), F32)],
         products=total * 2 * one,
         moved=2 * one,
-    )(cot, cot_recv, gate, up, act, weight, gate_w, gate_rest, up_w)
+    )(cot, cot_recv, gate, up, act, weight, gate_w, up_w)
     in_recv = swap(in_away, "core")
     routed_mine, routed_away = call(
         routed_body,
         [shaped((groups, ROWS, LANES), BF16)] * 2,
-        [VMEM] * 5 + [ANY],
+        [VMEM] * 4 + [ANY],
         [pltpu.VMEM((total, ROWS, LANES), F32)],
         products=total * one,
         moved=one,
-    )(act, act_recv, weight, down_own, down_away, in_mine)
+    )(act, act_recv, weight, down_w, in_mine)
     routed_recv = swap(routed_away, "core")
     summed = jnp.concatenate(
         [

time: 52.6 us -> 48.5 us (0.922)
  Pallas kernels: 18.7 us -> 13.3 us
  waiting for transfers between devices: 0.97 us -> 2.05 us
    pallas_call x1, Pallas kernels: 4.84 us -> 2.42 us  [fast_device(): call(cot_body, [shaped((total, hidden), BF16), shaped((total, hidden), F3...]
    pallas_call x4, Pallas kernels: 8.55 us -> 6.98 us  [the longest x1 4.2 us: fast_device(): call(input_body, [shaped((groups, ROWS, COLS), BF16)] * 2, [VMEM] * 8, [p...]
    pallas_call x1, Pallas kernels: 4.07 us -> 2.68 us  [fast_device(): call(forward_body, [shaped((total, hidden), F32), shaped((total, hidden),...]
    ppermute x5, waiting for transfers between devices: 0.97 us -> 2.05 us  [swap(): return lax.ppermute(x, axis, [(0, 1), (1, 0)])]
  transfers between devices with their start and end apart: 5 -> 5, of which waited for: 2 -> 3; matrix products, arithmetic and copies ran while one was open for 0% -> 0% of each run, Pallas kernels for 20% -> 15%
where the time goes in v6:
time: 48.5 us; the launch traced here: 48.2 us
  blocking collectives  29.4 us (61%)
  Pallas kernels  13.3 us (27%)
  starting transfers between devices  2.66 us (5%)
  waiting for transfers between devices  2.05 us (4%)
  between operations  0.77 us (2%)
    all_to_all x1, blocking collectives, fast_device(): lax.all_to_all(packed, ('chip', 'local'), split_axis=0, concat_axis=0, ti...  17 us
    all_to_all x1, blocking collectives, fast_device(): lax.all_to_all(summed, ('chip', 'local'), split_axis=0, concat_axis=0, ti...  12.3 us
    pallas_call x1, Pallas kernels, fast_device(): call(input_body, [shaped((groups, ROWS, COLS), BF16)] * 2, [VMEM] * 8, [p...  4.2 us
    pallas_call x1, Pallas kernels, fast_device(): call(forward_body, [shaped((total, hidden), F32), shaped((total, hidden),...  2.68 us
    ppermute x5, starting transfers between devices, swap(): return lax.ppermute(x, axis, [(0, 1), (1, 0)])  2.66 us
    pallas_call x1, Pallas kernels, fast_device(): call(cot_body, [shaped((total, hidden), BF16), shaped((total, hidden), F3...  2.42 us
    ppermute x5, waiting for transfers between devices, swap(): return lax.ppermute(x, axis, [(0, 1), (1, 0)])  2.05 us
    pallas_call x1, Pallas kernels, fast_device(): call(routed_body, [shaped((groups, ROWS, LANES), BF16)] * 2, [VMEM] * 4 +...  1.44 us
  transfers between devices with their start and end apart: 5, of which 3 were waited for; matrix products, arithmetic and copies ran while one was open for 0% of the time, Pallas kernels for 15%

profile of v6, /device:TPU:0, one launch (start us, length us, event | category | flops | bytes accessed | tf_op | source)
XLA Modules:
  0.0 48.2 jit_solution(9428753633157717615)
XLA Ops:
  0.6 0.0 slice-start
  0.6 0.0 slice-start.2
  0.7 0.0 slice-start.1
  0.7 0.0 slice-start.3
  0.7 1.0 %shard_map.94 = bf16[16,16,384]{2,1,0:T(8,128)(2,1)S(1)} custom-call(s32[1,1,8]{2,1,0:T(1,128)} %ids_ref.1, f32[1,1,8]{2,1,0:T(1,128)} %probs_hbm.1, bf16[1,1,3584]{2,1,0:T(2,128)(2,1)} %tok_hbm.1, bf16[1,1,3584]{2,1,0:T(2,128)(2,1)} %grad_hbm.1, bf16[3584,1024]{1,0:T(8,128)(2,1)} %bitcast.3, bf16[3584,1024]{1,0:T(8,128)(2,1)} %bitcast.8, ...), custom_call_target="tpu_custom_call" | custom-call | bytes 88080384 | tf_op jit(solution)/shard_map/pallas_call | solution.py:254
  1.7 17.0 %all_to_all.10.in_ref = bf16[16,16,384]{2,1,0:T(8,128)(2,1)S(1)} all-to-all(bf16[16,16,384]{2,1,0:T(8,128)(2,1)S(1)} %shard_map.94), channel_id=1, replica_groups=mesh['chip'=8,'core'=2,'local'=2] {'chip','local'}, dimensions={0} | all-to-all | bytes 393216 | tf_op jit(solution)/shard_map/all_to_all | solution.py:268
  18.7 0.0 collective-permute-start
  18.7 0.4 shard_map.95
  19.1 1.1 %collective-permute-done.other_ref = bf16[16,16,384]{2,1,0:T(8,128)(2,1)S(1)} collective-permute-done((bf16[16,16,384]{2,1,0:T(8,128)(2,1)S(1)}, bf16[16,16,384]{2,1,0:T(8,128)(2,1)S(1)}, u32[]{:S(2)}, u32[]{:S(2)}) %collective-permute-start) | collective-permute-done | bytes 196640 | tf_op jit(solution)/shard_map/ppermute | solution.py:243
  20.1 2.4 %shard_map.96 = (bf16[32,1024]{1,0:T(8,128)(2,1)S(1)}, f32[32,1024]{1,0:T(8,128)S(1)}, f32[32,128]{1,0:T(8,128)S(1)}, bf16[32,3584]{1,0:T(8,128)(2,1)S(1)}) custom-call(bf16[16,16,384]{2,1,0:T(8,128)(2,1)S(1)} %collective-permute-done.other_ref, bf16[16,3584]{1,0:T(8,128)(2,1)S(1)} %get-tuple-element.17.rows_in, ...), custom_call_target="tpu_custom_call" | custom-call | flops 234881024 | bytes 7340032 | tf_op jit(solution)/shard_map/pallas_call | solution.py:281
  22.6 0.9 %collective-permute-start.1 = (bf16[32,1024]{1,0:T(8,128)(2,1)S(1)}, bf16[32,1024]{1,0:T(8,128)(2,1)S(1)}, u32[]{:S(2)}, u32[]{:S(2)}) collective-permute-start(bf16[32,1024]{1,0:T(8,128)(2,1)S(1)} %get-tuple-element.21), channel_id=1, source_target_pairs={{0,1},{1,0},{2,3},{3,2},{4,5},{5,4},{6,7},{7,6},{8,9},{9,8},{10,11... | collective-permute-start | bytes 196616 | tf_op jit(solution)/shard_map/ppermute | solution.py:243
  23.5 2.7 %shard_map.97 = (f32[32,1024]{1,0:T(8,128)S(1)}, f32[32,1024]{1,0:T(8,128)S(1)}, bf16[32,1024]{1,0:T(8,128)(2,1)S(1)}) custom-call(bf16[32,3584]{1,0:T(8,128)(2,1)S(1)} %get-tuple-element.22.rows_ref, bf16[3584,1024]{1,0:T(8,128)(2,1)S(1)} %bitcast.6, bf16[3584,1024]{1,0:T(8,128)(2,1)S(1)} %bitcast.11), custom_call_target="tpu_custom_call" | custom-call | flops 469762048 | bytes 14680064 | tf_op jit(solution)/shard_map/pallas_call | solution.py:295
  26.2 1.1 %collective-permute-start.3 = (bf16[32,1024]{1,0:T(8,128)(2,1)S(1)}, bf16[32,1024]{1,0:T(8,128)(2,1)S(1)}, u32[]{:S(2)}, u32[]{:S(2)}) collective-permute-start(bf16[32,1024]{1,0:T(8,128)(2,1)S(1)} %get-tuple-element.25.act_ref), channel_id=1, source_target_pairs={{0,1},{1,0},{2,3},{3,2},{4,5},{5,4},{6,7},{7,6},{8,9},{9,8},{10,11... | collective-permute-start | bytes 196616 | tf_op jit(solution)/shard_map/ppermute | solution.py:243
  27.4 0.0 collective-permute-done.1.recv_ref
  27.4 4.2 %shard_map.98 = (bf16[16,16,256]{2,1,0:T(8,128)(2,1)S(1)}, bf16[16,16,256]{2,1,0:T(8,128)(2,1)S(1)}) custom-call(f32[32,1024]{1,0:T(8,128)S(1)} %get-tuple-element.20.cot_ref, bf16[32,1024]{1,0:T(8,128)(2,1)S(1)} %collective-permute-done.1.recv_ref, f32[32,1024]{1,0:T(8,128)S(1)} %get-tuple-element.23.gate_in, f32[32,1024]{1,0:T(8,128)S(1)} %get-tuple-element.24.up_in, ...), custom_call_target="tpu_custom_call" | custom-call | flops 469762048 | bytes 14680064 | tf_op jit(solution)/shard_map/pallas_call | solution.py:307
  31.6 0.0 copy-start.1
  31.6 0.0 collective-permute-done.3.recv_ref
  31.6 1.4 %shard_map.99 = (bf16[16,16,128]{2,1,0:T(8,128)(2,1)S(1)}, bf16[16,16,128]{2,1,0:T(8,128)(2,1)S(1)}) custom-call(bf16[32,1024]{1,0:T(8,128)(2,1)S(1)} %get-tuple-element.25.act_ref, bf16[32,1024]{1,0:T(8,128)(2,1)S(1)} %collective-permute-done.3.recv_ref, f32[32,128]{1,0:T(8,128)S(1)} %get-tuple-element.26.weight_in, bf16[2048,1792]{1,0:T(8,128)(2,1)S(1)} %bitcast.15, ...), custom_call_target="tpu_custom_call" | custom-call | flops 234881024 | bytes 7340032 | tf_op jit(solution)/shard_map/pallas_call | solution.py:316
  33.1 0.1 collective-permute-start.4
  33.1 0.5 %collective-permute-start.2 = (bf16[16,16,256]{2,1,0:T(8,128)(2,1)S(1)}, bf16[16,16,256]{2,1,0:T(8,128)(2,1)S(1)}, u32[]{:S(2)}, u32[]{:S(2)}) collective-permute-start(bf16[16,16,256]{2,1,0:T(8,128)(2,1)S(1)} %get-tuple-element.28), channel_id=1, source_target_pairs={{0,2},{2,0},{1,3},{3,1},{4,6},{6,4},{5,7},{7,5},{8,10},{10,8},{9,1... | collective-permute-start | bytes 393224 | tf_op jit(solution)/shard_map/ppermute | solution.py:243
  33.6 0.7 %collective-permute-done.4 = bf16[16,16,128]{2,1,0:T(8,128)(2,1)S(1)} collective-permute-done((bf16[16,16,128]{2,1,0:T(8,128)(2,1)S(1)}, bf16[16,16,128]{2,1,0:T(8,128)(2,1)S(1)}, u32[]{:S(2)}, u32[]{:S(2)}) %collective-permute-start.4) | collective-permute-done | bytes 65568 | tf_op jit(solution)/shard_map/ppermute | solution.py:243
  34.4 0.2 collective-permute-done.2
  34.7 12.3 %all_to_all.11.in_ref = bf16[16,16,384]{2,1,0:T(8,128)(2,1)S(1)} all-to-all(bf16[16,16,384]{2,1,0:T(8,128)(2,1)S(1)} %pad_maximum_fusion), channel_id=1, replica_groups=mesh['chip'=8,'core'=2,'local'=2] {'chip','local'}, dimensions={0} | all-to-all | bytes 393216 | tf_op jit(solution)/shard_map/all_to_all | solution.py:332
  47.0 1.2 %shard_map.100 = (bf16[1,1,3584]{2,1,0:T(2,128)(2,1)}, bf16[1,1,3584]{2,1,0:T(2,128)(2,1)}, f32[1,1,8]{2,1,0:T(1,128)}) custom-call(bf16[16,16,384]{2,1,0:T(8,128)(2,1)S(1)} %all_to_all.11.in_ref, s32[1,1,8]{2,1,0:T(1,128)S(1)} %copy-done.1), custom_call_target="tpu_custom_call" | custom-call | tf_op jit(solution)/shard_map/pallas_call | solution.py:333
  (12 shorter events, 0.1 us)
Async XLA Ops:
  0.6 22.9 %slice-start = ((s8[7340032]{0:T(1024)(128)(4,1)}), s8[4194304]{0:T(1024)(128)(4,1)S(1)}, s32[]{:S(2)}) async-start(s8[7340032]{0:T(1024)(128)(4,1)} %bitcast.4), calls=%async_computation.2 | async-start | bytes 8388608
  0.6 22.9 %slice-start.2 = ((s8[7340032]{0:T(1024)(128)(4,1)}), s8[4194304]{0:T(1024)(128)(4,1)S(1)}, s32[]{:S(2)}) async-start(s8[7340032]{0:T(1024)(128)(4,1)} %bitcast.9), calls=%async_computation.4 | async-start | bytes 8388608
  0.7 19.5 %copy-start = (bf16[1,2048,1792]{2,1,0:T(8,128)(2,1)S(1)}, bf16[1,2048,1792]{2,1,0:T(8,128)(2,1)}, u32[]{:S(2)}) copy-start(bf16[1,2048,1792]{2,1,0:T(8,128)(2,1)} %param.12) | copy-start | bytes 22020100
  0.7 22.9 %slice-start.1 = ((s8[7340032]{0:T(1024)(128)(4,1)}), s8[3145728]{0:T(1024)(128)(4,1)S(1)}, s32[]{:S(2)}) async-start(s8[7340032]{0:T(1024)(128)(4,1)} %bitcast.4), calls=%async_computation.3 | async-start | bytes 6291456
  0.7 22.8 %slice-start.3 = ((s8[7340032]{0:T(1024)(128)(4,1)}), s8[3145728]{0:T(1024)(128)(4,1)S(1)}, s32[]{:S(2)}) async-start(s8[7340032]{0:T(1024)(128)(4,1)} %bitcast.9), calls=%async_computation.5 | async-start | bytes 6291456
  18.7 1.4 %collective-permute-start = (bf16[16,16,384]{2,1,0:T(8,128)(2,1)S(1)}, bf16[16,16,384]{2,1,0:T(8,128)(2,1)S(1)}, u32[]{:S(2)}, u32[]{:S(2)}) collective-permute-start(bf16[16,16,384]{2,1,0:T(8,128)(2,1)S(1)} %all_to_all.10.in_ref), channel_id=1, source_target_pairs={{0,2},{2,0},{1,3},{3,1},{4,6},{6,4},{5,7},{7,5},{8,10},{10,8},{9,1... | collective-permute-start | bytes 589832 | tf_op jit(solution)/shard_map/ppermute | solution.py:243
  22.6 4.8 %collective-permute-start.1 = (bf16[32,1024]{1,0:T(8,128)(2,1)S(1)}, bf16[32,1024]{1,0:T(8,128)(2,1)S(1)}, u32[]{:S(2)}, u32[]{:S(2)}) collective-permute-start(bf16[32,1024]{1,0:T(8,128)(2,1)S(1)} %get-tuple-element.21), channel_id=1, source_target_pairs={{0,1},{1,0},{2,3},{3,2},{4,5},{5,4},{6,7},{7,6},{8,9},{9,8},{10,11... | collective-permute-start | bytes 196616 | tf_op jit(solution)/shard_map/ppermute | solution.py:243
  26.2 5.4 %collective-permute-start.3 = (bf16[32,1024]{1,0:T(8,128)(2,1)S(1)}, bf16[32,1024]{1,0:T(8,128)(2,1)S(1)}, u32[]{:S(2)}, u32[]{:S(2)}) collective-permute-start(bf16[32,1024]{1,0:T(8,128)(2,1)S(1)} %get-tuple-element.25.act_ref), channel_id=1, source_target_pairs={{0,1},{1,0},{2,3},{3,2},{4,5},{5,4},{6,7},{7,6},{8,9},{9,8},{10,11... | collective-permute-start | bytes 196616 | tf_op jit(solution)/shard_map/ppermute | solution.py:243
  31.6 15.4 %copy-start.1 = (s32[1,1,8]{2,1,0:T(1,128)S(1)}, s32[1,1,8]{2,1,0:T(1,128)}, u32[]{:S(2)}) copy-start(s32[1,1,8]{2,1,0:T(1,128)} %ids_ref.1) | copy-start | bytes 100
  33.1 1.3 %collective-permute-start.4 = (bf16[16,16,128]{2,1,0:T(8,128)(2,1)S(1)}, bf16[16,16,128]{2,1,0:T(8,128)(2,1)S(1)}, u32[]{:S(2)}, u32[]{:S(2)}) collective-permute-start(bf16[16,16,128]{2,1,0:T(8,128)(2,1)S(1)} %get-tuple-element.30), channel_id=1, source_target_pairs={{0,2},{2,0},{1,3},{3,1},{4,6},{6,4},{5,7},{7,5},{8,10},{10,8},{9,1... | collective-permute-start | bytes 196616 | tf_op jit(solution)/shard_map/ppermute | solution.py:243
  33.1 1.5 %collective-permute-start.2 = (bf16[16,16,256]{2,1,0:T(8,128)(2,1)S(1)}, bf16[16,16,256]{2,1,0:T(8,128)(2,1)S(1)}, u32[]{:S(2)}, u32[]{:S(2)}) collective-permute-start(bf16[16,16,256]{2,1,0:T(8,128)(2,1)S(1)} %get-tuple-element.28), channel_id=1, source_target_pairs={{0,2},{2,0},{1,3},{3,1},{4,6},{6,4},{5,7},{7,5},{8,10},{10,8},{9,1... | collective-permute-start | bytes 393224 | tf_op jit(solution)/shard_map/ppermute | solution.py:243

commit v7 on v6

--- a/solution.py
+++ b/solution.py
@@ -18,7 +18,6 @@
 NT = (((1,), (1,)), ((), ()))
 VMEM = pl.BlockSpec(memory_space=pltpu.VMEM)
 ANY = pl.BlockSpec(memory_space=pl.ANY)
-SMEM = pl.BlockSpec(memory_space=pltpu.SMEM)
 
 
 def call(body, outs, ins, scratch=(), products=0, moved=0):
@@ -57,7 +56,8 @@
 
 
 def pack_body(
-    ids_hbm, probs_hbm, tok_hbm, grad_hbm, gate_hbm, up_hbm, down_hbm, out_ref, wide, ids_ref, probs_ref, tok_ref, grad_ref, sems
+    ids_hbm, probs_hbm, tok_hbm, grad_hbm, gate_hbm, up_hbm, down_hbm, out_ref, named_ref,
+    wide, ids_ref, probs_ref, tok_ref, grad_ref, sems
 ):
     pairs = ((ids_hbm, ids_ref), (probs_hbm, probs_ref), (tok_hbm, tok_ref), (grad_hbm, grad_ref))
     copies = [pltpu.make_async_copy(a, b, sems.at[i]) for i, (a, b) in enumerate(pairs)]
@@ -69,7 +69,9 @@
     for copy in copies:
         copy.wait()
     for k in range(ids_ref.shape[2]):
-        weight = jnp.where(lane == ids_ref[0, 0, k], probs_ref[0, 0, k], weight)
+        named = lane == ids_ref[0, 0, k]
+        weight = jnp.where(named, probs_ref[0, 0, k], weight)
+        named_ref[k : k + 1, :] = named.astype(F32)
     width = tok_ref.shape[2]
     meta = width // COLS
     half = width // 2
@@ -178,7 +180,11 @@
     steps = width // COLS
     for n in range(steps):
         at = slice(n * COLS, (n + 1) * COLS)
-        wide[:, n, :] = (dot(gate_ref[at, :], gate_turned) + dot(up_ref[at, :], up_turned)).T
+        if n % 3 == 0:
+            part = (dot(gate_ref[at, :], gate_turned) + dot(up_ref[at, :], up_turned)).T
+        else:
+            part = dot_nt(gate_grad, gate_ref[at, :]) + dot_nt(up_grad, up_ref[at, :])
+        wide[:, n, :] = part
     lane = lax.broadcasted_iota(jnp.int32, (total, LANES), 1)
     high, low = high_low(jnp.where(lane == expert, prob, 0.0))
     wide[:, steps, 0:LANES] = high
@@ -189,7 +195,9 @@
     other_ref[...] = wide[count:].astype(BF16)
 
 
-def routed_body(act_ref, recv_ref, weight_in, down_ref, after_ref, mine_ref, other_ref, wide):
+def routed_body(
+    act_ref, recv_ref, weight_in, down_ref, in_mine, in_away, mine_ref, other_ref, wide
+):
     total, hidden = act_ref.shape
     count = total // 2
     feats = down_ref.shape[1]
@@ -206,11 +214,12 @@
         wide[:, 2 * n + 1, :] = part[:, LANES:]
     for n in range(feats // LANES, ROWS):
         wide[:, n, :] = jnp.zeros((total, LANES), F32)
-    mine_ref[...] = wide[:count].astype(BF16)
-    other_ref[...] = wide[count:].astype(BF16)
-
-
-def final_body(in_ref, ids_ref, comb_ref, grad_ref, prob_ref, wide):
+    for ref, part, at in ((mine_ref, in_mine, 0), (other_ref, in_away, count)):
+        ref[:, :, 0:COLS] = part[...]
+        ref[:, :, COLS:SPAN] = wide[at : at + count].astype(BF16)
+
+
+def final_body(in_ref, named_ref, comb_ref, grad_ref, prob_ref, wide):
     groups = in_ref.shape[0]
     width = comb_ref.shape[2]
     half = width // 2
@@ -220,21 +229,18 @@
             total = total + in_ref[i].astype(F32)
         wide[j] = total
     meta = width // COLS
-    for c in range(meta):
-        grad_ref[0, :, c * COLS : (c + 1) * COLS] = (
-            wide[0, c : c + 1, 0:COLS] + wide[1, c : c + 1, 0:COLS]
-        ).astype(BF16)
-    for j in range(2):
-        for c in range(half // LANES):
-            at = j * half + c * LANES
-            comb_ref[0, :, at : at + LANES] = wide[j, c : c + 1, COLS:SPAN].astype(BF16)
+    total = wide[0] + wide[1]
+    grad_ref[0] = jnp.concatenate([total[c : c + 1, 0:COLS] for c in range(meta)], axis=1).astype(BF16)
+    comb_ref[0] = jnp.concatenate(
+        [wide[j, c : c + 1, COLS:SPAN] for j in range(2) for c in range(half // LANES)], axis=1
+    ).astype(BF16)
     prob = wide[0, meta : meta + 1, 0:COLS] + wide[1, meta : meta + 1, 0:COLS]
     prob = prob[:, 0:LANES] + prob[:, LANES:COLS]
     lane = lax.broadcasted_iota(jnp.int32, (1, LANES), 1)
-    top = ids_ref.shape[2]
+    top = named_ref.shape[0]
     out = jnp.zeros((1, LANES), F32)
     for k in range(top):
-        value = jnp.sum(jnp.where(lane == ids_ref[0, 0, k], prob, 0.0), axis=1, keepdims=True)
+        value = jnp.sum(named_ref[k : k + 1, :] * prob, axis=1, keepdims=True)
         out = jnp.where(lane == k, value, out)
     prob_ref[0] = out[:, :top]
 
@@ -251,9 +257,9 @@
     feats = down_weight.shape[2]
     one = width * hidden * 2
     gate_w, up_w, down_w = gate_weight[0], up_weight[0], down_weight[0]
-    (packed,) = call(
+    packed, named = call(
         pack_body,
-        [shaped((groups, ROWS, SPAN), BF16)],
+        [shaped((groups, ROWS, SPAN), BF16), shaped((expert_ids.shape[2], LANES), F32)],
         [ANY] * 7,
         [
             pltpu.VMEM((ROWS, SPAN), F32),
@@ -312,23 +318,15 @@
         products=total * 2 * one,
         moved=2 * one,
     )(cot, cot_recv, gate, up, act, weight, gate_w, up_w)
-    in_recv = swap(in_away, "core")
-    routed_mine, routed_away = call(
+    mine, away = call(
         routed_body,
-        [shaped((groups, ROWS, LANES), BF16)] * 2,
-        [VMEM] * 4 + [ANY],
+        [shaped((groups, ROWS, SPAN), BF16)] * 2,
+        [VMEM] * 6,
         [pltpu.VMEM((total, ROWS, LANES), F32)],
         products=total * one,
         moved=one,
-    )(act, act_recv, weight, down_w, in_mine)
-    routed_recv = swap(routed_away, "core")
-    summed = jnp.concatenate(
-        [
-            (in_mine.astype(F32) + in_recv.astype(F32)).astype(BF16),
-            (routed_mine.astype(F32) + routed_recv.astype(F32)).astype(BF16),
-        ],
-        axis=2,
-    )
+    )(act, act_recv, weight, down_w, in_mine, in_away)
+    summed = (mine.astype(F32) + swap(away, "core").astype(F32)).astype(BF16)
     back = lax.all_to_all(summed, ("chip", "local"), split_axis=0, concat_axis=0, tiled=True)
     return call(
         final_body,
@@ -337,9 +335,9 @@
             shaped((1, 1, width), BF16),
             shaped(expert_ids.shape, F32),
         ],
-        [VMEM, SMEM],
+        [VMEM, VMEM],
         [pltpu.VMEM((2, ROWS, SPAN), F32)],
-    )(back, expert_ids)
+    )(back, named)
 
 
 def selector(flags, capacity):

time: 48.5 us -> 47.7 us (0.984)
  Pallas kernels: 13.3 us -> 12.8 us
  starting transfers between devices: 2.66 us -> 2.17 us
    pallas_call x1, Pallas kernels: 1.21 us -> 0.67 us  [fast_device(): call(final_body, [shaped((1, 1, width), BF16), shaped((1, 1, width), BF16...]
    ppermute x5 -> x4, starting transfers between devices: 2.66 us -> 2.17 us  [swap(): return lax.ppermute(x, axis, [(0, 1), (1, 0)])]
    ppermute x5 -> x4, waiting for transfers between devices: 2.05 us -> 2.51 us  [swap(): return lax.ppermute(x, axis, [(0, 1), (1, 0)])]
  transfers between devices with their start and end apart: 5 -> 4, of which waited for: 3 -> 2; matrix products, arithmetic and copies ran while one was open for 0% -> 0% of each run, Pallas kernels for 15% -> 15%
where the time goes in v7:
time: 47.7 us; the launch traced here: 47.4 us
  blocking collectives  29.1 us (61%)
  Pallas kernels  12.8 us (27%)
  waiting for transfers between devices  2.51 us (5%)
  starting transfers between devices  2.17 us (5%)
  between operations  0.75 us (2%)
    all_to_all x1, blocking collectives, fast_device(): lax.all_to_all(packed, ('chip', 'local'), split_axis=0, concat_axis=0, ti...  17 us
    all_to_all x1, blocking collectives, fast_device(): lax.all_to_all(summed, ('chip', 'local'), split_axis=0, concat_axis=0, ti...  12.1 us
    pallas_call x1, Pallas kernels, fast_device(): call(input_body, [shaped((groups, ROWS, COLS), BF16)] * 2, [VMEM] * 8, [p...  4.21 us
    pallas_call x1, Pallas kernels, fast_device(): call(forward_body, [shaped((total, hidden), F32), shaped((total, hidden),...  2.68 us
    ppermute x4, waiting for transfers between devices, swap(): return lax.ppermute(x, axis, [(0, 1), (1, 0)])  2.51 us
    pallas_call x1, Pallas kernels, fast_device(): call(cot_body, [shaped((total, hidden), BF16), shaped((total, hidden), F3...  2.42 us
    ppermute x4, starting transfers between devices, swap(): return lax.ppermute(x, axis, [(0, 1), (1, 0)])  2.17 us
    pallas_call x1, Pallas kernels, fast_device(): call(routed_body, [shaped((groups, ROWS, SPAN), BF16)] * 2, [VMEM] * 6, [...  1.45 us
  transfers between devices with their start and end apart: 4, of which 2 were waited for; matrix products, arithmetic and copies ran while one was open for 0% of the time, Pallas kernels for 15%

profile of v7, /device:TPU:0, one launch (start us, length us, event | category | flops | bytes accessed | tf_op | source)
XLA Modules:
  0.0 47.4 jit_solution(6189536580330445344)
XLA Ops:
  0.6 0.0 slice-start
  0.6 0.0 slice-start.2
  0.7 0.0 slice-start.1
  0.7 0.0 slice-start.3
  0.7 1.0 %shard_map.94 = (bf16[16,16,384]{2,1,0:T(8,128)(2,1)S(1)}, f32[8,128]{1,0:T(8,128)S(1)}) custom-call(s32[1,1,8]{2,1,0:T(1,128)} %ids_hbm.1, f32[1,1,8]{2,1,0:T(1,128)} %probs_hbm.1, bf16[1,1,3584]{2,1,0:T(2,128)(2,1)} %tok_hbm.1, bf16[1,1,3584]{2,1,0:T(2,128)(2,1)} %grad_hbm.1, bf16[3584,1024]{1,0:T(8,128)(2,1)} %bitcast.3, bf16[3584,1024]{1,0:T(8,128)(2,1)} %bitcast.8, ...), custom_call_target="tpu_custom_call" | custom-call | bytes 88080384 | tf_op jit(solution)/shard_map/pallas_call | solution.py:260
  1.7 17.0 %all_to_all.10.in_ref = bf16[16,16,384]{2,1,0:T(8,128)(2,1)S(1)} all-to-all(bf16[16,16,384]{2,1,0:T(8,128)(2,1)S(1)} %get-tuple-element.19), channel_id=1, replica_groups=mesh['chip'=8,'core'=2,'local'=2] {'chip','local'}, dimensions={0} | all-to-all | bytes 393216 | tf_op jit(solution)/shard_map/all_to_all | solution.py:274
  18.7 0.0 collective-permute-start
  18.7 0.4 shard_map.95
  19.0 1.1 %collective-permute-done.other_ref = bf16[16,16,384]{2,1,0:T(8,128)(2,1)S(1)} collective-permute-done((bf16[16,16,384]{2,1,0:T(8,128)(2,1)S(1)}, bf16[16,16,384]{2,1,0:T(8,128)(2,1)S(1)}, u32[]{:S(2)}, u32[]{:S(2)}) %collective-permute-start) | collective-permute-done | bytes 196640 | tf_op jit(solution)/shard_map/ppermute | solution.py:249
  20.1 0.0 copy-done
  20.1 2.4 %shard_map.96 = (bf16[32,1024]{1,0:T(8,128)(2,1)S(1)}, f32[32,1024]{1,0:T(8,128)S(1)}, f32[32,128]{1,0:T(8,128)S(1)}, bf16[32,3584]{1,0:T(8,128)(2,1)S(1)}) custom-call(bf16[16,16,384]{2,1,0:T(8,128)(2,1)S(1)} %collective-permute-done.other_ref, bf16[16,3584]{1,0:T(8,128)(2,1)S(1)} %get-tuple-element.20.rows_in, ...), custom_call_target="tpu_custom_call" | custom-call | flops 234881024 | bytes 7340032 | tf_op jit(solution)/shard_map/pallas_call | solution.py:287
  22.6 0.9 %collective-permute-start.2 = (bf16[32,1024]{1,0:T(8,128)(2,1)S(1)}, bf16[32,1024]{1,0:T(8,128)(2,1)S(1)}, u32[]{:S(2)}, u32[]{:S(2)}) collective-permute-start(bf16[32,1024]{1,0:T(8,128)(2,1)S(1)} %get-tuple-element.27), channel_id=1, source_target_pairs={{0,1},{1,0},{2,3},{3,2},{4,5},{5,4},{6,7},{7,6},{8,9},{9,8},{10,11... | collective-permute-start | bytes 196616 | tf_op jit(solution)/shard_map/ppermute | solution.py:249
  23.5 0.0 slice-done.1
  23.5 2.7 %shard_map.97 = (f32[32,1024]{1,0:T(8,128)S(1)}, f32[32,1024]{1,0:T(8,128)S(1)}, bf16[32,1024]{1,0:T(8,128)(2,1)S(1)}) custom-call(bf16[32,3584]{1,0:T(8,128)(2,1)S(1)} %get-tuple-element.23.rows_ref, bf16[3584,1024]{1,0:T(8,128)(2,1)S(1)} %bitcast.6, bf16[3584,1024]{1,0:T(8,128)(2,1)S(1)} %bitcast.11), custom_call_target="tpu_custom_call" | custom-call | flops 469762048 | bytes 14680064 | tf_op jit(solution)/shard_map/pallas_call | solution.py:301
  26.2 1.1 %collective-permute-start.1 = (bf16[32,1024]{1,0:T(8,128)(2,1)S(1)}, bf16[32,1024]{1,0:T(8,128)(2,1)S(1)}, u32[]{:S(2)}, u32[]{:S(2)}) collective-permute-start(bf16[32,1024]{1,0:T(8,128)(2,1)S(1)} %get-tuple-element.24.act_ref), channel_id=1, source_target_pairs={{0,1},{1,0},{2,3},{3,2},{4,5},{5,4},{6,7},{7,6},{8,9},{9,8},{10,11... | collective-permute-start | bytes 196616 | tf_op jit(solution)/shard_map/ppermute | solution.py:249
  27.4 0.0 collective-permute-done.2.recv_ref
  27.4 4.2 %shard_map.98 = (bf16[16,16,256]{2,1,0:T(8,128)(2,1)S(1)}, bf16[16,16,256]{2,1,0:T(8,128)(2,1)S(1)}) custom-call(f32[32,1024]{1,0:T(8,128)S(1)} %get-tuple-element.26.cot_ref, bf16[32,1024]{1,0:T(8,128)(2,1)S(1)} %collective-permute-done.2.recv_ref, f32[32,1024]{1,0:T(8,128)S(1)} %get-tuple-element.28.gate_in, f32[32,1024]{1,0:T(8,128)S(1)} %get-tuple-element.29.up_in, ...), custom_call_target="tpu_custom_call" | custom-call | flops 469762048 | bytes 14680064 | tf_op jit(solution)/shard_map/pallas_call | solution.py:313
  31.6 0.0 collective-permute-done.1.recv_ref
  31.6 1.5 %shard_map.99 = (bf16[16,16,384]{2,1,0:T(8,128)(2,1)S(1)}, bf16[16,16,384]{2,1,0:T(8,128)(2,1)S(1)}) custom-call(bf16[32,1024]{1,0:T(8,128)(2,1)S(1)} %get-tuple-element.24.act_ref, bf16[32,1024]{1,0:T(8,128)(2,1)S(1)} %collective-permute-done.1.recv_ref, f32[32,128]{1,0:T(8,128)S(1)} %get-tuple-element.25.weight_in, bf16[2048,1792]{1,0:T(8,128)(2,1)S(1)} %bitcast.15, ...), custom_call_target="tpu_custom_call" | custom-call | flops 234881024 | bytes 7340032 | tf_op jit(solution)/shard_map/pallas_call | solution.py:321
  33.1 0.1 collective-permute-start.3
  33.1 1.4 %collective-permute-done.3 = bf16[16,16,384]{2,1,0:T(8,128)(2,1)S(1)} collective-permute-done((bf16[16,16,384]{2,1,0:T(8,128)(2,1)S(1)}, bf16[16,16,384]{2,1,0:T(8,128)(2,1)S(1)}, u32[]{:S(2)}, u32[]{:S(2)}) %collective-permute-start.3) | collective-permute-done | bytes 196640 | tf_op jit(solution)/shard_map/ppermute | solution.py:249
  34.6 0.1 add_convert_fusion
  34.6 12.1 %all_to_all.11.in_ref = bf16[16,16,384]{2,1,0:T(8,128)(2,1)S(1)} all-to-all(bf16[16,16,384]{2,1,0:T(8,128)(2,1)S(1)} %add_convert_fusion), channel_id=1, replica_groups=mesh['chip'=8,'core'=2,'local'=2] {'chip','local'}, dimensions={0} | all-to-all | bytes 393216 | tf_op jit(solution)/shard_map/all_to_all | solution.py:330
  46.7 0.7 %shard_map.100 = (bf16[1,1,3584]{2,1,0:T(2,128)(2,1)}, bf16[1,1,3584]{2,1,0:T(2,128)(2,1)}, f32[1,1,8]{2,1,0:T(1,128)}) custom-call(bf16[16,16,384]{2,1,0:T(8,128)(2,1)S(1)} %all_to_all.11.in_ref, f32[8,128]{1,0:T(8,128)S(1)} %get-tuple-element.34.named_ref), custom_call_target="tpu_custom_call" | custom-call | tf_op jit(solution)/shard_map/pallas_call | solution.py:331
  (6 shorter events, 0.0 us)
Async XLA Ops:
  0.6 22.9 %slice-start = ((s8[7340032]{0:T(1024)(128)(4,1)}), s8[4194304]{0:T(1024)(128)(4,1)S(1)}, s32[]{:S(2)}) async-start(s8[7340032]{0:T(1024)(128)(4,1)} %bitcast.4), calls=%async_computation.2 | async-start | bytes 8388608
  0.6 22.9 %slice-start.2 = ((s8[7340032]{0:T(1024)(128)(4,1)}), s8[4194304]{0:T(1024)(128)(4,1)S(1)}, s32[]{:S(2)}) async-start(s8[7340032]{0:T(1024)(128)(4,1)} %bitcast.9), calls=%async_computation.4 | async-start | bytes 8388608
  0.7 19.5 %copy-start = (bf16[1,2048,1792]{2,1,0:T(8,128)(2,1)S(1)}, bf16[1,2048,1792]{2,1,0:T(8,128)(2,1)}, u32[]{:S(2)}) copy-start(bf16[1,2048,1792]{2,1,0:T(8,128)(2,1)} %param.12) | copy-start | bytes 22020100
  0.7 22.8 %slice-start.1 = ((s8[7340032]{0:T(1024)(128)(4,1)}), s8[3145728]{0:T(1024)(128)(4,1)S(1)}, s32[]{:S(2)}) async-start(s8[7340032]{0:T(1024)(128)(4,1)} %bitcast.4), calls=%async_computation.3 | async-start | bytes 6291456
  0.7 22.8 %slice-start.3 = ((s8[7340032]{0:T(1024)(128)(4,1)}), s8[3145728]{0:T(1024)(128)(4,1)S(1)}, s32[]{:S(2)}) async-start(s8[7340032]{0:T(1024)(128)(4,1)} %bitcast.9), calls=%async_computation.5 | async-start | bytes 6291456
  18.7 1.4 %collective-permute-start = (bf16[16,16,384]{2,1,0:T(8,128)(2,1)S(1)}, bf16[16,16,384]{2,1,0:T(8,128)(2,1)S(1)}, u32[]{:S(2)}, u32[]{:S(2)}) collective-permute-start(bf16[16,16,384]{2,1,0:T(8,128)(2,1)S(1)} %all_to_all.10.in_ref), channel_id=1, source_target_pairs={{0,2},{2,0},{1,3},{3,1},{4,6},{6,4},{5,7},{7,5},{8,10},{10,8},{9,1... | collective-permute-start | bytes 589832 | tf_op jit(solution)/shard_map/ppermute | solution.py:249
  22.6 4.8 %collective-permute-start.2 = (bf16[32,1024]{1,0:T(8,128)(2,1)S(1)}, bf16[32,1024]{1,0:T(8,128)(2,1)S(1)}, u32[]{:S(2)}, u32[]{:S(2)}) collective-permute-start(bf16[32,1024]{1,0:T(8,128)(2,1)S(1)} %get-tuple-element.27), channel_id=1, source_target_pairs={{0,1},{1,0},{2,3},{3,2},{4,5},{5,4},{6,7},{7,6},{8,9},{9,8},{10,11... | collective-permute-start | bytes 196616 | tf_op jit(solution)/shard_map/ppermute | solution.py:249
  26.2 5.4 %collective-permute-start.1 = (bf16[32,1024]{1,0:T(8,128)(2,1)S(1)}, bf16[32,1024]{1,0:T(8,128)(2,1)S(1)}, u32[]{:S(2)}, u32[]{:S(2)}) collective-permute-start(bf16[32,1024]{1,0:T(8,128)(2,1)S(1)} %get-tuple-element.24.act_ref), channel_id=1, source_target_pairs={{0,1},{1,0},{2,3},{3,2},{4,5},{5,4},{6,7},{7,6},{8,9},{9,8},{10,11... | collective-permute-start | bytes 196616 | tf_op jit(solution)/shard_map/ppermute | solution.py:249
  33.1 1.5 %collective-permute-start.3 = (bf16[16,16,384]{2,1,0:T(8,128)(2,1)S(1)}, bf16[16,16,384]{2,1,0:T(8,128)(2,1)S(1)}, u32[]{:S(2)}, u32[]{:S(2)}) collective-permute-start(bf16[16,16,384]{2,1,0:T(8,128)(2,1)S(1)} %get-tuple-element.33), channel_id=1, source_target_pairs={{0,2},{2,0},{1,3},{3,1},{4,6},{6,4},{5,7},{7,5},{8,10},{10,8},{9,1... | collective-permute-start | bytes 589832 | tf_op jit(solution)/shard_map/ppermute | solution.py:249

commit v8 on v7

--- a/solution.py
+++ b/solution.py
@@ -113,7 +113,10 @@
     weight_out[first : first + count, :] = jnp.broadcast_to(both, (count, LANES))
 
 
-def unpack_body(in_ref, rows, grads, weight_out, wide):
+def unpack_body(in_ref, gate_ref, rows, grads, weight_out, gate_turned, wide):
+    for n in range(gate_turned.shape[1] // COLS):
+        at = slice(n * COLS, (n + 1) * COLS)
+        gate_turned[:, at] = gate_ref[at, :].T
     meta = rows.shape[1] // COLS
     wide[...] = in_ref[...].astype(F32)
     unpack_grads(wide, grads, 0)
@@ -161,7 +164,7 @@
 
 
 def input_body(
-    cot_ref, recv_ref, gate_in, up_in, act_ref, weight_in, gate_ref, up_ref,
+    cot_ref, recv_ref, gate_in, up_in, act_ref, weight_in, gate_ref, up_ref, turned_ref,
     mine_ref, other_ref,
     wide,
 ):
@@ -180,10 +183,10 @@
     steps = width // COLS
     for n in range(steps):
         at = slice(n * COLS, (n + 1) * COLS)
-        if n % 3 == 0:
+        if n * COLS < turned_ref.shape[1]:
+            part = dot(gate_grad, turned_ref[:, at]) + dot_nt(up_grad, up_ref[at, :])
+        else:
             part = (dot(gate_ref[at, :], gate_turned) + dot(up_ref[at, :], up_turned)).T
-        else:
-            part = dot_nt(gate_grad, gate_ref[at, :]) + dot_nt(up_grad, up_ref[at, :])
         wide[:, n, :] = part
     lane = lax.broadcasted_iota(jnp.int32, (total, LANES), 1)
     high, low = high_low(jnp.where(lane == expert, prob, 0.0))
@@ -273,17 +276,19 @@
     )(*in_hbm(expert_ids, route_probs, tokens, out_grad, gate_w, up_w, down_w))
     own = lax.all_to_all(packed, ("chip", "local"), split_axis=0, concat_axis=0, tiled=True)
     other = swap(own, "core")
-    own_rows, own_grads, own_weight = call(
+    early = width // COLS * 8 // 14 * COLS
+    own_rows, own_grads, own_weight, gate_turned = call(
         unpack_body,
         [
             shaped((groups, width), BF16),
             shaped((groups, feats), BF16),
             shaped((groups, LANES), F32),
+            pltpu.VMEM((hidden, early), BF16),
         ],
-        [VMEM],
+        [VMEM, VMEM],
         [pltpu.VMEM((groups, ROWS, SPAN), F32)],
         moved=one // 4,
-    )(own)
+    )(own, gate_w)
     away, cot, weight, rows = call(
         cot_body,
         [
@@ -313,11 +318,11 @@
     in_mine, in_away = call(
         input_body,
         [shaped((groups, ROWS, COLS), BF16)] * 2,
-        [VMEM] * 8,
+        [VMEM] * 9,
         [pltpu.VMEM((total, ROWS, COLS), F32)],
         products=total * 2 * one,
         moved=2 * one,
-    )(cot, cot_recv, gate, up, act, weight, gate_w, up_w)
+    )(cot, cot_recv, gate, up, act, weight, gate_w, up_w, gate_turned)
     mine, away = call(
         routed_body,
         [shaped((groups, ROWS, SPAN), BF16)] * 2,

time: 47.7 us -> 47.4 us (level)
  waiting for transfers between devices: 2.51 us -> 1.44 us
  Pallas kernels: 12.8 us -> 13.5 us
    pallas_call x1, Pallas kernels: 0.35 us -> 1.44 us  [fast_device(): call(unpack_body, [shaped((groups, width), BF16), shaped((groups, feats),...]
    ppermute x4, waiting for transfers between devices: 2.51 us -> 1.44 us  [swap(): return lax.ppermute(x, axis, [(0, 1), (1, 0)])]
  transfers between devices with their start and end apart: 4 -> 4, of which waited for: 2 -> 1; matrix products, arithmetic and copies ran while one was open for 0% -> 0% of each run, Pallas kernels for 15% -> 17%
where the time goes in v8:
time: 47.4 us; the launch traced here: 47.1 us
  blocking collectives  29.1 us (61%)
  Pallas kernels  13.5 us (28%)
  starting transfers between devices  2.17 us (5%)
  waiting for transfers between devices  1.44 us (3%)
  between operations  0.76 us (2%)
    all_to_all x1, blocking collectives, fast_device(): lax.all_to_all(packed, ('chip', 'local'), split_axis=0, concat_axis=0, ti...  17 us
    all_to_all x1, blocking collectives, fast_device(): lax.all_to_all(summed, ('chip', 'local'), split_axis=0, concat_axis=0, ti...  12.1 us
    pallas_call x1, Pallas kernels, fast_device(): call(input_body, [shaped((groups, ROWS, COLS), BF16)] * 2, [VMEM] * 9, [p...  3.89 us
    pallas_call x1, Pallas kernels, fast_device(): call(forward_body, [shaped((total, hidden), F32), shaped((total, hidden),...  2.68 us
    pallas_call x1, Pallas kernels, fast_device(): call(cot_body, [shaped((total, hidden), BF16), shaped((total, hidden), F3...  2.43 us
    ppermute x4, starting transfers between devices, swap(): return lax.ppermute(x, axis, [(0, 1), (1, 0)])  2.17 us
    pallas_call x1, Pallas kernels, fast_device(): call(routed_body, [shaped((groups, ROWS, SPAN), BF16)] * 2, [VMEM] * 6, [...  1.45 us
    pallas_call x1, Pallas kernels, fast_device(): call(unpack_body, [shaped((groups, width), BF16), shaped((groups, feats),...  1.44 us
  transfers between devices with their start and end apart: 4, of which 1 were waited for; matrix products, arithmetic and copies ran while one was open for 0% of the time, Pallas kernels for 17%

profile of v8, /device:TPU:0, one launch (start us, length us, event | category | flops | bytes accessed | tf_op | source)
XLA Modules:
  0.0 47.1 jit_solution(420736442960530204)
XLA Ops:
  0.6 0.0 slice-start.2
  0.6 0.0 copy-start
  0.7 0.0 slice-start.3
  0.7 1.0 %shard_map.94 = (bf16[16,16,384]{2,1,0:T(8,128)(2,1)S(1)}, f32[8,128]{1,0:T(8,128)S(1)}) custom-call(s32[1,1,8]{2,1,0:T(1,128)} %ids_hbm.1, f32[1,1,8]{2,1,0:T(1,128)} %probs_hbm.1, bf16[1,1,3584]{2,1,0:T(2,128)(2,1)} %tok_hbm.1, bf16[1,1,3584]{2,1,0:T(2,128)(2,1)} %grad_hbm.1, bf16[3584,1024]{1,0:T(8,128)(2,1)} %bitcast.3, bf16[3584,1024]{1,0:T(8,128)(2,1)} %bitcast.7, ...), custom_call_target="tpu_custom_call" | custom-call | bytes 88080384 | tf_op jit(solution)/shard_map/pallas_call | solution.py:263
  1.6 17.0 %all_to_all.10.in_ref = bf16[16,16,384]{2,1,0:T(8,128)(2,1)S(1)} all-to-all(bf16[16,16,384]{2,1,0:T(8,128)(2,1)S(1)} %get-tuple-element.20), channel_id=1, replica_groups=mesh['chip'=8,'core'=2,'local'=2] {'chip','local'}, dimensions={0} | all-to-all | bytes 393216 | tf_op jit(solution)/shard_map/all_to_all | solution.py:277
  18.7 0.0 collective-permute-start
  18.7 1.4 %shard_map.95 = (bf16[16,3584]{1,0:T(8,128)(2,1)S(1)}, bf16[16,1792]{1,0:T(8,128)(2,1)S(1)}, f32[16,128]{1,0:T(8,128)S(1)}, bf16[1024,2048]{1,0:T(8,128)(2,1)S(1)}) custom-call(bf16[16,16,384]{2,1,0:T(8,128)(2,1)S(1)} %all_to_all.10.in_ref, bf16[3584,1024]{1,0:T(8,128)(2,1)S(1)} %bitcast.4), custom_call_target="tpu_custom_call" | custom-call | bytes 1835008 | tf_op jit(solution)/shard_map/pallas_call | solution.py:280
  20.1 0.0 collective-permute-done.other_ref
  20.1 0.0 slice-done.2
  20.1 0.0 slice-done.3
  20.2 0.0 slice-start.1
  20.2 2.4 %shard_map.96 = (bf16[32,1024]{1,0:T(8,128)(2,1)S(1)}, f32[32,1024]{1,0:T(8,128)S(1)}, f32[32,128]{1,0:T(8,128)S(1)}, bf16[32,3584]{1,0:T(8,128)(2,1)S(1)}) custom-call(bf16[16,16,384]{2,1,0:T(8,128)(2,1)S(1)} %collective-permute-done.other_ref, bf16[16,3584]{1,0:T(8,128)(2,1)S(1)} %get-tuple-element.21.rows_in, ...), custom_call_target="tpu_custom_call" | custom-call | flops 234881024 | bytes 7340032 | tf_op jit(solution)/shard_map/pallas_call | solution.py:292
  22.6 0.9 %collective-permute-start.2 = (bf16[32,1024]{1,0:T(8,128)(2,1)S(1)}, bf16[32,1024]{1,0:T(8,128)(2,1)S(1)}, u32[]{:S(2)}, u32[]{:S(2)}) collective-permute-start(bf16[32,1024]{1,0:T(8,128)(2,1)S(1)} %get-tuple-element.28), channel_id=1, source_target_pairs={{0,1},{1,0},{2,3},{3,2},{4,5},{5,4},{6,7},{7,6},{8,9},{9,8},{10,11... | collective-permute-start | bytes 196616 | tf_op jit(solution)/shard_map/ppermute | solution.py:252
  23.6 2.7 %shard_map.97 = (f32[32,1024]{1,0:T(8,128)S(1)}, f32[32,1024]{1,0:T(8,128)S(1)}, bf16[32,1024]{1,0:T(8,128)(2,1)S(1)}) custom-call(bf16[32,3584]{1,0:T(8,128)(2,1)S(1)} %get-tuple-element.24.rows_ref, bf16[3584,1024]{1,0:T(8,128)(2,1)S(1)} %bitcast.5, bf16[3584,1024]{1,0:T(8,128)(2,1)S(1)} %bitcast.10), custom_call_target="tpu_custom_call" | custom-call | flops 469762048 | bytes 14680064 | tf_op jit(solution)/shard_map/pallas_call | solution.py:306
  26.3 1.1 %collective-permute-start.1 = (bf16[32,1024]{1,0:T(8,128)(2,1)S(1)}, bf16[32,1024]{1,0:T(8,128)(2,1)S(1)}, u32[]{:S(2)}, u32[]{:S(2)}) collective-permute-start(bf16[32,1024]{1,0:T(8,128)(2,1)S(1)} %get-tuple-element.25.act_ref), channel_id=1, source_target_pairs={{0,1},{1,0},{2,3},{3,2},{4,5},{5,4},{6,7},{7,6},{8,9},{9,8},{10,11... | collective-permute-start | bytes 196616 | tf_op jit(solution)/shard_map/ppermute | solution.py:252
  27.4 0.0 collective-permute-done.2.recv_ref
  27.4 3.9 %shard_map.98 = (bf16[16,16,256]{2,1,0:T(8,128)(2,1)S(1)}, bf16[16,16,256]{2,1,0:T(8,128)(2,1)S(1)}) custom-call(f32[32,1024]{1,0:T(8,128)S(1)} %get-tuple-element.27.cot_ref, bf16[32,1024]{1,0:T(8,128)(2,1)S(1)} %collective-permute-done.2.recv_ref, f32[32,1024]{1,0:T(8,128)S(1)} %get-tuple-element.29.gate_in, f32[32,1024]{1,0:T(8,128)S(1)} %get-tuple-element.30.up_in, ...), custom_call_target="tpu_custom_call" | custom-call | flops 469762048 | bytes 14680064 | tf_op jit(solution)/shard_map/pallas_call | solution.py:318
  31.3 0.0 collective-permute-done.1.recv_ref
  31.3 1.5 %shard_map.99 = (bf16[16,16,384]{2,1,0:T(8,128)(2,1)S(1)}, bf16[16,16,384]{2,1,0:T(8,128)(2,1)S(1)}) custom-call(bf16[32,1024]{1,0:T(8,128)(2,1)S(1)} %get-tuple-element.25.act_ref, bf16[32,1024]{1,0:T(8,128)(2,1)S(1)} %collective-permute-done.1.recv_ref, f32[32,128]{1,0:T(8,128)S(1)} %get-tuple-element.26.weight_in, bf16[2048,1792]{1,0:T(8,128)(2,1)S(1)} %bitcast.16, ...), custom_call_target="tpu_custom_call" | custom-call | flops 234881024 | bytes 7340032 | tf_op jit(solution)/shard_map/pallas_call | solution.py:326
  32.8 0.1 collective-permute-start.3
  32.8 1.4 %collective-permute-done.3 = bf16[16,16,384]{2,1,0:T(8,128)(2,1)S(1)} collective-permute-done((bf16[16,16,384]{2,1,0:T(8,128)(2,1)S(1)}, bf16[16,16,384]{2,1,0:T(8,128)(2,1)S(1)}, u32[]{:S(2)}, u32[]{:S(2)}) %collective-permute-start.3) | collective-permute-done | bytes 196640 | tf_op jit(solution)/shard_map/ppermute | solution.py:252
  34.3 0.1 add_convert_fusion
  34.3 12.1 %all_to_all.11.in_ref = bf16[16,16,384]{2,1,0:T(8,128)(2,1)S(1)} all-to-all(bf16[16,16,384]{2,1,0:T(8,128)(2,1)S(1)} %add_convert_fusion), channel_id=1, replica_groups=mesh['chip'=8,'core'=2,'local'=2] {'chip','local'}, dimensions={0} | all-to-all | bytes 393216 | tf_op jit(solution)/shard_map/all_to_all | solution.py:335
  46.4 0.7 %shard_map.100 = (bf16[1,1,3584]{2,1,0:T(2,128)(2,1)}, bf16[1,1,3584]{2,1,0:T(2,128)(2,1)}, f32[1,1,8]{2,1,0:T(1,128)}) custom-call(bf16[16,16,384]{2,1,0:T(8,128)(2,1)S(1)} %all_to_all.11.in_ref, f32[8,128]{1,0:T(8,128)S(1)} %get-tuple-element.36.named_ref), custom_call_target="tpu_custom_call" | custom-call | tf_op jit(solution)/shard_map/pallas_call | solution.py:336
  (6 shorter events, 0.0 us)
Async XLA Ops:
  0.6 19.5 %slice-start.2 = ((s8[7340032]{0:T(1024)(128)(4,1)}), s8[4194304]{0:T(1024)(128)(4,1)S(1)}, s32[]{:S(2)}) async-start(s8[7340032]{0:T(1024)(128)(4,1)} %bitcast.13), calls=%async_computation.4 | async-start | bytes 8388608
  0.6 18.0 %copy-start = (bf16[1,3584,1024]{2,1,0:T(8,128)(2,1)S(1)}, bf16[1,3584,1024]{2,1,0:T(8,128)(2,1)}, u32[]{:S(2)}) copy-start(bf16[1,3584,1024]{2,1,0:T(8,128)(2,1)} %param.10) | copy-start | bytes 22020100
  0.7 19.5 %slice-start.3 = ((s8[7340032]{0:T(1024)(128)(4,1)}), s8[3145728]{0:T(1024)(128)(4,1)S(1)}, s32[]{:S(2)}) async-start(s8[7340032]{0:T(1024)(128)(4,1)} %bitcast.13), calls=%async_computation.5 | async-start | bytes 6291456
  18.7 4.9 %slice-start = ((s8[7340032]{0:T(1024)(128)(4,1)}), s8[4194304]{0:T(1024)(128)(4,1)S(1)}, s32[]{:S(2)}) async-start(s8[7340032]{0:T(1024)(128)(4,1)} %bitcast.8), calls=%async_computation.2 | async-start | bytes 8388608
  18.7 1.5 %collective-permute-start = (bf16[16,16,384]{2,1,0:T(8,128)(2,1)S(1)}, bf16[16,16,384]{2,1,0:T(8,128)(2,1)S(1)}, u32[]{:S(2)}, u32[]{:S(2)}) collective-permute-start(bf16[16,16,384]{2,1,0:T(8,128)(2,1)S(1)} %all_to_all.10.in_ref), channel_id=1, source_target_pairs={{0,2},{2,0},{1,3},{3,1},{4,6},{6,4},{5,7},{7,5},{8,10},{10,8},{9,1... | collective-permute-start | bytes 589832 | tf_op jit(solution)/shard_map/ppermute | solution.py:252
  20.2 3.4 %slice-start.1 = ((s8[7340032]{0:T(1024)(128)(4,1)}), s8[3145728]{0:T(1024)(128)(4,1)S(1)}, s32[]{:S(2)}) async-start(s8[7340032]{0:T(1024)(128)(4,1)} %bitcast.8), calls=%async_computation.3 | async-start | bytes 6291456
  22.6 4.8 %collective-permute-start.2 = (bf16[32,1024]{1,0:T(8,128)(2,1)S(1)}, bf16[32,1024]{1,0:T(8,128)(2,1)S(1)}, u32[]{:S(2)}, u32[]{:S(2)}) collective-permute-start(bf16[32,1024]{1,0:T(8,128)(2,1)S(1)} %get-tuple-element.28), channel_id=1, source_target_pairs={{0,1},{1,0},{2,3},{3,2},{4,5},{5,4},{6,7},{7,6},{8,9},{9,8},{10,11... | collective-permute-start | bytes 196616 | tf_op jit(solution)/shard_map/ppermute | solution.py:252
  26.3 5.0 %collective-permute-start.1 = (bf16[32,1024]{1,0:T(8,128)(2,1)S(1)}, bf16[32,1024]{1,0:T(8,128)(2,1)S(1)}, u32[]{:S(2)}, u32[]{:S(2)}) collective-permute-start(bf16[32,1024]{1,0:T(8,128)(2,1)S(1)} %get-tuple-element.25.act_ref), channel_id=1, source_target_pairs={{0,1},{1,0},{2,3},{3,2},{4,5},{5,4},{6,7},{7,6},{8,9},{9,8},{10,11... | collective-permute-start | bytes 196616 | tf_op jit(solution)/shard_map/ppermute | solution.py:252
  32.8 1.5 %collective-permute-start.3 = (bf16[16,16,384]{2,1,0:T(8,128)(2,1)S(1)}, bf16[16,16,384]{2,1,0:T(8,128)(2,1)S(1)}, u32[]{:S(2)}, u32[]{:S(2)}) collective-permute-start(bf16[16,16,384]{2,1,0:T(8,128)(2,1)S(1)} %get-tuple-element.35), channel_id=1, source_target_pairs={{0,2},{2,0},{1,3},{3,1},{4,6},{6,4},{5,7},{7,5},{8,10},{10,8},{9,1... | collective-permute-start | bytes 589832 | tf_op jit(solution)/shard_map/ppermute | solution.py:252

commit v9 on v8

--- a/solution.py
+++ b/solution.py
@@ -153,9 +153,13 @@
     rows[:count, :] = rows_in[...]
 
 
-def forward_body(rows_ref, gate_ref, up_ref, gate_out, up_out, act_ref):
+def forward_body(rows_ref, gate_ref, up_ref, gate_out, up_out, act_ref, up_turned):
     tokens = rows_ref[...]
-    for n in range(gate_ref.shape[1] // COLS):
+    steps = gate_ref.shape[1] // COLS
+    for n in range(steps):
+        for i in range(n, up_turned.shape[1] // COLS, steps):
+            at = slice(i * COLS, (i + 1) * COLS)
+            up_turned[:, at] = up_ref[at, :].T
         cols = slice(n * COLS, (n + 1) * COLS)
         gate, up = dot(tokens, gate_ref[:, cols]), dot(tokens, up_ref[:, cols])
         gate_out[:, cols] = gate
@@ -164,7 +168,7 @@
 
 
 def input_body(
-    cot_ref, recv_ref, gate_in, up_in, act_ref, weight_in, gate_ref, up_ref, turned_ref,
+    cot_ref, recv_ref, gate_in, up_in, act_ref, weight_in, gate_ref, up_ref, turned_ref, up_turned_ref,
     mine_ref, other_ref,
     wide,
 ):
@@ -179,14 +183,17 @@
     hidden_grad = cot * weight_in[:, 0:1]
     gate_grad = (hidden_grad * up * sig * (1.0 + gate * (1.0 - sig))).astype(BF16)
     up_grad = (hidden_grad * (gate * sig)).astype(BF16)
-    gate_turned, up_turned = gate_grad.T, up_grad.T
     steps = width // COLS
     for n in range(steps):
         at = slice(n * COLS, (n + 1) * COLS)
         if n * COLS < turned_ref.shape[1]:
-            part = dot(gate_grad, turned_ref[:, at]) + dot_nt(up_grad, up_ref[at, :])
+            part = dot(gate_grad, turned_ref[:, at])
         else:
-            part = (dot(gate_ref[at, :], gate_turned) + dot(up_ref[at, :], up_turned)).T
+            part = dot_nt(gate_grad, gate_ref[at, :])
+        if n * COLS < up_turned_ref.shape[1]:
+            part += dot(up_grad, up_turned_ref[:, at])
+        else:
+            part += dot_nt(up_grad, up_ref[at, :])
         wide[:, n, :] = part
     lane = lax.broadcasted_iota(jnp.int32, (total, LANES), 1)
     high, low = high_low(jnp.where(lane == expert, prob, 0.0))
@@ -303,12 +310,13 @@
         moved=one,
     )(other, own_rows, own_grads, own_weight, down_w)
     cot_recv = swap(away, "local")
-    gate, up, act = call(
+    gate, up, act, up_turned = call(
         forward_body,
         [
             shaped((total, hidden), F32),
             shaped((total, hidden), F32),
             shaped((total, hidden), BF16),
+            pltpu.VMEM((hidden, width // COLS * 14 // 14 * COLS), BF16),
         ],
         [VMEM] * 3,
         products=total * 2 * one,
@@ -318,11 +326,11 @@
     in_mine, in_away = call(
         input_body,
         [shaped((groups, ROWS, COLS), BF16)] * 2,
-        [VMEM] * 9,
+        [VMEM] * 10,
         [pltpu.VMEM((total, ROWS, COLS), F32)],
         products=total * 2 * one,
         moved=2 * one,
-    )(cot, cot_recv, gate, up, act, weight, gate_w, up_w, gate_turned)
+    )(cot, cot_recv, gate, up, act, weight, gate_w, up_w, gate_turned, up_turned)
     mine, away = call(
         routed_body,
         [shaped((groups, ROWS, SPAN), BF16)] * 2,

time: 47.4 us -> 47.4 us (level)
  Pallas kernels: 13.5 us -> 13 us
  blocking collectives: 29.1 us -> 29.6 us
    pallas_call x1, Pallas kernels: 3.89 us -> 3.17 us  [fast_device(): call(input_body, [shaped((groups, ROWS, COLS), BF16)] * 2, [VMEM] * 10, [...]
    all_to_all x1, blocking collectives: 12.1 us -> 12.6 us  [fast_device(): lax.all_to_all(summed, ('chip', 'local'), split_axis=0, concat_axis=0, ti...]
  transfers between devices with their start and end apart: 4 -> 4, of which waited for: 1 -> 1; matrix products, arithmetic and copies ran while one was open for 0% -> 0% of each run, Pallas kernels for 17% -> 16%
where the time goes in v9:
time: 47.4 us; the launch traced here: 47.1 us
  blocking collectives  29.6 us (62%)
  Pallas kernels  13 us (27%)
  starting transfers between devices  2.17 us (5%)
  waiting for transfers between devices  1.44 us (3%)
  between operations  0.76 us (2%)
    all_to_all x1, blocking collectives, fast_device(): lax.all_to_all(packed, ('chip', 'local'), split_axis=0, concat_axis=0, ti...  17 us
    all_to_all x1, blocking collectives, fast_device(): lax.all_to_all(summed, ('chip', 'local'), split_axis=0, concat_axis=0, ti...  12.6 us
    pallas_call x1, Pallas kernels, fast_device(): call(input_body, [shaped((groups, ROWS, COLS), BF16)] * 2, [VMEM] * 10, [...  3.17 us
    pallas_call x1, Pallas kernels, fast_device(): call(forward_body, [shaped((total, hidden), F32), shaped((total, hidden),...  2.86 us
    pallas_call x1, Pallas kernels, fast_device(): call(cot_body, [shaped((total, hidden), BF16), shaped((total, hidden), F3...  2.43 us
    ppermute x4, starting transfers between devices, swap(): return lax.ppermute(x, axis, [(0, 1), (1, 0)])  2.17 us
    pallas_call x1, Pallas kernels, fast_device(): call(routed_body, [shaped((groups, ROWS, SPAN), BF16)] * 2, [VMEM] * 6, [...  1.46 us
    pallas_call x1, Pallas kernels, fast_device(): call(unpack_body, [shaped((groups, width), BF16), shaped((groups, feats),...  1.44 us
  transfers between devices with their start and end apart: 4, of which 1 were waited for; matrix products, arithmetic and copies ran while one was open for 0% of the time, Pallas kernels for 16%

profile of v9, /device:TPU:0, one launch (start us, length us, event | category | flops | bytes accessed | tf_op | source)
XLA Modules:
  0.0 47.1 jit_solution(17688468545031267387)
XLA Ops:
  0.6 0.0 slice-start.2
  0.6 0.0 copy-start
  0.7 0.0 slice-start.3
  0.7 1.0 %shard_map.94 = (bf16[16,16,384]{2,1,0:T(8,128)(2,1)S(1)}, f32[8,128]{1,0:T(8,128)S(1)}) custom-call(s32[1,1,8]{2,1,0:T(1,128)} %ids_hbm.1, f32[1,1,8]{2,1,0:T(1,128)} %probs_hbm.1, bf16[1,1,3584]{2,1,0:T(2,128)(2,1)} %tok_hbm.1, bf16[1,1,3584]{2,1,0:T(2,128)(2,1)} %grad_hbm.1, bf16[3584,1024]{1,0:T(8,128)(2,1)} %bitcast.3, bf16[3584,1024]{1,0:T(8,128)(2,1)} %bitcast.7, ...), custom_call_target="tpu_custom_call" | custom-call | bytes 88080384 | tf_op jit(solution)/shard_map/pallas_call | solution.py:270
  1.6 17.0 %all_to_all.10.in_ref = bf16[16,16,384]{2,1,0:T(8,128)(2,1)S(1)} all-to-all(bf16[16,16,384]{2,1,0:T(8,128)(2,1)S(1)} %get-tuple-element.21), channel_id=1, replica_groups=mesh['chip'=8,'core'=2,'local'=2] {'chip','local'}, dimensions={0} | all-to-all | bytes 393216 | tf_op jit(solution)/shard_map/all_to_all | solution.py:284
  18.7 0.0 collective-permute-start
  18.7 1.4 %shard_map.95 = (bf16[16,3584]{1,0:T(8,128)(2,1)S(1)}, bf16[16,1792]{1,0:T(8,128)(2,1)S(1)}, f32[16,128]{1,0:T(8,128)S(1)}, bf16[1024,2048]{1,0:T(8,128)(2,1)S(1)}) custom-call(bf16[16,16,384]{2,1,0:T(8,128)(2,1)S(1)} %all_to_all.10.in_ref, bf16[3584,1024]{1,0:T(8,128)(2,1)S(1)} %bitcast.4), custom_call_target="tpu_custom_call" | custom-call | bytes 1835008 | tf_op jit(solution)/shard_map/pallas_call | solution.py:287
  20.1 0.0 collective-permute-done.other_ref
  20.1 0.0 slice-done.2
  20.1 0.0 slice-done.3
  20.2 0.0 slice-start.1
  20.2 2.4 %shard_map.96 = (bf16[32,1024]{1,0:T(8,128)(2,1)S(1)}, f32[32,1024]{1,0:T(8,128)S(1)}, f32[32,128]{1,0:T(8,128)S(1)}, bf16[32,3584]{1,0:T(8,128)(2,1)S(1)}) custom-call(bf16[16,16,384]{2,1,0:T(8,128)(2,1)S(1)} %collective-permute-done.other_ref, bf16[16,3584]{1,0:T(8,128)(2,1)S(1)} %get-tuple-element.22.rows_in, ...), custom_call_target="tpu_custom_call" | custom-call | flops 234881024 | bytes 7340032 | tf_op jit(solution)/shard_map/pallas_call | solution.py:299
  22.6 0.9 %collective-permute-start.2 = (bf16[32,1024]{1,0:T(8,128)(2,1)S(1)}, bf16[32,1024]{1,0:T(8,128)(2,1)S(1)}, u32[]{:S(2)}, u32[]{:S(2)}) collective-permute-start(bf16[32,1024]{1,0:T(8,128)(2,1)S(1)} %get-tuple-element.29), channel_id=1, source_target_pairs={{0,1},{1,0},{2,3},{3,2},{4,5},{5,4},{6,7},{7,6},{8,9},{9,8},{10,11... | collective-permute-start | bytes 196616 | tf_op jit(solution)/shard_map/ppermute | solution.py:259
  23.6 2.9 %shard_map.97 = (f32[32,1024]{1,0:T(8,128)S(1)}, f32[32,1024]{1,0:T(8,128)S(1)}, bf16[32,1024]{1,0:T(8,128)(2,1)S(1)}, bf16[1024,3584]{1,0:T(8,128)(2,1)S(1)}) custom-call(bf16[32,3584]{1,0:T(8,128)(2,1)S(1)} %get-tuple-element.25.rows_ref, bf16[3584,1024]{1,0:T(8,128)(2,1)S(1)} %bitcast.5, bf16[3584,1024]{1,0:T(8,128)(2,1)S(1)} %bitcast.10), custom_call_target="tpu_custom_call" | custom-call | flops 469762048 | bytes 14680064 | tf_op jit(solution)/shard_map/pallas_call | solution.py:313
  26.4 1.1 %collective-permute-start.1 = (bf16[32,1024]{1,0:T(8,128)(2,1)S(1)}, bf16[32,1024]{1,0:T(8,128)(2,1)S(1)}, u32[]{:S(2)}, u32[]{:S(2)}) collective-permute-start(bf16[32,1024]{1,0:T(8,128)(2,1)S(1)} %get-tuple-element.26.act_ref), channel_id=1, source_target_pairs={{0,1},{1,0},{2,3},{3,2},{4,5},{5,4},{6,7},{7,6},{8,9},{9,8},{10,11... | collective-permute-start | bytes 196616 | tf_op jit(solution)/shard_map/ppermute | solution.py:259
  27.6 0.0 collective-permute-done.2.recv_ref
  27.6 3.2 %shard_map.98 = (bf16[16,16,256]{2,1,0:T(8,128)(2,1)S(1)}, bf16[16,16,256]{2,1,0:T(8,128)(2,1)S(1)}) custom-call(f32[32,1024]{1,0:T(8,128)S(1)} %get-tuple-element.28.cot_ref, bf16[32,1024]{1,0:T(8,128)(2,1)S(1)} %collective-permute-done.2.recv_ref, f32[32,1024]{1,0:T(8,128)S(1)} %get-tuple-element.30.gate_in, f32[32,1024]{1,0:T(8,128)S(1)} %get-tuple-element.31.up_in, ...), custom_call_target="tpu_custom_call" | custom-call | flops 469762048 | bytes 14680064 | tf_op jit(solution)/shard_map/pallas_call | solution.py:326
  30.8 0.0 collective-permute-done.1.recv_ref
  30.8 1.5 %shard_map.99 = (bf16[16,16,384]{2,1,0:T(8,128)(2,1)S(1)}, bf16[16,16,384]{2,1,0:T(8,128)(2,1)S(1)}) custom-call(bf16[32,1024]{1,0:T(8,128)(2,1)S(1)} %get-tuple-element.26.act_ref, bf16[32,1024]{1,0:T(8,128)(2,1)S(1)} %collective-permute-done.1.recv_ref, f32[32,128]{1,0:T(8,128)S(1)} %get-tuple-element.27.weight_in, bf16[2048,1792]{1,0:T(8,128)(2,1)S(1)} %bitcast.16, ...), custom_call_target="tpu_custom_call" | custom-call | flops 234881024 | bytes 7340032 | tf_op jit(solution)/shard_map/pallas_call | solution.py:334
  32.2 0.1 collective-permute-start.3
  32.3 1.4 %collective-permute-done.3 = bf16[16,16,384]{2,1,0:T(8,128)(2,1)S(1)} collective-permute-done((bf16[16,16,384]{2,1,0:T(8,128)(2,1)S(1)}, bf16[16,16,384]{2,1,0:T(8,128)(2,1)S(1)}, u32[]{:S(2)}, u32[]{:S(2)}) %collective-permute-start.3) | collective-permute-done | bytes 196640 | tf_op jit(solution)/shard_map/ppermute | solution.py:259
  33.7 0.1 add_convert_fusion
  33.8 12.6 %all_to_all.11.in_ref = bf16[16,16,384]{2,1,0:T(8,128)(2,1)S(1)} all-to-all(bf16[16,16,384]{2,1,0:T(8,128)(2,1)S(1)} %add_convert_fusion), channel_id=1, replica_groups=mesh['chip'=8,'core'=2,'local'=2] {'chip','local'}, dimensions={0} | all-to-all | bytes 393216 | tf_op jit(solution)/shard_map/all_to_all | solution.py:343
  46.4 0.7 %shard_map.100 = (bf16[1,1,3584]{2,1,0:T(2,128)(2,1)}, bf16[1,1,3584]{2,1,0:T(2,128)(2,1)}, f32[1,1,8]{2,1,0:T(1,128)}) custom-call(bf16[16,16,384]{2,1,0:T(8,128)(2,1)S(1)} %all_to_all.11.in_ref, f32[8,128]{1,0:T(8,128)S(1)} %get-tuple-element.38.named_ref), custom_call_target="tpu_custom_call" | custom-call | tf_op jit(solution)/shard_map/pallas_call | solution.py:344
  (6 shorter events, 0.0 us)
Async XLA Ops:
  0.6 19.5 %slice-start.2 = ((s8[7340032]{0:T(1024)(128)(4,1)}), s8[4194304]{0:T(1024)(128)(4,1)S(1)}, s32[]{:S(2)}) async-start(s8[7340032]{0:T(1024)(128)(4,1)} %bitcast.13), calls=%async_computation.4 | async-start | bytes 8388608
  0.6 18.0 %copy-start = (bf16[1,3584,1024]{2,1,0:T(8,128)(2,1)S(1)}, bf16[1,3584,1024]{2,1,0:T(8,128)(2,1)}, u32[]{:S(2)}) copy-start(bf16[1,3584,1024]{2,1,0:T(8,128)(2,1)} %param.10) | copy-start | bytes 22020100
  0.7 19.5 %slice-start.3 = ((s8[7340032]{0:T(1024)(128)(4,1)}), s8[3145728]{0:T(1024)(128)(4,1)S(1)}, s32[]{:S(2)}) async-start(s8[7340032]{0:T(1024)(128)(4,1)} %bitcast.13), calls=%async_computation.5 | async-start | bytes 6291456
  18.7 4.9 %slice-start = ((s8[7340032]{0:T(1024)(128)(4,1)}), s8[4194304]{0:T(1024)(128)(4,1)S(1)}, s32[]{:S(2)}) async-start(s8[7340032]{0:T(1024)(128)(4,1)} %bitcast.8), calls=%async_computation.2 | async-start | bytes 8388608
  18.7 1.5 %collective-permute-start = (bf16[16,16,384]{2,1,0:T(8,128)(2,1)S(1)}, bf16[16,16,384]{2,1,0:T(8,128)(2,1)S(1)}, u32[]{:S(2)}, u32[]{:S(2)}) collective-permute-start(bf16[16,16,384]{2,1,0:T(8,128)(2,1)S(1)} %all_to_all.10.in_ref), channel_id=1, source_target_pairs={{0,2},{2,0},{1,3},{3,1},{4,6},{6,4},{5,7},{7,5},{8,10},{10,8},{9,1... | collective-permute-start | bytes 589832 | tf_op jit(solution)/shard_map/ppermute | solution.py:259
  20.2 3.4 %slice-start.1 = ((s8[7340032]{0:T(1024)(128)(4,1)}), s8[3145728]{0:T(1024)(128)(4,1)S(1)}, s32[]{:S(2)}) async-start(s8[7340032]{0:T(1024)(128)(4,1)} %bitcast.8), calls=%async_computation.3 | async-start | bytes 6291456
  22.6 5.0 %collective-permute-start.2 = (bf16[32,1024]{1,0:T(8,128)(2,1)S(1)}, bf16[32,1024]{1,0:T(8,128)(2,1)S(1)}, u32[]{:S(2)}, u32[]{:S(2)}) collective-permute-start(bf16[32,1024]{1,0:T(8,128)(2,1)S(1)} %get-tuple-element.29), channel_id=1, source_target_pairs={{0,1},{1,0},{2,3},{3,2},{4,5},{5,4},{6,7},{7,6},{8,9},{9,8},{10,11... | collective-permute-start | bytes 196616 | tf_op jit(solution)/shard_map/ppermute | solution.py:259
  26.4 4.3 %collective-permute-start.1 = (bf16[32,1024]{1,0:T(8,128)(2,1)S(1)}, bf16[32,1024]{1,0:T(8,128)(2,1)S(1)}, u32[]{:S(2)}, u32[]{:S(2)}) collective-permute-start(bf16[32,1024]{1,0:T(8,128)(2,1)S(1)} %get-tuple-element.26.act_ref), channel_id=1, source_target_pairs={{0,1},{1,0},{2,3},{3,2},{4,5},{5,4},{6,7},{7,6},{8,9},{9,8},{10,11... | collective-permute-start | bytes 196616 | tf_op jit(solution)/shard_map/ppermute | solution.py:259
  32.2 1.5 %collective-permute-start.3 = (bf16[16,16,384]{2,1,0:T(8,128)(2,1)S(1)}, bf16[16,16,384]{2,1,0:T(8,128)(2,1)S(1)}, u32[]{:S(2)}, u32[]{:S(2)}) collective-permute-start(bf16[16,16,384]{2,1,0:T(8,128)(2,1)S(1)} %get-tuple-element.37), channel_id=1, source_target_pairs={{0,2},{2,0},{1,3},{3,1},{4,6},{6,4},{5,7},{7,5},{8,10},{10,8},{9,1... | collective-permute-start | bytes 589832 | tf_op jit(solution)/shard_map/ppermute | solution.py:259

commit v10 on v9

--- a/solution.py
+++ b/solution.py
@@ -126,8 +126,8 @@
 
 
 def cot_body(
-    other_ref, rows_in, grads_in, weight_in, down_ref,
-    away_ref, cot_ref, weight_out, rows,
+    other_ref, rows_in, grads_in, weight_in, down_ref, gate_ref,
+    away_ref, cot_ref, weight_out, rows, gate_late,
     wide, grads,
 ):
     count = other_ref.shape[0]
@@ -139,13 +139,17 @@
     wide[...] = other_ref[...].astype(F32)
     unpack_grads(wide, grads, count)
     grads[:count, :] = grads_in[...]
-    grad = grads[...]
+    grad = grads[...].T
+    late = gate_late.shape[1]
     for n in range(steps):
         at = slice(n * COLS, (n + 1) * COLS)
-        away_ref[:, at] = dot_nt(grad, down_ref[side_rows(1 - local, hidden, n), :]).astype(BF16)
+        away_ref[:, at] = dot(down_ref[side_rows(1 - local, hidden, n), :], grad).astype(BF16).T
+        for i in range(n, late // COLS, steps):
+            first = gate_ref.shape[0] - late + i * COLS
+            gate_late[:, i * COLS : (i + 1) * COLS] = gate_ref[first : first + COLS, :].T
     for n in range(steps):
         at = slice(n * COLS, (n + 1) * COLS)
-        cot_ref[:, at] = dot_nt(grad, down_ref[side_rows(local, hidden, n), :])
+        cot_ref[:, at] = dot(down_ref[side_rows(local, hidden, n), :], grad).T
     for i in range(meta):
         unpack_row(wide, rows, count, i)
     unpack_weight(wide, weight_out, count, meta)
@@ -168,13 +172,13 @@
 
 
 def input_body(
-    cot_ref, recv_ref, gate_in, up_in, act_ref, weight_in, gate_ref, up_ref, turned_ref, up_turned_ref,
+    cot_ref, recv_ref, gate_in, up_in, act_ref, weight_in, gate_first, gate_late, up_turned,
     mine_ref, other_ref,
     wide,
 ):
     total = cot_ref.shape[0]
     count = total // 2
-    width = up_ref.shape[0]
+    width, early = up_turned.shape[1], gate_first.shape[1]
     expert = lax.axis_index("chip") * 2 + lax.axis_index("core")
     gate, up = gate_in[...], up_in[...]
     sig = jax.nn.sigmoid(gate)
@@ -186,14 +190,11 @@
     steps = width // COLS
     for n in range(steps):
         at = slice(n * COLS, (n + 1) * COLS)
-        if n * COLS < turned_ref.shape[1]:
-            part = dot(gate_grad, turned_ref[:, at])
+        if n * COLS < early:
+            gate_part = gate_first[:, at]
         else:
-            part = dot_nt(gate_grad, gate_ref[at, :])
-        if n * COLS < up_turned_ref.shape[1]:
-            part += dot(up_grad, up_turned_ref[:, at])
-        else:
-            part += dot_nt(up_grad, up_ref[at, :])
+            gate_part = gate_late[:, n * COLS - early : (n + 1) * COLS - early]
+        part = dot(gate_grad, gate_part) + dot(up_grad, up_turned[:, at])
         wide[:, n, :] = part
     lane = lax.broadcasted_iota(jnp.int32, (total, LANES), 1)
     high, low = high_low(jnp.where(lane == expert, prob, 0.0))
@@ -296,19 +297,20 @@
         [pltpu.VMEM((groups, ROWS, SPAN), F32)],
         moved=one // 4,
     )(own, gate_w)
-    away, cot, weight, rows = call(
+    away, cot, weight, rows, gate_late = call(
         cot_body,
         [
             shaped((total, hidden), BF16),
             shaped((total, hidden), F32),
             shaped((total, LANES), F32),
             shaped((total, width), BF16),
+            pltpu.VMEM((hidden, width - early), BF16),
         ],
-        [VMEM] * 5,
+        [VMEM] * 6,
         [pltpu.VMEM((groups, ROWS, SPAN), F32), pltpu.VMEM((total, feats), BF16)],
         products=total * one,
         moved=one,
-    )(other, own_rows, own_grads, own_weight, down_w)
+    )(other, own_rows, own_grads, own_weight, down_w, gate_w)
     cot_recv = swap(away, "local")
     gate, up, act, up_turned = call(
         forward_body,
@@ -326,11 +328,11 @@
     in_mine, in_away = call(
         input_body,
         [shaped((groups, ROWS, COLS), BF16)] * 2,
-        [VMEM] * 10,
+        [VMEM] * 9,
         [pltpu.VMEM((total, ROWS, COLS), F32)],
         products=total * 2 * one,
         moved=2 * one,
-    )(cot, cot_recv, gate, up, act, weight, gate_w, up_w, gate_turned, up_turned)
+    )(cot, cot_recv, gate, up, act, weight, gate_turned, gate_late, up_turned)
     mine, away = call(
         routed_body,
         [shaped((groups, ROWS, SPAN), BF16)] * 2,

time: 47.4 us -> 47.4 us (level)
  transfers between devices with their start and end apart: 4 -> 4, of which waited for: 1 -> 2; matrix products, arithmetic and copies ran while one was open for 0% -> 0% of each run, Pallas kernels for 16% -> 15%
where the time goes in v10:
time: 47.4 us; the launch traced here: 47.1 us
  blocking collectives  29.6 us (62%)
  Pallas kernels  12.6 us (27%)
  starting transfers between devices  2.22 us (5%)
  waiting for transfers between devices  1.83 us (4%)
  between operations  0.75 us (2%)
    all_to_all x1, blocking collectives, fast_device(): lax.all_to_all(packed, ('chip', 'local'), split_axis=0, concat_axis=0, ti...  17 us
    all_to_all x1, blocking collectives, fast_device(): lax.all_to_all(summed, ('chip', 'local'), split_axis=0, concat_axis=0, ti...  12.6 us
    pallas_call x1, Pallas kernels, fast_device(): call(forward_body, [shaped((total, hidden), F32), shaped((total, hidden),...  2.85 us
    pallas_call x1, Pallas kernels, fast_device(): call(input_body, [shaped((groups, ROWS, COLS), BF16)] * 2, [VMEM] * 9, [p...  2.78 us
    pallas_call x1, Pallas kernels, fast_device(): call(cot_body, [shaped((total, hidden), BF16), shaped((total, hidden), F3...  2.4 us
    ppermute x4, starting transfers between devices, swap(): return lax.ppermute(x, axis, [(0, 1), (1, 0)])  2.22 us
    ppermute x4, waiting for transfers between devices, swap(): return lax.ppermute(x, axis, [(0, 1), (1, 0)])  1.83 us
    pallas_call x1, Pallas kernels, fast_device(): call(routed_body, [shaped((groups, ROWS, SPAN), BF16)] * 2, [VMEM] * 6, [...  1.44 us
  transfers between devices with their start and end apart: 4, of which 2 were waited for; matrix products, arithmetic and copies ran while one was open for 0% of the time, Pallas kernels for 15%

profile of v10, /device:TPU:0, one launch (start us, length us, event | category | flops | bytes accessed | tf_op | source)
XLA Modules:
  0.0 47.1 jit_solution(1099488819977379168)
XLA Ops:
  0.6 0.0 slice-start
  0.7 0.0 slice-start.1
  0.7 1.0 %shard_map.94 = (bf16[16,16,384]{2,1,0:T(8,128)(2,1)S(1)}, f32[8,128]{1,0:T(8,128)S(1)}) custom-call(s32[1,1,8]{2,1,0:T(1,128)} %ids_hbm.1, f32[1,1,8]{2,1,0:T(1,128)} %probs_hbm.1, bf16[1,1,3584]{2,1,0:T(2,128)(2,1)} %tok_hbm.1, bf16[1,1,3584]{2,1,0:T(2,128)(2,1)} %grad_hbm.1, bf16[3584,1024]{1,0:T(8,128)(2,1)} %bitcast.3, bf16[3584,1024]{1,0:T(8,128)(2,1)} %bitcast.12, ...), custom_call_target="tpu_custom_call" | custom-call | bytes 88080384 | tf_op jit(solution)/shard_map/pallas_call | solution.py:271
  1.6 17.0 %all_to_all.10.in_ref = bf16[16,16,384]{2,1,0:T(8,128)(2,1)S(1)} all-to-all(bf16[16,16,384]{2,1,0:T(8,128)(2,1)S(1)} %get-tuple-element.22), channel_id=1, replica_groups=mesh['chip'=8,'core'=2,'local'=2] {'chip','local'}, dimensions={0} | all-to-all | bytes 393216 | tf_op jit(solution)/shard_map/all_to_all | solution.py:285
  18.7 0.0 collective-permute-start
  18.7 1.4 %shard_map.95 = (bf16[16,3584]{1,0:T(8,128)(2,1)S(1)}, bf16[16,1792]{1,0:T(8,128)(2,1)S(1)}, f32[16,128]{1,0:T(8,128)S(1)}, bf16[1024,2048]{1,0:T(8,128)(2,1)S(1)}) custom-call(bf16[16,16,384]{2,1,0:T(8,128)(2,1)S(1)} %all_to_all.10.in_ref, bf16[3584,1024]{1,0:T(8,128)(2,1)S(1)} %bitcast.4), custom_call_target="tpu_custom_call" | custom-call | bytes 1835008 | tf_op jit(solution)/shard_map/pallas_call | solution.py:288
  20.1 0.0 collective-permute-done.other_ref
  20.1 0.0 slice-done
  20.1 0.0 slice-done.1
  20.2 0.0 slice-start.3
  20.2 2.4 %shard_map.96 = (bf16[32,1024]{1,0:T(8,128)(2,1)S(1)}, f32[32,1024]{1,0:T(8,128)S(1)}, f32[32,128]{1,0:T(8,128)S(1)}, bf16[32,3584]{1,0:T(8,128)(2,1)S(1)}, bf16[1024,1536]{1,0:T(8,128)(2,1)S(1)}) custom-call(bf16[16,16,384]{2,1,0:T(8,128)(2,1)S(1)} %collective-permute-done.other_ref, bf16[16,3584]{1,0:T(8,128)(2,1)S(1)} %get-tuple-element.23.rows_in, ...), custom_call_target="tpu_custom_call" | custom-call | flops 234881024 | bytes 7340032 | tf_op jit(solution)/shard_map/pallas_call | solution.py:300
  22.6 1.0 %collective-permute-start.2 = (bf16[32,1024]{1,0:T(8,128)(2,1)S(1)}, bf16[32,1024]{1,0:T(8,128)(2,1)S(1)}, u32[]{:S(2)}, u32[]{:S(2)}) collective-permute-start(bf16[32,1024]{1,0:T(8,128)(2,1)S(1)} %get-tuple-element.30), channel_id=1, source_target_pairs={{0,1},{1,0},{2,3},{3,2},{4,5},{5,4},{6,7},{7,6},{8,9},{9,8},{10,11... | collective-permute-start | bytes 196616 | tf_op jit(solution)/shard_map/ppermute | solution.py:260
  23.6 0.0 slice-done.3
  23.6 2.8 %shard_map.97 = (f32[32,1024]{1,0:T(8,128)S(1)}, f32[32,1024]{1,0:T(8,128)S(1)}, bf16[32,1024]{1,0:T(8,128)(2,1)S(1)}, bf16[1024,3584]{1,0:T(8,128)(2,1)S(1)}) custom-call(bf16[32,3584]{1,0:T(8,128)(2,1)S(1)} %get-tuple-element.26.rows_ref, bf16[3584,1024]{1,0:T(8,128)(2,1)S(1)} %bitcast.6, bf16[3584,1024]{1,0:T(8,128)(2,1)S(1)} %bitcast.15), custom_call_target="tpu_custom_call" | custom-call | flops 469762048 | bytes 14680064 | tf_op jit(solution)/shard_map/pallas_call | solution.py:315
  26.4 1.1 %collective-permute-start.1 = (bf16[32,1024]{1,0:T(8,128)(2,1)S(1)}, bf16[32,1024]{1,0:T(8,128)(2,1)S(1)}, u32[]{:S(2)}, u32[]{:S(2)}) collective-permute-start(bf16[32,1024]{1,0:T(8,128)(2,1)S(1)} %get-tuple-element.27.act_ref), channel_id=1, source_target_pairs={{0,1},{1,0},{2,3},{3,2},{4,5},{5,4},{6,7},{7,6},{8,9},{9,8},{10,11... | collective-permute-start | bytes 196616 | tf_op jit(solution)/shard_map/ppermute | solution.py:260
  27.6 0.0 collective-permute-done.2.recv_ref
  27.6 2.8 %shard_map.98 = (bf16[16,16,256]{2,1,0:T(8,128)(2,1)S(1)}, bf16[16,16,256]{2,1,0:T(8,128)(2,1)S(1)}) custom-call(f32[32,1024]{1,0:T(8,128)S(1)} %get-tuple-element.29.cot_ref, bf16[32,1024]{1,0:T(8,128)(2,1)S(1)} %collective-permute-done.2.recv_ref, f32[32,1024]{1,0:T(8,128)S(1)} %get-tuple-element.31.gate_in, f32[32,1024]{1,0:T(8,128)S(1)} %get-tuple-element.32.up_in, ...), custom_call_target="tpu_custom_call" | custom-call | flops 469762048 | bytes 14680064 | tf_op jit(solution)/shard_map/pallas_call | solution.py:328
  30.4 0.4 collective-permute-done.1.recv_ref
  30.8 1.4 %shard_map.99 = (bf16[16,16,384]{2,1,0:T(8,128)(2,1)S(1)}, bf16[16,16,384]{2,1,0:T(8,128)(2,1)S(1)}) custom-call(bf16[32,1024]{1,0:T(8,128)(2,1)S(1)} %get-tuple-element.27.act_ref, bf16[32,1024]{1,0:T(8,128)(2,1)S(1)} %collective-permute-done.1.recv_ref, f32[32,128]{1,0:T(8,128)S(1)} %get-tuple-element.28.weight_in, bf16[2048,1792]{1,0:T(8,128)(2,1)S(1)} %bitcast.11, ...), custom_call_target="tpu_custom_call" | custom-call | flops 234881024 | bytes 7340032 | tf_op jit(solution)/shard_map/pallas_call | solution.py:336
  32.2 0.1 collective-permute-start.3
  32.3 1.4 %collective-permute-done.3 = bf16[16,16,384]{2,1,0:T(8,128)(2,1)S(1)} collective-permute-done((bf16[16,16,384]{2,1,0:T(8,128)(2,1)S(1)}, bf16[16,16,384]{2,1,0:T(8,128)(2,1)S(1)}, u32[]{:S(2)}, u32[]{:S(2)}) %collective-permute-start.3) | collective-permute-done | bytes 196640 | tf_op jit(solution)/shard_map/ppermute | solution.py:260
  33.7 0.1 add_convert_fusion
  33.8 12.6 %all_to_all.11.in_ref = bf16[16,16,384]{2,1,0:T(8,128)(2,1)S(1)} all-to-all(bf16[16,16,384]{2,1,0:T(8,128)(2,1)S(1)} %add_convert_fusion), channel_id=1, replica_groups=mesh['chip'=8,'core'=2,'local'=2] {'chip','local'}, dimensions={0} | all-to-all | bytes 393216 | tf_op jit(solution)/shard_map/all_to_all | solution.py:345
  46.4 0.7 %shard_map.100 = (bf16[1,1,3584]{2,1,0:T(2,128)(2,1)}, bf16[1,1,3584]{2,1,0:T(2,128)(2,1)}, f32[1,1,8]{2,1,0:T(1,128)}) custom-call(bf16[16,16,384]{2,1,0:T(8,128)(2,1)S(1)} %all_to_all.11.in_ref, f32[8,128]{1,0:T(8,128)S(1)} %get-tuple-element.40.named_ref), custom_call_target="tpu_custom_call" | custom-call | tf_op jit(solution)/shard_map/pallas_call | solution.py:346
  (6 shorter events, 0.0 us)
Async XLA Ops:
  0.6 19.5 %slice-start = ((s8[7340032]{0:T(1024)(128)(4,1)}), s8[4194304]{0:T(1024)(128)(4,1)S(1)}, s32[]{:S(2)}) async-start(s8[7340032]{0:T(1024)(128)(4,1)} %bitcast.8), calls=%async_computation.2 | async-start | bytes 8388608
  0.6 18.0 %copy-start = (bf16[1,3584,1024]{2,1,0:T(8,128)(2,1)S(1)}, bf16[1,3584,1024]{2,1,0:T(8,128)(2,1)}, u32[]{:S(2)}) copy-start(bf16[1,3584,1024]{2,1,0:T(8,128)(2,1)} %param.10) | copy-start | bytes 22020100
  0.7 19.5 %slice-start.1 = ((s8[7340032]{0:T(1024)(128)(4,1)}), s8[3145728]{0:T(1024)(128)(4,1)S(1)}, s32[]{:S(2)}) async-start(s8[7340032]{0:T(1024)(128)(4,1)} %bitcast.8), calls=%async_computation.3 | async-start | bytes 6291456
  18.7 1.5 %collective-permute-start = (bf16[16,16,384]{2,1,0:T(8,128)(2,1)S(1)}, bf16[16,16,384]{2,1,0:T(8,128)(2,1)S(1)}, u32[]{:S(2)}, u32[]{:S(2)}) collective-permute-start(bf16[16,16,384]{2,1,0:T(8,128)(2,1)S(1)} %all_to_all.10.in_ref), channel_id=1, source_target_pairs={{0,2},{2,0},{1,3},{3,1},{4,6},{6,4},{5,7},{7,5},{8,10},{10,8},{9,1... | collective-permute-start | bytes 589832 | tf_op jit(solution)/shard_map/ppermute | solution.py:260
  18.7 4.9 %slice-start.2 = ((s8[7340032]{0:T(1024)(128)(4,1)}), s8[4194304]{0:T(1024)(128)(4,1)S(1)}, s32[]{:S(2)}) async-start(s8[7340032]{0:T(1024)(128)(4,1)} %bitcast.13), calls=%async_computation.4 | async-start | bytes 8388608
  20.2 3.4 %slice-start.3 = ((s8[7340032]{0:T(1024)(128)(4,1)}), s8[3145728]{0:T(1024)(128)(4,1)S(1)}, s32[]{:S(2)}) async-start(s8[7340032]{0:T(1024)(128)(4,1)} %bitcast.13), calls=%async_computation.5 | async-start | bytes 6291456
  22.6 5.0 %collective-permute-start.2 = (bf16[32,1024]{1,0:T(8,128)(2,1)S(1)}, bf16[32,1024]{1,0:T(8,128)(2,1)S(1)}, u32[]{:S(2)}, u32[]{:S(2)}) collective-permute-start(bf16[32,1024]{1,0:T(8,128)(2,1)S(1)} %get-tuple-element.30), channel_id=1, source_target_pairs={{0,1},{1,0},{2,3},{3,2},{4,5},{5,4},{6,7},{7,6},{8,9},{9,8},{10,11... | collective-permute-start | bytes 196616 | tf_op jit(solution)/shard_map/ppermute | solution.py:260
  26.4 4.3 %collective-permute-start.1 = (bf16[32,1024]{1,0:T(8,128)(2,1)S(1)}, bf16[32,1024]{1,0:T(8,128)(2,1)S(1)}, u32[]{:S(2)}, u32[]{:S(2)}) collective-permute-start(bf16[32,1024]{1,0:T(8,128)(2,1)S(1)} %get-tuple-element.27.act_ref), channel_id=1, source_target_pairs={{0,1},{1,0},{2,3},{3,2},{4,5},{5,4},{6,7},{7,6},{8,9},{9,8},{10,11... | collective-permute-start | bytes 196616 | tf_op jit(solution)/shard_map/ppermute | solution.py:260
  32.2 1.5 %collective-permute-start.3 = (bf16[16,16,384]{2,1,0:T(8,128)(2,1)S(1)}, bf16[16,16,384]{2,1,0:T(8,128)(2,1)S(1)}, u32[]{:S(2)}, u32[]{:S(2)}) collective-permute-start(bf16[16,16,384]{2,1,0:T(8,128)(2,1)S(1)} %get-tuple-element.39), channel_id=1, source_target_pairs={{0,2},{2,0},{1,3},{3,1},{4,6},{6,4},{5,7},{7,5},{8,10},{10,8},{9,1... | collective-permute-start | bytes 589832 | tf_op jit(solution)/shard_map/ppermute | solution.py:260
